TPU v7x, 32 devices: a whole 2x2x4 slice. The times are simulated.
32 devices in a mesh: parts: 1, prow: 32 (over z, y, x, core), pcol: 1.
Axes of the slice: x: 2, y: 2, z: 4, core: 2. Of those that a mesh axis runs over, the one named last changes fastest.
Arguments:
- rhs: bfloat16 [3, 32, 128, 128], P('parts', 'prow', 'pcol'), may hold values from -6 to 6
- lower_factor_t: bfloat16 [3, 32, 128, 3, 32, 128], P('parts', 'pcol', None, None, 'prow'), may hold values from -0.1875 to 0.1875
- upper_factor_t: bfloat16 [3, 32, 128, 3, 32, 128], P('parts', 'pcol', None, None, 'prow'), may hold values from -0.1875 to 0.1875
- lower_snode: int32 [64], P('parts'), may hold values from 0 to 4, never falling along the last dimension, each value on 1 to 16 neighbouring positions
- upper_snode: int32 [32], P('parts'), may hold values from 0 to 3, never falling along the last dimension, each value on 1 to 16 neighbouring positions
- parent: int32 [5, 1], P('parts'), may hold values from 0 to 3
- pattern: int32 [32, 5], P('parts'), may hold values 0 or 1
Outputs:
- forward_solution: float32 [3, 32, 128, 128], P('parts', 'prow', 'pcol')
- backward_solution: float32 [3, 32, 128, 128], P('parts', 'prow', 'pcol')
Inputs may be any that keep to these rules, and one draw needn't show every extreme that they name: `lower_snode`: never falls; each supernode spans 1 to 16 blocks of 128 rows and every number from 0 to 4 is used. `upper_snode`: never falls; each supernode spans 1 to 16 blocks of 128 rows and every number from 0 to 3 is used. Every upper supernode is the parent of at least one lower supernode.
All inputs are finite; a program needn't handle non-finite values.
Results may differ from a plain program's by a relative error of at most 0.0042.
Values may be sent and summed in bfloat16 or wider, within the bound.
No kernel may reach another device: no remote copies, remote signals or barrier semaphores. Data moves between devices by JAX's collectives and lax.ppermute only.
A program may use at most 128 MiB of HBM per device.

v0:
```python
import jax
import jax.numpy as jnp
from jax import lax
from jax.sharding import PartitionSpec as P


def block_masks(lower_snode, upper_snode, parent, pattern):
    count_lower = parent.shape[0]
    snode_ids = jnp.concatenate([lower_snode, upper_snode + count_lower])
    same = snode_ids[:, None] == snode_ids[None, :]
    onehot = (lower_snode[:, None] == jnp.arange(count_lower, dtype=jnp.int32)[None, :]).astype(
        jnp.int32
    )
    parent_block = jnp.sum(onehot * parent[:, 0][None, :], axis=1)
    pattern_block = jnp.sum(pattern[:, None, :] * onehot[None, :, :], axis=2)
    link = (upper_snode[:, None] == parent_block[None, :]) & (pattern_block == 1)
    return (same, link)


def couplings(link):
    upper_count, lower_count = link.shape
    total = upper_count + lower_count
    couple_lower = jnp.concatenate(
        [
            jnp.zeros((lower_count, total), bool),
            jnp.concatenate([link, jnp.zeros((upper_count, upper_count), bool)], 1),
        ],
        0,
    )
    couple_upper = jnp.concatenate(
        [
            jnp.concatenate([jnp.zeros((lower_count, lower_count), bool), link.T], 1),
            jnp.zeros((upper_count, total), bool),
        ],
        0,
    )
    return (couple_lower, couple_upper)


def on_device(rhs, lower_factor_t, upper_factor_t, lower_snode, upper_snode, parent, pattern):
    rows_axis = lax.axis_size("prow")
    row_index = lax.axis_index("prow")
    col_index = lax.axis_index("pcol")
    blocks_local = rhs.shape[0]
    sub_rows = rhs.shape[2]
    col_group = lower_factor_t.shape[1]
    block_size = lower_factor_t.shape[2]
    lower_local = lower_snode.shape[0] // rows_axis
    same, link = block_masks(lower_snode, upper_snode, parent, pattern)
    couple_lower, couple_upper = couplings(link)
    all_blocks = same.shape[0]

    def local_blocks(whole):
        selected = lax.dynamic_index_in_dim(
            whole.reshape(blocks_local, rows_axis, all_blocks), row_index, 1, keepdims=False
        )
        selected = selected.reshape(blocks_local, blocks_local, rows_axis)
        selected = lax.dynamic_slice_in_dim(selected, col_index * col_group, col_group, 2)
        return jnp.transpose(selected, (1, 2, 0)).reshape(
            blocks_local, col_group, 1, blocks_local, 1, 1
        )

    local_ids = jnp.arange(blocks_local, dtype=jnp.int32)
    row_elem = (
        (local_ids[:, None] * rows_axis + row_index) * block_size
        + jnp.arange(block_size, dtype=jnp.int32)[None, :]
    ).reshape(1, 1, 1, blocks_local, 1, block_size)
    own_cols = col_index * col_group + jnp.arange(col_group, dtype=jnp.int32)
    col_block = local_ids[:, None] * rows_axis + own_cols[None, :]
    col_elem = (
        col_block[:, :, None] * block_size + jnp.arange(block_size, dtype=jnp.int32)[None, None, :]
    ).reshape(blocks_local, col_group, block_size, 1, 1, 1)
    same_local = local_blocks(same)
    keep_lower = same_local & (row_elem >= col_elem) | local_blocks(couple_lower)
    keep_upper = same_local & (row_elem <= col_elem) | local_blocks(couple_upper)
    lower_kept = jnp.where(keep_lower, lower_factor_t, jnp.zeros((), lower_factor_t.dtype))
    upper_kept = jnp.where(keep_upper, upper_factor_t, jnp.zeros((), upper_factor_t.dtype))

    def apply_factor(factor, vector, col_range, row_range):
        window = factor[col_range[0] : col_range[1], :, :, row_range[0] : row_range[1], 0, :]
        pieces_in = lax.all_gather(vector, "prow", axis=1, tiled=True)
        selector = (
            jnp.arange(pieces_in.shape[1], dtype=jnp.int32)[:, None] == own_cols[None, :]
        ).astype(jnp.bfloat16)
        picked = jnp.einsum(
            "rjen,jq->rqen", pieces_in, selector, preferred_element_type=jnp.float32
        ).astype(jnp.bfloat16)
        summed = lax.dot_general(
            window, picked, (((0, 1, 2), (0, 1, 2)), ((), ())), preferred_element_type=jnp.float32
        )[:, None]
        return lax.psum(summed, "pcol")

    source = lax.all_gather(rhs, "pcol", axis=2, tiled=True)
    rhs_width = source.shape[3]
    lower_span = (0, lower_local)
    upper_span = (lower_local, blocks_local)
    rhs_lower = source[:lower_local]
    rhs_upper = source[lower_local:]
    forward_lower = apply_factor(lower_kept, rhs_lower, lower_span, lower_span)
    lower_known = forward_lower.astype(jnp.bfloat16)
    coupling = apply_factor(lower_kept, lower_known, lower_span, upper_span).astype(jnp.bfloat16)
    joined = apply_factor(
        lower_kept, jnp.concatenate([rhs_upper, coupling], 3), upper_span, upper_span
    )
    upper_direct = joined[..., :rhs_width]
    upper_update = joined[..., rhs_width:]
    forward_upper = upper_direct - upper_update
    upper_known = forward_upper.astype(jnp.bfloat16)
    backward_upper = apply_factor(upper_kept, upper_known, upper_span, upper_span)
    back_known = backward_upper.astype(jnp.bfloat16)
    correction = apply_factor(upper_kept, back_known, upper_span, lower_span).astype(jnp.bfloat16)
    joined_lower = apply_factor(
        upper_kept, jnp.concatenate([lower_known, correction], 3), lower_span, lower_span
    )
    lower_direct = joined_lower[..., :rhs_width]
    lower_update = joined_lower[..., rhs_width:]
    backward_lower = lower_direct - lower_update
    forward_solution = jnp.concatenate([forward_lower, forward_upper], 0)
    backward_solution = jnp.concatenate([backward_lower, backward_upper], 0)
    forward_solution = lax.dynamic_slice_in_dim(forward_solution, col_index * sub_rows, sub_rows, 2)
    backward_solution = lax.dynamic_slice_in_dim(
        backward_solution, col_index * sub_rows, sub_rows, 2
    )
    return (forward_solution, backward_solution)


def solution(mesh):
    placed = (
        P("parts", "prow", "pcol", None),
        P("parts", "pcol", None, None, "prow", None),
        P("parts", "pcol", None, None, "prow", None),
        P("parts"),
        P("parts"),
        P("parts", None),
        P("parts", None),
    )
    return jax.shard_map(
        on_device,
        mesh=mesh,
        in_specs=placed,
        out_specs=(P("parts", "prow", "pcol", None), P("parts", "prow", "pcol", None)),
        check_vma=False,
    )
```

profile of v0, /device:TPU:0, one launch (start us, length us, event | category | flops | bytes accessed | tf_op | source)
XLA Modules:
  0.0 400.8 jit_solution(11686160062265669645)
XLA Ops:
  7.2 1.5 slice.48
  9.4 0.8 select_reduce_fusion
  10.2 0.8 multiply_reduce_fusion
  11.0 0.7 bitcast_and_fusion
  11.7 0.7 compare_and_fusion
  13.5 0.7 pad_add_fusion
  14.8 14.9 %or_select_fusion = (bf16[3,32,128,3,1,128]{5,2,1,3,0,4:T(8,128)(2,1)}, bf16[3,32,128,3,1,128]{5,2,1,3,0,4:T(8,128)(2,1)}) fusion(bf16[3,32,128,3,1,128]{5,2,4,3,1,0:T(8,128)(2,1)} %param.9, s32[3,32,128]{2,1,0:T(8,128)S(1)} %iota_add_fusion, s32[3,128]{1,0:T(4,128)S(1)} %iota_add_fusion.1, pred[3,32,3]{1,2,0:T(4,128)(4,1)S(1)} %copy.136, ...), kind=kLoop, calls=%fused_computation | loop fusion | flops 37748736 | bytes 37800288 | tf_op jit(solution)/shard_map/jit(_where)/select_n | solution.py:77
  29.7 40.8 %all-gather.9.cloned.1.call-done = bf16[2,32,128,128]{3,2,0,1:T(8,128)(2,1)} async-done(((bf16[2,1,128,128]{3,2,0,1:T(8,128)(2,1)}), bf16[2,32,128,128]{3,2,0,1:T(8,128)(2,1)}) %all-gather.9.cloned.1.call-update) | async-done | bytes 2097168 | tf_op jit(solution)/shard_map/all_gather | solution.py:81
  70.5 3.0 convert_bitcast_fusion.2
  73.6 4.3 %bitcast_convert_fusion = (bf16[2,128,128]{1,2,0:T(8,128)(2,1)}, f32[2,128,128,1,1]{1,2,4,0,3:T(8,128)S(1)}) fusion(bf16[3,32,128,3,1,128]{5,2,1,3,0,4:T(8,128)(2,1)} %get-tuple-element.19, bf16[2,32,128,128,1]{3,1,2,0,4:T(8,128)(2,1)S(1)} %convert_bitcast_fusion.2), kind=kOutput, calls=%fused_computation.48 | convolution fusion | flops 536903680 | bytes 6488064 | tf_op jit(solution)/shard_map/dot_general | solution.py:88
  78.0 0.8 slice.39
  78.8 51.3 %all-gather.17.cloned.1.call-done = bf16[2,4096,128]{1,2,0:T(8,128)(2,1)} async-done(((bf16[2,128,128]{1,2,0:T(8,128)(2,1)}), bf16[2,4096,128]{1,2,0:T(8,128)(2,1)}) %all-gather.17.cloned.1.call-update) | async-done | bytes 2097168 | tf_op jit(solution)/shard_map/all_gather | solution.py:81
  130.2 2.1 copy.170
  132.2 3.8 copy.128
  136.1 2.3 convert_bitcast_fusion.1
  138.3 2.9 fusion.38
  141.2 0.7 copy.130
  142.1 55.4 %all-gather.11.cloned.1.call-done = bf16[1,32,128,256]{3,2,0,1:T(8,128)(2,1)} async-done(((bf16[1,1,128,256]{3,2,0,1:T(8,128)(2,1)}), bf16[1,32,128,256]{3,2,0,1:T(8,128)(2,1)}) %all-gather.11.cloned.1.call-update) | async-done | bytes 2097168 | tf_op jit(solution)/shard_map/all_gather | solution.py:81
  197.4 2.9 fusion.20
  200.3 3.3 fusion.26
  204.6 52.4 %all-gather.13.cloned.1.call-done = bf16[1,32,128,128]{3,2,0,1:T(8,128)(2,1)} async-done(((bf16[1,1,128,128]{3,2,0,1:T(8,128)(2,1)}), bf16[1,32,128,128]{3,2,0,1:T(8,128)(2,1)}) %all-gather.13.cloned.1.call-update) | async-done | bytes 1048592 | tf_op jit(solution)/shard_map/all_gather | solution.py:81
  257.1 2.0 convolution_convert_fusion.1
  259.0 2.4 bitcast_convert_fusion.1
  261.5 52.7 %all-gather.19.cloned.1.call-done = bf16[4096,128]{1,0:T(8,128)(2,1)} async-done(((bf16[128,128]{1,0:T(8,128)(2,1)}), bf16[4096,128]{1,0:T(8,128)(2,1)}) %all-gather.19.cloned.1.call-update) | async-done | bytes 1048592 | tf_op jit(solution)/shard_map/all_gather | solution.py:81
  314.3 2.0 convolution_convert_fusion
  316.2 1.0 copy.143
  317.2 2.0 fusion.31
  319.3 0.8 copy.144
  320.1 0.8 copy.149
  320.9 60.3 %all-gather.15.cloned.1.call-done = bf16[2,32,128,256]{3,2,0,1:T(8,128)(2,1)} async-done(((bf16[2,1,128,256]{3,2,0,1:T(8,128)(2,1)}), bf16[2,32,128,256]{3,2,0,1:T(8,128)(2,1)}) %all-gather.15.cloned.1.call-update) | async-done | bytes 4194320 | tf_op jit(solution)/shard_map/all_gather | solution.py:81
  381.3 4.8 %convert_bitcast_fusion = bf16[2,32,128,256,1]{3,1,2,0,4:T(8,128)(2,1)S(1)} fusion(bf16[2,32,128,256]{3,2,0,1:T(8,128)(2,1)} %all-gather.15.cloned.1.call-done), kind=kOutput, calls=%fused_computation.9 | convolution fusion | flops 136315904 | bytes 8388608 | tf_op jit(solution)/shard_map/rjen,jq->rqen/dot_general | solution.py:85
  386.0 7.2 %fusion.23 = f32[2,1,128,256]{3,2,0,1:T(8,128)S(1)} fusion(bf16[2,32,128,256,1]{3,1,2,0,4:T(8,128)(2,1)S(1)} %convert_bitcast_fusion, bf16[3,32,128,3,1,128]{5,2,1,3,0,4:T(8,128)(2,1)} %get-tuple-element.18), kind=kOutput, calls=%fused_computation.28 | convolution fusion | flops 1073741824 | bytes 8650752 | tf_op jit(solution)/shard_map/dot_general | solution.py:88
  (43 shorter events, 4.4 us)
Async XLA Ops:
  7.2 63.4 %all-gather.9.cloned.1.call-start = ((), (), s32[]{:S(2)}) async-start(), calls=%async_computation | async-start | bytes 2162688 | tf_op jit(solution)/shard_map/all_gather | solution.py:81
  8.7 121.4 %all-gather.17.cloned.1.call-start = ((), (), s32[]{:S(2)}) async-start(), calls=%async_computation.4 | async-start | bytes 2162688 | tf_op jit(solution)/shard_map/all_gather | solution.py:81
  77.9 119.5 %all-gather.11.cloned.1.call-start = ((), (), s32[]{:S(2)}) async-start(), calls=%async_computation.1 | async-start | bytes 2162688 | tf_op jit(solution)/shard_map/all_gather | solution.py:81
  142.0 115.0 %all-gather.13.cloned.1.call-start = ((), (), s32[]{:S(2)}) async-start(), calls=%async_computation.2 | async-start | bytes 1081344 | tf_op jit(solution)/shard_map/all_gather | solution.py:81
  204.4 109.9 %all-gather.19.cloned.1.call-start = ((), (), s32[]{:S(2)}) async-start(), calls=%async_computation.5 | async-start | bytes 1081344 | tf_op jit(solution)/shard_map/all_gather | solution.py:81
  261.5 57.8 %copy-start = (bf16[2,128,128]{1,2,0:T(8,128)(2,1)S(1)}, bf16[2,128,128]{1,2,0:T(8,128)(2,1)}, u32[]{:S(2)}) copy-start(bf16[2,128,128]{1,2,0:T(8,128)(2,1)} %get-tuple-element.20) | copy-start | bytes 196612
  261.5 119.8 %all-gather.15.cloned.1.call-start = ((), (), s32[]{:S(2)}) async-start(), calls=%async_computation.3 | async-start | bytes 4325376 | tf_op jit(solution)/shard_map/all_gather | solution.py:81
Sparse Core Ops, SparseCore 0:
  11.4 59.0 all-gather.8
  78.0 52.0 all-gather.16
  142.1 55.2 all-gather.10
  204.5 52.5 all-gather.12
  261.6 52.6 all-gather.18
  320.2 60.9 all-gather.14
where the time goes:
time: 402 us; the launch traced here: 401 us
  waiting for transfers between devices  313 us (78%)
  matrix products  39.1 us (10%)
  other arithmetic  21 us (5%)
  between operations  14.3 us (4%)
  local copies, waits for them, and re-layouts  13 us (3%)
    all_gather x6, waiting for transfers between devices, apply_factor(): pieces_in = lax.all_gather(vector, 'prow', axis=1, tiled=True)  313 us
    dot_general x6, matrix products, apply_factor(): lax.dot_general(window, picked, (((0, 1, 2), (0, 1, 2)), ((), ())), prefe...  22.2 us
    dot_general x6, matrix products, apply_factor(): jnp.einsum('rjen,jq->rqen', pieces_in, selector, preferred_element_type=j...  16.9 us
    select_n x1, other arithmetic, on_device(): jnp.where(keep_upper, upper_factor_t, jnp.zeros((), upper_factor_t.dtype))  14.9 us
  transfers between devices with their start and end apart: 6, of which 6 were waited for; matrix products, arithmetic and copies ran while one was open for 6% of the time, Pallas kernels for 0%

commit v1 on v0

--- a/solution.py
+++ b/solution.py
@@ -1,7 +1,360 @@
+import functools
 import jax
 import jax.numpy as jnp
 from jax import lax
+from jax.experimental import pallas as pl
+from jax.experimental.pallas import tpu as pltpu
 from jax.sharding import PartitionSpec as P
+
+SPAN = 16
+PLANE = 8
+PLANES = 4
+VMEM_BYTES = 48 * 1024 * 1024
+
+
+def window_start(block, direction, count):
+    if direction > 0:
+        return jnp.maximum(block - (SPAN - 1), 0)
+    return jnp.minimum(block, count - SPAN)
+
+
+def keep_window(out, block, start, direction, snode, first):
+    own = snode[block]
+
+    def clear(step, carry):
+        other = start + step
+        if direction > 0:
+            kept = (snode[other] == own) & (other <= block)
+        else:
+            kept = (snode[other] == own) & (other >= block)
+
+        @pl.when(jnp.logical_not(kept))
+        def _():
+            out[first + step] = jnp.zeros(out.shape[1:], out.dtype)
+
+        return carry
+
+    lax.fori_loop(0, SPAN, clear, 0)
+    size = out.shape[1]
+    col = lax.broadcasted_iota(jnp.int32, (size, size), 0)
+    row = lax.broadcasted_iota(jnp.int32, (size, size), 1)
+    tri = row >= col if direction > 0 else row <= col
+    diagonal = out[first + block - start]
+    out[first + block - start] = jnp.where(tri, diagonal, jnp.zeros_like(diagonal))
+
+
+def pack_level_kernel(direction, base, rows, row_first, count, factor, snode, out, sems):
+    me = lax.axis_index("prow")
+    copies = []
+    for row in range(rows):
+        block = row * PLANE * PLANES + me
+        start = window_start(block, direction, count)
+        copy = pltpu.make_async_copy(
+            factor.at[pl.ds(base + start, SPAN), row_first + row],
+            out.at[pl.ds(row * SPAN, SPAN)],
+            sems.at[row],
+        )
+        copy.start()
+        copies.append((copy, block, start))
+    for row, (copy, block, start) in enumerate(copies):
+        copy.wait()
+        keep_window(out, block, start, direction, snode, row * SPAN)
+
+
+def pack_level(factor, snode, direction, base, rows, row_first, count):
+    size = factor.shape[-1]
+    return pl.pallas_call(
+        functools.partial(pack_level_kernel, direction, base, rows, row_first, count),
+        out_shape=jax.ShapeDtypeStruct((rows * SPAN, size, size), factor.dtype),
+        in_specs=[
+            pl.BlockSpec(memory_space=pl.ANY),
+            pl.BlockSpec(memory_space=pltpu.SMEM),
+        ],
+        out_specs=pl.BlockSpec(memory_space=pltpu.VMEM),
+        scratch_shapes=[pltpu.SemaphoreType.DMA((rows,))],
+        compiler_params=pltpu.CompilerParams(vmem_limit_bytes=VMEM_BYTES),
+        cost_estimate=pl.CostEstimate(flops=0, bytes_accessed=4 * rows * SPAN * size * size, transcendentals=0),
+        name="pack_level",
+    )(factor, snode)
+
+
+def pack_down_kernel(factor, lower_snode, upper_snode, parent, pattern, out, sem):
+    me = lax.axis_index("prow")
+    count = out.shape[0]
+    copy = pltpu.make_async_copy(factor.at[pl.ds(0, count), 2], out, sem)
+    copy.start()
+    copy.wait()
+
+    def clear(block, carry):
+        child = lower_snode[block]
+        linked = (parent[child, 0] == upper_snode[me]) & (pattern[me, child] == 1)
+
+        @pl.when(jnp.logical_not(linked))
+        def _():
+            out[block] = jnp.zeros(out.shape[1:], out.dtype)
+
+        return carry
+
+    lax.fori_loop(0, count, clear, 0)
+
+
+def pack_up_kernel(factor, lower_snode, upper_snode, parent, pattern, out, sems):
+    me = lax.axis_index("prow")
+    count = out.shape[1]
+    copies = []
+    for row in range(2):
+        copy = pltpu.make_async_copy(
+            factor.at[pl.ds(2 * count, count), row], out.at[row], sems.at[row]
+        )
+        copy.start()
+        copies.append(copy)
+    for row in range(2):
+        copies[row].wait()
+        child = lower_snode[row * count + me]
+        above = parent[child, 0]
+
+        def clear(block, carry):
+            linked = (above == upper_snode[block]) & (pattern[block, child] == 1)
+
+            @pl.when(jnp.logical_not(linked))
+            def _():
+                out[row, block] = jnp.zeros(out.shape[2:], out.dtype)
+
+            return carry
+
+        lax.fori_loop(0, count, clear, 0)
+
+
+def pack_coupling(kernel, name, shape, sems, factor, *tables):
+    return pl.pallas_call(
+        kernel,
+        out_shape=jax.ShapeDtypeStruct(shape, factor.dtype),
+        in_specs=[pl.BlockSpec(memory_space=pl.ANY)]
+        + [pl.BlockSpec(memory_space=pltpu.SMEM)] * 4,
+        out_specs=pl.BlockSpec(memory_space=pltpu.VMEM),
+        scratch_shapes=[sems],
+        compiler_params=pltpu.CompilerParams(vmem_limit_bytes=VMEM_BYTES),
+        cost_estimate=pl.CostEstimate(flops=0, bytes_accessed=4 * 64 * 128 * 128, transcendentals=0),
+        name=name,
+    )(factor, *tables)
+
+
+def gather(block, shifts):
+    total = PLANE * PLANES
+
+    def move(value, pairs):
+        return lax.ppermute(value, "prow", pairs)
+
+    parts = [block[None]]
+    for shift in shifts:
+        if shift[0] == "xor":
+            pairs = [(i, i ^ (PLANE * shift[1])) for i in range(total)]
+        else:
+            pairs = [(i, (i + PLANE * shift[1]) % total) for i in range(total)]
+        parts.append(move(block[None], pairs))
+    pieces = {0: jnp.concatenate(parts, 0)}
+    for k in (6, 2, 4):
+        pieces[k] = move(pieces[0], [(i, i ^ k) for i in range(total)])
+    for k in (0, 6, 2, 4):
+        pieces[k + 1] = move(pieces[k], [(i, i ^ 1) for i in range(total)])
+    return [pieces[k] for k in range(PLANE)]
+
+
+def copy_window(pieces, xs, block, start, direction):
+    me = lax.axis_index("prow")
+    offset = me & (PLANE - 1)
+    size = xs.shape[0]
+    for k in range(PLANE):
+        other = offset ^ k
+        first = (other - start) & (PLANE - 1)
+        for half in range(SPAN // PLANE):
+            slot = first + half * PLANE
+            source = start + slot
+            apart = direction * (block // PLANE - source // PLANE)
+            apart = jnp.clip(apart, 0, 2)
+            level = source // (PLANE * PLANES) if pieces[k].shape[1] > 1 else 0
+            at = pl.multiple_of(slot * size, size)
+            xs[:, pl.ds(at, size)] = pieces[k][apart, level]
+
+
+def dot(left, right):
+    return jnp.dot(left, right, preferred_element_type=jnp.float32)
+
+
+def forward_lower_kernel(*refs):
+    pieces, (factor, solved, known, xs) = refs[:PLANE], refs[PLANE:]
+    me = lax.axis_index("prow")
+    size = xs.shape[0]
+    for row in range(2):
+        block = row * PLANE * PLANES + me
+        start = window_start(block, 1, 2 * PLANE * PLANES)
+        copy_window(pieces, xs, block, start, 1)
+        result = dot(xs[...], factor[row * SPAN : (row + 1) * SPAN].reshape(SPAN * size, size))
+        solved[row] = result
+        known[row] = result.astype(known.dtype)
+
+
+def coupling_kernel(*refs):
+    pieces, (factor, rhs, out, xs) = refs[:PLANE], refs[PLANE:]
+    me = lax.axis_index("prow")
+    offset, plane = me & (PLANE - 1), me // PLANE
+    size = xs.shape[0]
+    for k in range(PLANE):
+        for along in range(PLANES):
+            for row in range(2):
+                source = row * PLANE * PLANES + (plane ^ along) * PLANE + (offset ^ k)
+                xs[:, pl.ds(pl.multiple_of(source * size, size), size)] = pieces[k][along, row]
+    result = dot(xs[...], factor[...].reshape(2 * PLANE * PLANES * size, size))
+    out[0] = (rhs[2].astype(jnp.float32) - result).astype(out.dtype)
+
+
+def upper_kernel(direction, *refs):
+    pieces, (factor, solved, known, xs) = refs[:PLANE], refs[PLANE:]
+    me = lax.axis_index("prow")
+    size = xs.shape[0]
+    start = window_start(me, direction, PLANE * PLANES)
+    copy_window(pieces, xs, me, start, direction)
+    result = dot(xs[...], factor[...].reshape(SPAN * size, size))
+    solved[0] = result
+    known[0] = result.astype(known.dtype)
+
+
+def correction_kernel(*refs):
+    pieces, (factor, solved, out, xs) = refs[:PLANE], refs[PLANE:]
+    me = lax.axis_index("prow")
+    offset, plane = me & (PLANE - 1), me // PLANE
+    size = xs.shape[0]
+    for k in range(PLANE):
+        for along in range(PLANES):
+            source = (plane ^ along) * PLANE + (offset ^ k)
+            xs[:, pl.ds(pl.multiple_of(source * size, size), size)] = pieces[k][along, 0]
+    for row in range(2):
+        result = dot(xs[...], factor[row].reshape(PLANE * PLANES * size, size))
+        known = solved[row].astype(out.dtype).astype(jnp.float32)
+        out[row] = (known - result).astype(out.dtype)
+
+
+def backward_lower_kernel(*refs):
+    pieces, (factor, upper, out, xs) = refs[:PLANE], refs[PLANE:]
+    me = lax.axis_index("prow")
+    size = xs.shape[0]
+    for row in range(2):
+        block = row * PLANE * PLANES + me
+        start = window_start(block, -1, 2 * PLANE * PLANES)
+        copy_window(pieces, xs, block, start, -1)
+        result = dot(xs[...], factor[row * SPAN : (row + 1) * SPAN].reshape(SPAN * size, size))
+        out[row, 0] = result.T
+    out[2, 0] = upper[0].T
+
+
+def turn_kernel(value, out):
+    for row in range(3):
+        out[row] = value[row, 0].astype(jnp.float32).T.astype(out.dtype)
+
+
+def forward_out_kernel(lower, upper, out):
+    for row in range(2):
+        out[row, 0] = lower[row].T
+    out[2, 0] = upper[0].T
+
+
+def local_call(kernel, name, shapes, operands, width=0, flops=0):
+    size = 128
+    scratch = [pltpu.VMEM((size, width), jnp.bfloat16)] if width else []
+    outs = [jax.ShapeDtypeStruct(*shape) for shape in shapes]
+    return pl.pallas_call(
+        kernel,
+        out_shape=outs,
+        in_specs=[pl.BlockSpec(memory_space=pltpu.VMEM)] * len(operands),
+        out_specs=[pl.BlockSpec(memory_space=pltpu.VMEM)] * len(outs),
+        scratch_shapes=scratch,
+        compiler_params=pltpu.CompilerParams(vmem_limit_bytes=VMEM_BYTES),
+        cost_estimate=pl.CostEstimate(flops=flops, bytes_accessed=1 << 20, transcendentals=0),
+        name=name,
+    )(*operands)
+
+
+def fast_device(rhs, lower_factor_t, upper_factor_t, lower_snode, upper_snode, parent, pattern):
+    rows, _, size, width = rhs.shape
+    total = PLANE * PLANES
+    f32, bf16 = jnp.float32, jnp.bfloat16
+
+    def blocks(factor):
+        return jnp.transpose(factor, (0, 1, 3, 4, 2, 5)).reshape(rows * total, rows, size, size)
+
+    lower, upper = blocks(lower_factor_t), blocks(upper_factor_t)
+    tables = (lower_snode, upper_snode, parent, pattern)
+    own = local_call(turn_kernel, "turn", [((rows, width, size), bf16)], [rhs])[0]
+
+    forward = (("shift", 1), ("shift", 2))
+    backward = (("shift", -1), ("shift", -2))
+    whole = (("xor", 1), ("xor", 2), ("xor", 3))
+
+    pieces = gather(own[:2], forward)
+    pack_l1 = pack_level(lower, lower_snode, 1, 0, 2, 0, 2 * total)
+    solved, known = local_call(
+        forward_lower_kernel,
+        "forward_lower",
+        [((2, width, size), f32), ((2, width, size), bf16)],
+        [*pieces, pack_l1],
+        SPAN * size,
+    )
+    pieces = gather(known, whole)
+    pack_c = pack_coupling(
+        pack_down_kernel, "pack_down", (2 * total, size, size), pltpu.SemaphoreType.DMA, lower, *tables
+    )
+    (difference,) = local_call(
+        coupling_kernel,
+        "coupling",
+        [((1, width, size), bf16)],
+        [*pieces, pack_c, own],
+        2 * total * size,
+    )
+    pieces = gather(difference, forward)
+    pack_l2 = pack_level(lower, upper_snode, 1, 2 * total, 1, 2, total)
+    forward_upper, upper_known = local_call(
+        functools.partial(upper_kernel, 1),
+        "forward_upper",
+        [((1, width, size), f32), ((1, width, size), bf16)],
+        [*pieces, pack_l2],
+        SPAN * size,
+    )
+    pieces = gather(upper_known, backward)
+    pack_u2 = pack_level(upper, upper_snode, -1, 2 * total, 1, 2, total)
+    (forward_solution,) = local_call(
+        forward_out_kernel,
+        "forward_out",
+        [((rows, 1, size, width), f32)],
+        [solved, forward_upper],
+    )
+    backward_upper, back_known = local_call(
+        functools.partial(upper_kernel, -1),
+        "backward_upper",
+        [((1, width, size), f32), ((1, width, size), bf16)],
+        [*pieces, pack_u2],
+        SPAN * size,
+    )
+    pieces = gather(back_known, whole)
+    pack_k = pack_coupling(
+        pack_up_kernel, "pack_up", (2, total, size, size), pltpu.SemaphoreType.DMA((2,)), upper, *tables
+    )
+    (remainder,) = local_call(
+        correction_kernel,
+        "correction",
+        [((2, width, size), bf16)],
+        [*pieces, pack_k, solved],
+        total * size,
+    )
+    pieces = gather(remainder, backward)
+    pack_u1 = pack_level(upper, lower_snode, -1, 0, 2, 0, 2 * total)
+    (backward_solution,) = local_call(
+        backward_lower_kernel,
+        "backward_lower",
+        [((rows, 1, size, width), f32)],
+        [*pieces, pack_u1, backward_upper],
+        SPAN * size,
+    )
+    return forward_solution, backward_solution
 
 
 def block_masks(lower_snode, upper_snode, parent, pattern):
@@ -134,8 +487,10 @@
         P("parts", None),
         P("parts", None),
     )
+    total = PLANE * PLANES
+    simple = mesh.shape["prow"] == total and mesh.shape["pcol"] == 1
     return jax.shard_map(
-        on_device,
+        fast_device if simple else on_device,
         mesh=mesh,
         in_specs=placed,
         out_specs=(P("parts", "prow", "pcol", None), P("parts", "prow", "pcol", None)),

time: 402 us -> 133 us (0.33)
  waiting for transfers between devices: 313 us -> 60.6 us
  starting transfers between devices: 0.43 us -> 47.7 us
  matrix products: 39.1 us -> 0 us
  Pallas kernels: 0 us -> 21 us
  other arithmetic: 21 us -> 0.13 us
  between operations: 14.3 us -> 0.98 us
  local copies, waits for them, and re-layouts: 13 us -> 1.74 us
    all_gather x6 -> x0, waiting for transfers between devices: 313 us -> none  [apply_factor(): pieces_in = lax.all_gather(vector, 'prow', axis=1, tiled=True)]
    ppermute x0 -> x56, waiting for transfers between devices: none -> 60.6 us  [move(): return lax.ppermute(value, 'prow', pairs)]
    ppermute x0 -> x56, starting transfers between devices: none -> 47.7 us  [move(): return lax.ppermute(value, 'prow', pairs)]
    dot_general x12 -> x0, matrix products: 39.1 us -> none  [the longest x6 22.2 us: apply_factor(): lax.dot_general(window, picked, (((0, 1, 2), (0, 1, 2)), ((), ())), prefe...]
    pallas_call x0 -> x14, Pallas kernels: none -> 21 us  [the longest x4 7.62 us: pack_level(): pl.pallas_call(functools.partial(pack_level_kernel, direction, base, rows...]
    select_n x1 -> x0, other arithmetic: 14.9 us -> none  [on_device(): jnp.where(keep_upper, upper_factor_t, jnp.zeros((), upper_factor_t.dtype))]
  transfers between devices with their start and end apart: 6 -> 56, of which waited for: 6 -> 24; matrix products, arithmetic and copies ran while one was open for 6% -> 0% of each run, Pallas kernels for 0% -> 12%
where the time goes in v1:
time: 133 us; the launch traced here: 132 us
  waiting for transfers between devices  60.6 us (46%)
  starting transfers between devices  47.7 us (36%)
  Pallas kernels  21 us (16%)
  local copies, waits for them, and re-layouts  1.74 us (1%)
    ppermute x56, waiting for transfers between devices, move(): return lax.ppermute(value, 'prow', pairs)  60.6 us
    ppermute x56, starting transfers between devices, move(): return lax.ppermute(value, 'prow', pairs)  47.7 us
    pallas_call x4, Pallas kernels, pack_level(): pl.pallas_call(functools.partial(pack_level_kernel, direction, base, rows...  7.62 us
    pallas_call x2, Pallas kernels, pack_coupling(): pl.pallas_call(kernel, out_shape=jax.ShapeDtypeStruct(shape, factor.dtype...  6.9 us
    pallas_call x8, Pallas kernels, local_call(): pl.pallas_call(kernel, out_shape=outs, in_specs=[pl.BlockSpec(memory_spac...  6.43 us
  transfers between devices with their start and end apart: 56, of which 24 were waited for; matrix products, arithmetic and copies ran while one was open for 0% of the time, Pallas kernels for 12%

profile of v1, /device:TPU:0, one launch (start us, length us, event | category | flops | bytes accessed | tf_op | source)
XLA Modules:
  0.0 132.1 jit_solution(4123138420768887755)
XLA Ops:
  1.7 4.1 %collective-permute-start.1 = (bf16[1,2,128,128]{3,2,1,0:T(8,128)(2,1)S(1)}, bf16[1,2,128,128]{3,2,1,0:T(8,128)(2,1)S(1)}, u32[]{:S(2)}, u32[]{:S(2)}) collective-permute-start(bf16[1,2,128,128]{3,2,1,0:T(8,128)(2,1)S(1)} %slice_bitcast_fusion), channel_id=1, source_target_pairs={{0,16},{1,17},{2,18},{3,19},{4,20},{5,21},{6,22},{7,23},{8,24},{9,... | collective-permute-start | bytes 196616 | tf_op jit(solution)/shard_map/ppermute | solution.py:146
  7.3 2.1 %collective-permute-done.1 = bf16[1,2,128,128]{3,2,1,0:T(8,128)(2,1)S(1)} collective-permute-done((bf16[1,2,128,128]{3,2,1,0:T(8,128)(2,1)S(1)}, bf16[1,2,128,128]{3,2,1,0:T(8,128)(2,1)S(1)}, u32[]{:S(2)}, u32[]{:S(2)}) %collective-permute-start.1) | collective-permute-done | bytes 65568 | tf_op jit(solution)/shard_map/ppermute | solution.py:146
  9.4 2.4 %collective-permute-done = bf16[1,2,128,128]{3,2,1,0:T(8,128)(2,1)S(1)} collective-permute-done((bf16[1,2,128,128]{3,2,1,0:T(8,128)(2,1)S(1)}, bf16[1,2,128,128]{3,2,1,0:T(8,128)(2,1)S(1)}, u32[]{:S(2)}, u32[]{:S(2)}) %collective-permute-start) | collective-permute-done | bytes 65568 | tf_op jit(solution)/shard_map/ppermute | solution.py:146
  15.4 4.1 %collective-permute-done.3.refs_2_ = bf16[3,2,128,128]{3,2,1,0:T(8,128)(2,1)S(1)} collective-permute-done((bf16[3,2,128,128]{3,2,1,0:T(8,128)(2,1)S(1)}, bf16[3,2,128,128]{3,2,1,0:T(8,128)(2,1)S(1)}, u32[]{:S(2)}, u32[]{:S(2)}) %collective-permute-start.3) | collective-permute-done | bytes 196640 | tf_op jit(solution)/shard_map/ppermute | solution.py:146
  19.5 3.3 %collective-permute-done.5.refs_4_ = bf16[3,2,128,128]{3,2,1,0:T(8,128)(2,1)S(1)} collective-permute-done((bf16[3,2,128,128]{3,2,1,0:T(8,128)(2,1)S(1)}, bf16[3,2,128,128]{3,2,1,0:T(8,128)(2,1)S(1)}, u32[]{:S(2)}, u32[]{:S(2)}) %collective-permute-start.5) | collective-permute-done | bytes 196640 | tf_op jit(solution)/shard_map/ppermute | solution.py:146
  24.0 2.1 %pack_level.4.refs_8_ = bf16[32,128,128]{2,1,0:T(8,128)(2,1)S(1)} custom-call(bf16[96,3,128,128]{3,2,1,0:T(8,128)(2,1)} %bitcast.30, s32[64]{0:T(128)S(1)} %copy-done.2), custom_call_target="tpu_custom_call" | custom-call | bytes 2097152 | tf_op jit(solution)/shard_map/pack_level/pallas_call | solution.py:66
  26.9 2.0 %collective-permute-start.11 = (bf16[1,2,128,128]{3,2,1,0:T(8,128)(2,1)S(1)}, bf16[1,2,128,128]{3,2,1,0:T(8,128)(2,1)S(1)}, u32[]{:S(2)}, u32[]{:S(2)}) collective-permute-start(bf16[1,2,128,128]{3,2,1,0:T(8,128)(2,1)S(1)} %bitcast.19), channel_id=1, source_target_pairs={{0,24},{1,25},{2,26},{3,27},{4,28},{5,29},{6,30},{7,31},{8,16},{9,... | collective-permute-start | bytes 196616 | tf_op jit(solution)/shard_map/ppermute | solution.py:146
  29.4 2.0 %collective-permute-start.9 = (bf16[1,2,128,128]{3,2,1,0:T(8,128)(2,1)S(1)}, bf16[1,2,128,128]{3,2,1,0:T(8,128)(2,1)S(1)}, u32[]{:S(2)}, u32[]{:S(2)}) collective-permute-start(bf16[1,2,128,128]{3,2,1,0:T(8,128)(2,1)S(1)} %bitcast.21), channel_id=1, source_target_pairs={{0,8},{1,9},{2,10},{3,11},{4,12},{5,13},{6,14},{7,15},{8,0},{9,1},... | collective-permute-start | bytes 196616 | tf_op jit(solution)/shard_map/ppermute | solution.py:146
  31.4 2.2 %collective-permute-done.11 = bf16[1,2,128,128]{3,2,1,0:T(8,128)(2,1)S(1)} collective-permute-done((bf16[1,2,128,128]{3,2,1,0:T(8,128)(2,1)S(1)}, bf16[1,2,128,128]{3,2,1,0:T(8,128)(2,1)S(1)}, u32[]{:S(2)}, u32[]{:S(2)}) %collective-permute-start.11) | collective-permute-done | bytes 65568 | tf_op jit(solution)/shard_map/ppermute | solution.py:146
  33.6 2.3 %collective-permute-done.10 = bf16[1,2,128,128]{3,2,1,0:T(8,128)(2,1)S(1)} collective-permute-done((bf16[1,2,128,128]{3,2,1,0:T(8,128)(2,1)S(1)}, bf16[1,2,128,128]{3,2,1,0:T(8,128)(2,1)S(1)}, u32[]{:S(2)}, u32[]{:S(2)}) %collective-permute-start.10) | collective-permute-done | bytes 65568 | tf_op jit(solution)/shard_map/ppermute | solution.py:146
  39.4 5.7 %collective-permute-done.13.refs_2_ = bf16[4,2,128,128]{3,2,1,0:T(8,128)(2,1)S(1)} collective-permute-done((bf16[4,2,128,128]{3,2,1,0:T(8,128)(2,1)S(1)}, bf16[4,2,128,128]{3,2,1,0:T(8,128)(2,1)S(1)}, u32[]{:S(2)}, u32[]{:S(2)}) %collective-permute-start.13) | collective-permute-done | bytes 262176 | tf_op jit(solution)/shard_map/ppermute | solution.py:146
  45.1 5.6 %collective-permute-done.15.refs_4_ = bf16[4,2,128,128]{3,2,1,0:T(8,128)(2,1)S(1)} collective-permute-done((bf16[4,2,128,128]{3,2,1,0:T(8,128)(2,1)S(1)}, bf16[4,2,128,128]{3,2,1,0:T(8,128)(2,1)S(1)}, u32[]{:S(2)}, u32[]{:S(2)}) %collective-permute-start.15) | collective-permute-done | bytes 262176 | tf_op jit(solution)/shard_map/ppermute | solution.py:146
  51.4 3.7 %pack_down.1.refs_8_ = bf16[64,128,128]{2,1,0:T(8,128)(2,1)S(1)} custom-call(bf16[96,3,128,128]{3,2,1,0:T(8,128)(2,1)} %bitcast.31, s32[64]{0:T(128)S(1)} %copy-done.3, s32[32]{0:T(128)S(1)} %copy-done.1, s32[5,1]{1,0:T(8,128)S(1)} %copy.9.parent, s32[32,5]{1,0:T(8,128)S(1)} %copy.10.pattern), custom_call_target="tpu_custom_call" | custom-call | bytes 4194304 | tf_op jit(solution)/shard_map/pack_down/pallas_call | solution.py:129
  56.7 2.4 %collective-permute-start.19 = (bf16[1,1,128,128]{3,2,1,0:T(8,128)(2,1)S(1)}, bf16[1,1,128,128]{3,2,1,0:T(8,128)(2,1)S(1)}, u32[]{:S(2)}, u32[]{:S(2)}) collective-permute-start(bf16[1,1,128,128]{3,2,1,0:T(8,128)(2,1)S(1)} %bitcast.17), channel_id=1, source_target_pairs={{0,8},{1,9},{2,10},{3,11},{4,12},{5,13},{6,14},{7,15},{8,16},{9,17... | collective-permute-start | bytes 98312 | tf_op jit(solution)/shard_map/ppermute | solution.py:146
  59.1 2.6 %collective-permute-done.20 = bf16[1,1,128,128]{3,2,1,0:T(8,128)(2,1)S(1)} collective-permute-done((bf16[1,1,128,128]{3,2,1,0:T(8,128)(2,1)S(1)}, bf16[1,1,128,128]{3,2,1,0:T(8,128)(2,1)S(1)}, u32[]{:S(2)}, u32[]{:S(2)}) %collective-permute-start.20) | collective-permute-done | bytes 32800 | tf_op jit(solution)/shard_map/ppermute | solution.py:146
  66.0 1.7 %collective-permute-done.22.refs_2_ = bf16[3,1,128,128]{3,2,1,0:T(8,128)(2,1)S(1)} collective-permute-done((bf16[3,1,128,128]{3,2,1,0:T(8,128)(2,1)S(1)}, bf16[3,1,128,128]{3,2,1,0:T(8,128)(2,1)S(1)}, u32[]{:S(2)}, u32[]{:S(2)}) %collective-permute-start.22) | collective-permute-done | bytes 98336 | tf_op jit(solution)/shard_map/ppermute | solution.py:146
  70.2 1.8 %pack_level.5.refs_8_ = bf16[16,128,128]{2,1,0:T(8,128)(2,1)S(1)} custom-call(bf16[96,3,128,128]{3,2,1,0:T(8,128)(2,1)} %bitcast.32, s32[32]{0:T(128)S(1)} %copy-done.1), custom_call_target="tpu_custom_call" | custom-call | bytes 1048576 | tf_op jit(solution)/shard_map/pack_level/pallas_call | solution.py:66
  73.7 2.4 %collective-permute-start.28 = (bf16[1,1,128,128]{3,2,1,0:T(8,128)(2,1)S(1)}, bf16[1,1,128,128]{3,2,1,0:T(8,128)(2,1)S(1)}, u32[]{:S(2)}, u32[]{:S(2)}) collective-permute-start(bf16[1,1,128,128]{3,2,1,0:T(8,128)(2,1)S(1)} %bitcast.24), channel_id=1, source_target_pairs={{0,24},{1,25},{2,26},{3,27},{4,28},{5,29},{6,30},{7,31},{8,0},{9,1... | collective-permute-start | bytes 98312 | tf_op jit(solution)/shard_map/ppermute | solution.py:146
  76.0 2.3 %collective-permute-done.29 = bf16[1,1,128,128]{3,2,1,0:T(8,128)(2,1)S(1)} collective-permute-done((bf16[1,1,128,128]{3,2,1,0:T(8,128)(2,1)S(1)}, bf16[1,1,128,128]{3,2,1,0:T(8,128)(2,1)S(1)}, u32[]{:S(2)}, u32[]{:S(2)}) %collective-permute-start.29) | collective-permute-done | bytes 32800 | tf_op jit(solution)/shard_map/ppermute | solution.py:146
  80.0 1.9 %collective-permute-start.35 = (bf16[3,1,128,128]{3,2,1,0:T(8,128)(2,1)S(1)}, bf16[3,1,128,128]{3,2,1,0:T(8,128)(2,1)S(1)}, u32[]{:S(2)}, u32[]{:S(2)}) collective-permute-start(bf16[3,1,128,128]{3,2,1,0:T(8,128)(2,1)S(1)} %pad_maximum_fusion.5.refs_0_), channel_id=1, source_target_pairs={{0,6},{1,7},{2,4},{3,5},{4,2},{5,3},{6,0},{7,1},{8,14},{9,15},{10,... | collective-permute-start | bytes 294920 | tf_op jit(solution)/shard_map/ppermute | solution.py:146
  83.7 2.0 %collective-permute-done.33.refs_4_ = bf16[3,1,128,128]{3,2,1,0:T(8,128)(2,1)S(1)} collective-permute-done((bf16[3,1,128,128]{3,2,1,0:T(8,128)(2,1)S(1)}, bf16[3,1,128,128]{3,2,1,0:T(8,128)(2,1)S(1)}, u32[]{:S(2)}, u32[]{:S(2)}) %collective-permute-start.33) | collective-permute-done | bytes 98336 | tf_op jit(solution)/shard_map/ppermute | solution.py:146
  88.3 2.7 %collective-permute-start.39 = (bf16[1,1,128,128]{3,2,1,0:T(8,128)(2,1)S(1)}, bf16[1,1,128,128]{3,2,1,0:T(8,128)(2,1)S(1)}, u32[]{:S(2)}, u32[]{:S(2)}) collective-permute-start(bf16[1,1,128,128]{3,2,1,0:T(8,128)(2,1)S(1)} %bitcast.26), channel_id=1, source_target_pairs={{0,24},{1,25},{2,26},{3,27},{4,28},{5,29},{6,30},{7,31},{8,16},{9,... | collective-permute-start | bytes 98312 | tf_op jit(solution)/shard_map/ppermute | solution.py:146
  91.0 1.8 %collective-permute-start.37 = (bf16[1,1,128,128]{3,2,1,0:T(8,128)(2,1)S(1)}, bf16[1,1,128,128]{3,2,1,0:T(8,128)(2,1)S(1)}, u32[]{:S(2)}, u32[]{:S(2)}) collective-permute-start(bf16[1,1,128,128]{3,2,1,0:T(8,128)(2,1)S(1)} %bitcast.28), channel_id=1, source_target_pairs={{0,8},{1,9},{2,10},{3,11},{4,12},{5,13},{6,14},{7,15},{8,0},{9,1},... | collective-permute-start | bytes 98312 | tf_op jit(solution)/shard_map/ppermute | solution.py:146
  99.4 2.4 %collective-permute-done.41.refs_2_ = bf16[4,1,128,128]{3,2,1,0:T(8,128)(2,1)S(1)} collective-permute-done((bf16[4,1,128,128]{3,2,1,0:T(8,128)(2,1)S(1)}, bf16[4,1,128,128]{3,2,1,0:T(8,128)(2,1)S(1)}, u32[]{:S(2)}, u32[]{:S(2)}) %collective-permute-start.41) | collective-permute-done | bytes 131104 | tf_op jit(solution)/shard_map/ppermute | solution.py:146
  101.8 3.3 %collective-permute-done.43.refs_4_ = bf16[4,1,128,128]{3,2,1,0:T(8,128)(2,1)S(1)} collective-permute-done((bf16[4,1,128,128]{3,2,1,0:T(8,128)(2,1)S(1)}, bf16[4,1,128,128]{3,2,1,0:T(8,128)(2,1)S(1)}, u32[]{:S(2)}, u32[]{:S(2)}) %collective-permute-start.43) | collective-permute-done | bytes 131104 | tf_op jit(solution)/shard_map/ppermute | solution.py:146
  105.6 3.2 %pack_up.1.refs_8_ = bf16[2,32,128,128]{3,2,1,0:T(8,128)(2,1)S(1)} custom-call(bf16[96,3,128,128]{3,2,1,0:T(8,128)(2,1)} %bitcast.34, s32[64]{0:T(128)S(1)} %copy-done.3, s32[32]{0:T(128)S(1)} %copy-done.1, s32[5,1]{1,0:T(8,128)S(1)} %copy.9.parent, s32[32,5]{1,0:T(8,128)S(1)} %copy.10.pattern), custom_call_target="tpu_custom_call" | custom-call | bytes 4194304 | tf_op jit(solution)/shard_map/pack_up/pallas_call | solution.py:129
  109.8 2.0 %collective-permute-start.48 = (bf16[1,2,128,128]{3,2,1,0:T(8,128)(2,1)S(1)}, bf16[1,2,128,128]{3,2,1,0:T(8,128)(2,1)S(1)}, u32[]{:S(2)}, u32[]{:S(2)}) collective-permute-start(bf16[1,2,128,128]{3,2,1,0:T(8,128)(2,1)S(1)} %bitcast.13), channel_id=1, source_target_pairs={{0,16},{1,17},{2,18},{3,19},{4,20},{5,21},{6,22},{7,23},{8,24},{9,... | collective-permute-start | bytes 196616 | tf_op jit(solution)/shard_map/ppermute | solution.py:146
  112.9 3.6 %collective-permute-done.48 = bf16[1,2,128,128]{3,2,1,0:T(8,128)(2,1)S(1)} collective-permute-done((bf16[1,2,128,128]{3,2,1,0:T(8,128)(2,1)S(1)}, bf16[1,2,128,128]{3,2,1,0:T(8,128)(2,1)S(1)}, u32[]{:S(2)}, u32[]{:S(2)}) %collective-permute-start.48) | collective-permute-done | bytes 65568 | tf_op jit(solution)/shard_map/ppermute | solution.py:146
  118.3 2.1 %collective-permute-start.54 = (bf16[3,2,128,128]{3,2,1,0:T(8,128)(2,1)S(1)}, bf16[3,2,128,128]{3,2,1,0:T(8,128)(2,1)S(1)}, u32[]{:S(2)}, u32[]{:S(2)}) collective-permute-start(bf16[3,2,128,128]{3,2,1,0:T(8,128)(2,1)S(1)} %pad_maximum_fusion.2.refs_0_), channel_id=1, source_target_pairs={{0,6},{1,7},{2,4},{3,5},{4,2},{5,3},{6,0},{7,1},{8,14},{9,15},{10,... | collective-permute-start | bytes 589832 | tf_op jit(solution)/shard_map/ppermute | solution.py:146
  120.4 4.3 %collective-permute-done.50.refs_2_ = bf16[3,2,128,128]{3,2,1,0:T(8,128)(2,1)S(1)} collective-permute-done((bf16[3,2,128,128]{3,2,1,0:T(8,128)(2,1)S(1)}, bf16[3,2,128,128]{3,2,1,0:T(8,128)(2,1)S(1)}, u32[]{:S(2)}, u32[]{:S(2)}) %collective-permute-start.50) | collective-permute-done | bytes 196640 | tf_op jit(solution)/shard_map/ppermute | solution.py:146
  125.3 2.3 %collective-permute-done.54.refs_6_ = bf16[3,2,128,128]{3,2,1,0:T(8,128)(2,1)S(1)} collective-permute-done((bf16[3,2,128,128]{3,2,1,0:T(8,128)(2,1)S(1)}, bf16[3,2,128,128]{3,2,1,0:T(8,128)(2,1)S(1)}, u32[]{:S(2)}, u32[]{:S(2)}) %collective-permute-start.54) | collective-permute-done | bytes 196640 | tf_op jit(solution)/shard_map/ppermute | solution.py:146
  127.6 2.1 %pack_level.7.refs_8_ = bf16[32,128,128]{2,1,0:T(8,128)(2,1)S(1)} custom-call(bf16[96,3,128,128]{3,2,1,0:T(8,128)(2,1)} %bitcast.35, s32[64]{0:T(128)S(1)} %copy-done.3), custom_call_target="tpu_custom_call" | custom-call | bytes 2097152 | tf_op jit(solution)/shard_map/pack_level/pallas_call | solution.py:66
  (115 shorter events, 42.6 us)
Async XLA Ops:
  1.7 7.8 %collective-permute-start.1 = (bf16[1,2,128,128]{3,2,1,0:T(8,128)(2,1)S(1)}, bf16[1,2,128,128]{3,2,1,0:T(8,128)(2,1)S(1)}, u32[]{:S(2)}, u32[]{:S(2)}) collective-permute-start(bf16[1,2,128,128]{3,2,1,0:T(8,128)(2,1)S(1)} %slice_bitcast_fusion), channel_id=1, source_target_pairs={{0,16},{1,17},{2,18},{3,19},{4,20},{5,21},{6,22},{7,23},{8,24},{9,... | collective-permute-start | bytes 196616 | tf_op jit(solution)/shard_map/ppermute | solution.py:146
  5.8 6.1 %collective-permute-start = (bf16[1,2,128,128]{3,2,1,0:T(8,128)(2,1)S(1)}, bf16[1,2,128,128]{3,2,1,0:T(8,128)(2,1)S(1)}, u32[]{:S(2)}, u32[]{:S(2)}) collective-permute-start(bf16[1,2,128,128]{3,2,1,0:T(8,128)(2,1)S(1)} %slice_bitcast_fusion), channel_id=1, source_target_pairs={{0,8},{1,9},{2,10},{3,11},{4,12},{5,13},{6,14},{7,15},{8,16},{9,17... | collective-permute-start | bytes 196616 | tf_op jit(solution)/shard_map/ppermute | solution.py:146
  11.9 7.7 %collective-permute-start.3 = (bf16[3,2,128,128]{3,2,1,0:T(8,128)(2,1)S(1)}, bf16[3,2,128,128]{3,2,1,0:T(8,128)(2,1)S(1)}, u32[]{:S(2)}, u32[]{:S(2)}) collective-permute-start(bf16[3,2,128,128]{3,2,1,0:T(8,128)(2,1)S(1)} %pad_maximum_fusion.1.refs_0_), channel_id=1, source_target_pairs={{0,2},{1,3},{2,0},{3,1},{4,6},{5,7},{6,4},{7,5},{8,10},{9,11},{10,... | collective-permute-start | bytes 589832 | tf_op jit(solution)/shard_map/ppermute | solution.py:146
  13.4 9.4 %collective-permute-start.5 = (bf16[3,2,128,128]{3,2,1,0:T(8,128)(2,1)S(1)}, bf16[3,2,128,128]{3,2,1,0:T(8,128)(2,1)S(1)}, u32[]{:S(2)}, u32[]{:S(2)}) collective-permute-start(bf16[3,2,128,128]{3,2,1,0:T(8,128)(2,1)S(1)} %pad_maximum_fusion.1.refs_0_), channel_id=1, source_target_pairs={{0,4},{1,5},{2,6},{3,7},{4,0},{5,1},{6,2},{7,3},{8,12},{9,13},{10,... | collective-permute-start | bytes 589832 | tf_op jit(solution)/shard_map/ppermute | solution.py:146
  14.9 7.9 %collective-permute-start.7 = (bf16[3,2,128,128]{3,2,1,0:T(8,128)(2,1)S(1)}, bf16[3,2,128,128]{3,2,1,0:T(8,128)(2,1)S(1)}, u32[]{:S(2)}, u32[]{:S(2)}) collective-permute-start(bf16[3,2,128,128]{3,2,1,0:T(8,128)(2,1)S(1)} %pad_maximum_fusion.1.refs_0_), channel_id=1, source_target_pairs={{0,6},{1,7},{2,4},{3,5},{4,2},{5,3},{6,0},{7,1},{8,14},{9,15},{10,... | collective-permute-start | bytes 589832 | tf_op jit(solution)/shard_map/ppermute | solution.py:146
  15.4 10.7 %collective-permute-start.2 = (bf16[3,2,128,128]{3,2,1,0:T(8,128)(2,1)S(1)}, bf16[3,2,128,128]{3,2,1,0:T(8,128)(2,1)S(1)}, u32[]{:S(2)}, u32[]{:S(2)}) collective-permute-start(bf16[3,2,128,128]{3,2,1,0:T(8,128)(2,1)S(1)} %pad_maximum_fusion.1.refs_0_), channel_id=1, source_target_pairs={{0,1},{1,0},{2,3},{3,2},{4,5},{5,4},{6,7},{7,6},{8,9},{9,8},{10,11... | collective-permute-start | bytes 589832 | tf_op jit(solution)/shard_map/ppermute | solution.py:146
  19.5 6.6 %collective-permute-start.4 = (bf16[3,2,128,128]{3,2,1,0:T(8,128)(2,1)S(1)}, bf16[3,2,128,128]{3,2,1,0:T(8,128)(2,1)S(1)}, u32[]{:S(2)}, u32[]{:S(2)}) collective-permute-start(bf16[3,2,128,128]{3,2,1,0:T(8,128)(2,1)S(1)} %collective-permute-done.3.refs_2_), channel_id=1, source_target_pairs={{0,1},{1,0},{2,3},{3,2},{4,5},{5,4},{6,7},{7,6},{8,9},{9,8},{10,11... | collective-permute-start | bytes 589832 | tf_op jit(solution)/shard_map/ppermute | solution.py:146
  26.9 6.6 %collective-permute-start.11 = (bf16[1,2,128,128]{3,2,1,0:T(8,128)(2,1)S(1)}, bf16[1,2,128,128]{3,2,1,0:T(8,128)(2,1)S(1)}, u32[]{:S(2)}, u32[]{:S(2)}) collective-permute-start(bf16[1,2,128,128]{3,2,1,0:T(8,128)(2,1)S(1)} %bitcast.19), channel_id=1, source_target_pairs={{0,24},{1,25},{2,26},{3,27},{4,28},{5,29},{6,30},{7,31},{8,16},{9,... | collective-permute-start | bytes 196616 | tf_op jit(solution)/shard_map/ppermute | solution.py:146
  28.9 6.9 %collective-permute-start.10 = (bf16[1,2,128,128]{3,2,1,0:T(8,128)(2,1)S(1)}, bf16[1,2,128,128]{3,2,1,0:T(8,128)(2,1)S(1)}, u32[]{:S(2)}, u32[]{:S(2)}) collective-permute-start(bf16[1,2,128,128]{3,2,1,0:T(8,128)(2,1)S(1)} %bitcast.20), channel_id=1, source_target_pairs={{0,16},{1,17},{2,18},{3,19},{4,20},{5,21},{6,22},{7,23},{8,24},{9,... | collective-permute-start | bytes 196616 | tf_op jit(solution)/shard_map/ppermute | solution.py:146
  29.4 6.4 %collective-permute-start.9 = (bf16[1,2,128,128]{3,2,1,0:T(8,128)(2,1)S(1)}, bf16[1,2,128,128]{3,2,1,0:T(8,128)(2,1)S(1)}, u32[]{:S(2)}, u32[]{:S(2)}) collective-permute-start(bf16[1,2,128,128]{3,2,1,0:T(8,128)(2,1)S(1)} %bitcast.21), channel_id=1, source_target_pairs={{0,8},{1,9},{2,10},{3,11},{4,12},{5,13},{6,14},{7,15},{8,0},{9,1},... | collective-permute-start | bytes 196616 | tf_op jit(solution)/shard_map/ppermute | solution.py:146
  35.9 9.2 %collective-permute-start.13 = (bf16[4,2,128,128]{3,2,1,0:T(8,128)(2,1)S(1)}, bf16[4,2,128,128]{3,2,1,0:T(8,128)(2,1)S(1)}, u32[]{:S(2)}, u32[]{:S(2)}) collective-permute-start(bf16[4,2,128,128]{3,2,1,0:T(8,128)(2,1)S(1)} %pad_maximum_fusion.refs_0_), channel_id=1, source_target_pairs={{0,2},{1,3},{2,0},{3,1},{4,6},{5,7},{6,4},{7,5},{8,10},{9,11},{10,... | collective-permute-start | bytes 786440 | tf_op jit(solution)/shard_map/ppermute | solution.py:146
  37.3 13.5 %collective-permute-start.15 = (bf16[4,2,128,128]{3,2,1,0:T(8,128)(2,1)S(1)}, bf16[4,2,128,128]{3,2,1,0:T(8,128)(2,1)S(1)}, u32[]{:S(2)}, u32[]{:S(2)}) collective-permute-start(bf16[4,2,128,128]{3,2,1,0:T(8,128)(2,1)S(1)} %pad_maximum_fusion.refs_0_), channel_id=1, source_target_pairs={{0,4},{1,5},{2,6},{3,7},{4,0},{5,1},{6,2},{7,3},{8,12},{9,13},{10,... | collective-permute-start | bytes 786440 | tf_op jit(solution)/shard_map/ppermute | solution.py:146
  38.1 12.6 %collective-permute-start.17 = (bf16[4,2,128,128]{3,2,1,0:T(8,128)(2,1)S(1)}, bf16[4,2,128,128]{3,2,1,0:T(8,128)(2,1)S(1)}, u32[]{:S(2)}, u32[]{:S(2)}) collective-permute-start(bf16[4,2,128,128]{3,2,1,0:T(8,128)(2,1)S(1)} %pad_maximum_fusion.refs_0_), channel_id=1, source_target_pairs={{0,6},{1,7},{2,4},{3,5},{4,2},{5,3},{6,0},{7,1},{8,14},{9,15},{10,... | collective-permute-start | bytes 786440 | tf_op jit(solution)/shard_map/ppermute | solution.py:146
  39.4 15.7 %collective-permute-start.12 = (bf16[4,2,128,128]{3,2,1,0:T(8,128)(2,1)S(1)}, bf16[4,2,128,128]{3,2,1,0:T(8,128)(2,1)S(1)}, u32[]{:S(2)}, u32[]{:S(2)}) collective-permute-start(bf16[4,2,128,128]{3,2,1,0:T(8,128)(2,1)S(1)} %pad_maximum_fusion.refs_0_), channel_id=1, source_target_pairs={{0,1},{1,0},{2,3},{3,2},{4,5},{5,4},{6,7},{7,6},{8,9},{9,8},{10,11... | collective-permute-start | bytes 786440 | tf_op jit(solution)/shard_map/ppermute | solution.py:146
  45.1 10.1 %collective-permute-start.14 = (bf16[4,2,128,128]{3,2,1,0:T(8,128)(2,1)S(1)}, bf16[4,2,128,128]{3,2,1,0:T(8,128)(2,1)S(1)}, u32[]{:S(2)}, u32[]{:S(2)}) collective-permute-start(bf16[4,2,128,128]{3,2,1,0:T(8,128)(2,1)S(1)} %collective-permute-done.13.refs_2_), channel_id=1, source_target_pairs={{0,1},{1,0},{2,3},{3,2},{4,5},{5,4},{6,7},{7,6},{8,9},{9,8},{10,11... | collective-permute-start | bytes 786440 | tf_op jit(solution)/shard_map/ppermute | solution.py:146
  66.0 6.0 %collective-permute-start.21 = (bf16[3,1,128,128]{3,2,1,0:T(8,128)(2,1)S(1)}, bf16[3,1,128,128]{3,2,1,0:T(8,128)(2,1)S(1)}, u32[]{:S(2)}, u32[]{:S(2)}) collective-permute-start(bf16[3,1,128,128]{3,2,1,0:T(8,128)(2,1)S(1)} %pad_maximum_fusion.4.refs_0_), channel_id=1, source_target_pairs={{0,1},{1,0},{2,3},{3,2},{4,5},{5,4},{6,7},{7,6},{8,9},{9,8},{10,11... | collective-permute-start | bytes 294920 | tf_op jit(solution)/shard_map/ppermute | solution.py:146
  72.5 5.9 %collective-permute-start.29 = (bf16[1,1,128,128]{3,2,1,0:T(8,128)(2,1)S(1)}, bf16[1,1,128,128]{3,2,1,0:T(8,128)(2,1)S(1)}, u32[]{:S(2)}, u32[]{:S(2)}) collective-permute-start(bf16[1,1,128,128]{3,2,1,0:T(8,128)(2,1)S(1)} %bitcast.23), channel_id=1, source_target_pairs={{0,16},{1,17},{2,18},{3,19},{4,20},{5,21},{6,22},{7,23},{8,24},{9,... | collective-permute-start | bytes 98312 | tf_op jit(solution)/shard_map/ppermute | solution.py:146
  79.0 6.7 %collective-permute-start.33 = (bf16[3,1,128,128]{3,2,1,0:T(8,128)(2,1)S(1)}, bf16[3,1,128,128]{3,2,1,0:T(8,128)(2,1)S(1)}, u32[]{:S(2)}, u32[]{:S(2)}) collective-permute-start(bf16[3,1,128,128]{3,2,1,0:T(8,128)(2,1)S(1)} %pad_maximum_fusion.5.refs_0_), channel_id=1, source_target_pairs={{0,4},{1,5},{2,6},{3,7},{4,0},{5,1},{6,2},{7,3},{8,12},{9,13},{10,... | collective-permute-start | bytes 294920 | tf_op jit(solution)/shard_map/ppermute | solution.py:146
  82.0 5.8 %collective-permute-start.30 = (bf16[3,1,128,128]{3,2,1,0:T(8,128)(2,1)S(1)}, bf16[3,1,128,128]{3,2,1,0:T(8,128)(2,1)S(1)}, u32[]{:S(2)}, u32[]{:S(2)}) collective-permute-start(bf16[3,1,128,128]{3,2,1,0:T(8,128)(2,1)S(1)} %pad_maximum_fusion.5.refs_0_), channel_id=1, source_target_pairs={{0,1},{1,0},{2,3},{3,2},{4,5},{5,4},{6,7},{7,6},{8,9},{9,8},{10,11... | collective-permute-start | bytes 294920 | tf_op jit(solution)/shard_map/ppermute | solution.py:146
  88.3 5.8 %collective-permute-start.39 = (bf16[1,1,128,128]{3,2,1,0:T(8,128)(2,1)S(1)}, bf16[1,1,128,128]{3,2,1,0:T(8,128)(2,1)S(1)}, u32[]{:S(2)}, u32[]{:S(2)}) collective-permute-start(bf16[1,1,128,128]{3,2,1,0:T(8,128)(2,1)S(1)} %bitcast.26), channel_id=1, source_target_pairs={{0,24},{1,25},{2,26},{3,27},{4,28},{5,29},{6,30},{7,31},{8,16},{9,... | collective-permute-start | bytes 98312 | tf_op jit(solution)/shard_map/ppermute | solution.py:146
  95.8 5.9 %collective-permute-start.41 = (bf16[4,1,128,128]{3,2,1,0:T(8,128)(2,1)S(1)}, bf16[4,1,128,128]{3,2,1,0:T(8,128)(2,1)S(1)}, u32[]{:S(2)}, u32[]{:S(2)}) collective-permute-start(bf16[4,1,128,128]{3,2,1,0:T(8,128)(2,1)S(1)} %pad_maximum_fusion.3.refs_0_), channel_id=1, source_target_pairs={{0,2},{1,3},{2,0},{3,1},{4,6},{5,7},{6,4},{7,5},{8,10},{9,11},{10,... | collective-permute-start | bytes 393224 | tf_op jit(solution)/shard_map/ppermute | solution.py:146
  97.3 7.8 %collective-permute-start.43 = (bf16[4,1,128,128]{3,2,1,0:T(8,128)(2,1)S(1)}, bf16[4,1,128,128]{3,2,1,0:T(8,128)(2,1)S(1)}, u32[]{:S(2)}, u32[]{:S(2)}) collective-permute-start(bf16[4,1,128,128]{3,2,1,0:T(8,128)(2,1)S(1)} %pad_maximum_fusion.3.refs_0_), channel_id=1, source_target_pairs={{0,4},{1,5},{2,6},{3,7},{4,0},{5,1},{6,2},{7,3},{8,12},{9,13},{10,... | collective-permute-start | bytes 393224 | tf_op jit(solution)/shard_map/ppermute | solution.py:146
  98.8 6.3 %collective-permute-start.45 = (bf16[4,1,128,128]{3,2,1,0:T(8,128)(2,1)S(1)}, bf16[4,1,128,128]{3,2,1,0:T(8,128)(2,1)S(1)}, u32[]{:S(2)}, u32[]{:S(2)}) collective-permute-start(bf16[4,1,128,128]{3,2,1,0:T(8,128)(2,1)S(1)} %pad_maximum_fusion.3.refs_0_), channel_id=1, source_target_pairs={{0,6},{1,7},{2,4},{3,5},{4,2},{5,3},{6,0},{7,1},{8,14},{9,15},{10,... | collective-permute-start | bytes 393224 | tf_op jit(solution)/shard_map/ppermute | solution.py:146
  99.4 9.4 %collective-permute-start.40 = (bf16[4,1,128,128]{3,2,1,0:T(8,128)(2,1)S(1)}, bf16[4,1,128,128]{3,2,1,0:T(8,128)(2,1)S(1)}, u32[]{:S(2)}, u32[]{:S(2)}) collective-permute-start(bf16[4,1,128,128]{3,2,1,0:T(8,128)(2,1)S(1)} %pad_maximum_fusion.3.refs_0_), channel_id=1, source_target_pairs={{0,1},{1,0},{2,3},{3,2},{4,5},{5,4},{6,7},{7,6},{8,9},{9,8},{10,11... | collective-permute-start | bytes 393224 | tf_op jit(solution)/shard_map/ppermute | solution.py:146
  101.8 7.0 %collective-permute-start.42 = (bf16[4,1,128,128]{3,2,1,0:T(8,128)(2,1)S(1)}, bf16[4,1,128,128]{3,2,1,0:T(8,128)(2,1)S(1)}, u32[]{:S(2)}, u32[]{:S(2)}) collective-permute-start(bf16[4,1,128,128]{3,2,1,0:T(8,128)(2,1)S(1)} %collective-permute-done.41.refs_2_), channel_id=1, source_target_pairs={{0,1},{1,0},{2,3},{3,2},{4,5},{5,4},{6,7},{7,6},{8,9},{9,8},{10,11... | collective-permute-start | bytes 393224 | tf_op jit(solution)/shard_map/ppermute | solution.py:146
  109.8 6.6 %collective-permute-start.48 = (bf16[1,2,128,128]{3,2,1,0:T(8,128)(2,1)S(1)}, bf16[1,2,128,128]{3,2,1,0:T(8,128)(2,1)S(1)}, u32[]{:S(2)}, u32[]{:S(2)}) collective-permute-start(bf16[1,2,128,128]{3,2,1,0:T(8,128)(2,1)S(1)} %bitcast.13), channel_id=1, source_target_pairs={{0,16},{1,17},{2,18},{3,19},{4,20},{5,21},{6,22},{7,23},{8,24},{9,... | collective-permute-start | bytes 196616 | tf_op jit(solution)/shard_map/ppermute | solution.py:146
  116.9 7.9 %collective-permute-start.50 = (bf16[3,2,128,128]{3,2,1,0:T(8,128)(2,1)S(1)}, bf16[3,2,128,128]{3,2,1,0:T(8,128)(2,1)S(1)}, u32[]{:S(2)}, u32[]{:S(2)}) collective-permute-start(bf16[3,2,128,128]{3,2,1,0:T(8,128)(2,1)S(1)} %pad_maximum_fusion.2.refs_0_), channel_id=1, source_target_pairs={{0,2},{1,3},{2,0},{3,1},{4,6},{5,7},{6,4},{7,5},{8,10},{9,11},{10,... | collective-permute-start | bytes 589832 | tf_op jit(solution)/shard_map/ppermute | solution.py:146
  117.3 7.5 %collective-permute-start.52 = (bf16[3,2,128,128]{3,2,1,0:T(8,128)(2,1)S(1)}, bf16[3,2,128,128]{3,2,1,0:T(8,128)(2,1)S(1)}, u32[]{:S(2)}, u32[]{:S(2)}) collective-permute-start(bf16[3,2,128,128]{3,2,1,0:T(8,128)(2,1)S(1)} %pad_maximum_fusion.2.refs_0_), channel_id=1, source_target_pairs={{0,4},{1,5},{2,6},{3,7},{4,0},{5,1},{6,2},{7,3},{8,12},{9,13},{10,... | collective-permute-start | bytes 589832 | tf_op jit(solution)/shard_map/ppermute | solution.py:146
  118.3 9.3 %collective-permute-start.54 = (bf16[3,2,128,128]{3,2,1,0:T(8,128)(2,1)S(1)}, bf16[3,2,128,128]{3,2,1,0:T(8,128)(2,1)S(1)}, u32[]{:S(2)}, u32[]{:S(2)}) collective-permute-start(bf16[3,2,128,128]{3,2,1,0:T(8,128)(2,1)S(1)} %pad_maximum_fusion.2.refs_0_), channel_id=1, source_target_pairs={{0,6},{1,7},{2,4},{3,5},{4,2},{5,3},{6,0},{7,1},{8,14},{9,15},{10,... | collective-permute-start | bytes 589832 | tf_op jit(solution)/shard_map/ppermute | solution.py:146
  120.4 10.1 %collective-permute-start.49 = (bf16[3,2,128,128]{3,2,1,0:T(8,128)(2,1)S(1)}, bf16[3,2,128,128]{3,2,1,0:T(8,128)(2,1)S(1)}, u32[]{:S(2)}, u32[]{:S(2)}) collective-permute-start(bf16[3,2,128,128]{3,2,1,0:T(8,128)(2,1)S(1)} %pad_maximum_fusion.2.refs_0_), channel_id=1, source_target_pairs={{0,1},{1,0},{2,3},{3,2},{4,5},{5,4},{6,7},{7,6},{8,9},{9,8},{10,11... | collective-permute-start | bytes 589832 | tf_op jit(solution)/shard_map/ppermute | solution.py:146
  124.8 5.7 %collective-permute-start.51 = (bf16[3,2,128,128]{3,2,1,0:T(8,128)(2,1)S(1)}, bf16[3,2,128,128]{3,2,1,0:T(8,128)(2,1)S(1)}, u32[]{:S(2)}, u32[]{:S(2)}) collective-permute-start(bf16[3,2,128,128]{3,2,1,0:T(8,128)(2,1)S(1)} %collective-permute-done.50.refs_2_), channel_id=1, source_target_pairs={{0,1},{1,0},{2,3},{3,2},{4,5},{5,4},{6,7},{7,6},{8,9},{9,8},{10,11... | collective-permute-start | bytes 589832 | tf_op jit(solution)/shard_map/ppermute | solution.py:146
  124.8 5.7 %collective-permute-start.53 = (bf16[3,2,128,128]{3,2,1,0:T(8,128)(2,1)S(1)}, bf16[3,2,128,128]{3,2,1,0:T(8,128)(2,1)S(1)}, u32[]{:S(2)}, u32[]{:S(2)}) collective-permute-start(bf16[3,2,128,128]{3,2,1,0:T(8,128)(2,1)S(1)} %collective-permute-done.52.refs_4_), channel_id=1, source_target_pairs={{0,1},{1,0},{2,3},{3,2},{4,5},{5,4},{6,7},{7,6},{8,9},{9,8},{10,11... | collective-permute-start | bytes 589832 | tf_op jit(solution)/shard_map/ppermute | solution.py:146
  (30 other events, 302.2 us)

commit v2 on v1

--- a/solution.py
+++ b/solution.py
@@ -139,7 +139,7 @@
     )(factor, *tables)
 
 
-def gather(block, shifts):
+def gather(block, shifts, table, pack):
     total = PLANE * PLANES
 
     def move(value, pairs):
@@ -152,12 +152,14 @@
         else:
             pairs = [(i, (i + PLANE * shift[1]) % total) for i in range(total)]
         parts.append(move(block[None], pairs))
-    pieces = {0: jnp.concatenate(parts, 0)}
+    packed = pack(lax.optimization_barrier((table, block))[0])
+    stacked, packed = lax.optimization_barrier((jnp.concatenate(parts, 0), packed))
+    pieces = {0: stacked}
     for k in (6, 2, 4):
         pieces[k] = move(pieces[0], [(i, i ^ k) for i in range(total)])
     for k in (0, 6, 2, 4):
         pieces[k + 1] = move(pieces[k], [(i, i ^ 1) for i in range(total)])
-    return [pieces[k] for k in range(PLANE)]
+    return [pieces[k] for k in range(PLANE)], packed
 
 
 def copy_window(pieces, xs, block, start, direction):
@@ -205,7 +207,8 @@
                 source = row * PLANE * PLANES + (plane ^ along) * PLANE + (offset ^ k)
                 xs[:, pl.ds(pl.multiple_of(source * size, size), size)] = pieces[k][along, row]
     result = dot(xs[...], factor[...].reshape(2 * PLANE * PLANES * size, size))
-    out[0] = (rhs[2].astype(jnp.float32) - result).astype(out.dtype)
+    rounded = result.astype(out.dtype).astype(jnp.float32)
+    out[0] = (rhs[2].astype(jnp.float32) - rounded).astype(out.dtype)
 
 
 def upper_kernel(direction, *refs):
@@ -231,7 +234,8 @@
     for row in range(2):
         result = dot(xs[...], factor[row].reshape(PLANE * PLANES * size, size))
         known = solved[row].astype(out.dtype).astype(jnp.float32)
-        out[row] = (known - result).astype(out.dtype)
+        rounded = result.astype(out.dtype).astype(jnp.float32)
+        out[row] = (known - rounded).astype(out.dtype)
 
 
 def backward_lower_kernel(*refs):
@@ -290,37 +294,65 @@
     backward = (("shift", -1), ("shift", -2))
     whole = (("xor", 1), ("xor", 2), ("xor", 3))
 
-    pieces = gather(own[:2], forward)
-    pack_l1 = pack_level(lower, lower_snode, 1, 0, 2, 0, 2 * total)
+    def pack_l1(table):
+        return pack_level(lower, table, 1, 0, 2, 0, 2 * total)
+
+    def pack_c(table):
+        return pack_coupling(
+            pack_down_kernel,
+            "pack_down",
+            (2 * total, size, size),
+            pltpu.SemaphoreType.DMA,
+            lower,
+            table,
+            *tables[1:],
+        )
+
+    def pack_l2(table):
+        return pack_level(lower, table, 1, 2 * total, 1, 2, total)
+
+    def pack_u2(table):
+        return pack_level(upper, table, -1, 2 * total, 1, 2, total)
+
+    def pack_k(table):
+        return pack_coupling(
+            pack_up_kernel,
+            "pack_up",
+            (2, total, size, size),
+            pltpu.SemaphoreType.DMA((2,)),
+            upper,
+            table,
+            *tables[1:],
+        )
+
+    def pack_u1(table):
+        return pack_level(upper, table, -1, 0, 2, 0, 2 * total)
+
+    pieces, packed = gather(own[:2], forward, lower_snode, pack_l1)
     solved, known = local_call(
         forward_lower_kernel,
         "forward_lower",
         [((2, width, size), f32), ((2, width, size), bf16)],
-        [*pieces, pack_l1],
+        [*pieces, packed],
         SPAN * size,
     )
-    pieces = gather(known, whole)
-    pack_c = pack_coupling(
-        pack_down_kernel, "pack_down", (2 * total, size, size), pltpu.SemaphoreType.DMA, lower, *tables
-    )
+    pieces, packed = gather(known, whole, lower_snode, pack_c)
     (difference,) = local_call(
         coupling_kernel,
         "coupling",
         [((1, width, size), bf16)],
-        [*pieces, pack_c, own],
+        [*pieces, packed, own],
         2 * total * size,
     )
-    pieces = gather(difference, forward)
-    pack_l2 = pack_level(lower, upper_snode, 1, 2 * total, 1, 2, total)
+    pieces, packed = gather(difference, forward, upper_snode, pack_l2)
     forward_upper, upper_known = local_call(
         functools.partial(upper_kernel, 1),
         "forward_upper",
         [((1, width, size), f32), ((1, width, size), bf16)],
-        [*pieces, pack_l2],
+        [*pieces, packed],
         SPAN * size,
     )
-    pieces = gather(upper_known, backward)
-    pack_u2 = pack_level(upper, upper_snode, -1, 2 * total, 1, 2, total)
+    pieces, packed = gather(upper_known, backward, upper_snode, pack_u2)
     (forward_solution,) = local_call(
         forward_out_kernel,
         "forward_out",
@@ -331,27 +363,23 @@
         functools.partial(upper_kernel, -1),
         "backward_upper",
         [((1, width, size), f32), ((1, width, size), bf16)],
-        [*pieces, pack_u2],
+        [*pieces, packed],
         SPAN * size,
     )
-    pieces = gather(back_known, whole)
-    pack_k = pack_coupling(
-        pack_up_kernel, "pack_up", (2, total, size, size), pltpu.SemaphoreType.DMA((2,)), upper, *tables
-    )
+    pieces, packed = gather(back_known, whole, lower_snode, pack_k)
     (remainder,) = local_call(
         correction_kernel,
         "correction",
         [((2, width, size), bf16)],
-        [*pieces, pack_k, solved],
+        [*pieces, packed, solved],
         total * size,
     )
-    pieces = gather(remainder, backward)
-    pack_u1 = pack_level(upper, lower_snode, -1, 0, 2, 0, 2 * total)
+    pieces, packed = gather(remainder, backward, lower_snode, pack_u1)
     (backward_solution,) = local_call(
         backward_lower_kernel,
         "backward_lower",
         [((rows, 1, size, width), f32)],
-        [*pieces, pack_u1, backward_upper],
+        [*pieces, packed, backward_upper],
         SPAN * size,
     )
     return forward_solution, backward_solution

time: 133 us -> 123 us (0.925)
  waiting for transfers between devices: 60.6 us -> 49.8 us
    ppermute x56, waiting for transfers between devices: 60.6 us -> 49.8 us  [move(): return lax.ppermute(value, 'prow', pairs)]
  transfers between devices with their start and end apart: 56 -> 56, of which waited for: 24 -> 37; matrix products, arithmetic and copies ran while one was open for 0% -> 0% of each run, Pallas kernels for 12% -> 13%
where the time goes in v2:
time: 123 us; the launch traced here: 122 us
  waiting for transfers between devices  49.8 us (40%)
  starting transfers between devices  48.6 us (40%)
  Pallas kernels  21 us (17%)
  local copies, waits for them, and re-layouts  1.74 us (1%)
    ppermute x56, waiting for transfers between devices, move(): return lax.ppermute(value, 'prow', pairs)  49.8 us
    ppermute x56, starting transfers between devices, move(): return lax.ppermute(value, 'prow', pairs)  48.6 us
    pallas_call x4, Pallas kernels, pack_level(): pl.pallas_call(functools.partial(pack_level_kernel, direction, base, rows...  7.68 us
    pallas_call x2, Pallas kernels, pack_coupling(): pl.pallas_call(kernel, out_shape=jax.ShapeDtypeStruct(shape, factor.dtype...  6.96 us
    pallas_call x8, Pallas kernels, local_call(): pl.pallas_call(kernel, out_shape=outs, in_specs=[pl.BlockSpec(memory_spac...  6.4 us
  transfers between devices with their start and end apart: 56, of which 37 were waited for; matrix products, arithmetic and copies ran while one was open for 0% of the time, Pallas kernels for 13%

profile of v2, /device:TPU:0, one launch (start us, length us, event | category | flops | bytes accessed | tf_op | source)
XLA Modules:
  0.0 122.1 jit_solution(17409688008631508475)
XLA Ops:
  1.7 4.1 %collective-permute-start.1 = (bf16[1,2,128,128]{3,2,1,0:T(8,128)(2,1)S(1)}, bf16[1,2,128,128]{3,2,1,0:T(8,128)(2,1)S(1)}, u32[]{:S(2)}, u32[]{:S(2)}) collective-permute-start(bf16[1,2,128,128]{3,2,1,0:T(8,128)(2,1)S(1)} %slice_bitcast_fusion), channel_id=1, source_target_pairs={{0,16},{1,17},{2,18},{3,19},{4,20},{5,21},{6,22},{7,23},{8,24},{9,... | collective-permute-start | bytes 196616 | tf_op jit(solution)/shard_map/ppermute | solution.py:146
  5.8 1.6 %collective-permute-start = (bf16[1,2,128,128]{3,2,1,0:T(8,128)(2,1)S(1)}, bf16[1,2,128,128]{3,2,1,0:T(8,128)(2,1)S(1)}, u32[]{:S(2)}, u32[]{:S(2)}) collective-permute-start(bf16[1,2,128,128]{3,2,1,0:T(8,128)(2,1)S(1)} %slice_bitcast_fusion), channel_id=1, source_target_pairs={{0,8},{1,9},{2,10},{3,11},{4,12},{5,13},{6,14},{7,15},{8,16},{9,17... | collective-permute-start | bytes 196616 | tf_op jit(solution)/shard_map/ppermute | solution.py:146
  8.0 2.1 %pack_level.4.refs_8_ = bf16[32,128,128]{2,1,0:T(8,128)(2,1)S(1)} custom-call(bf16[96,3,128,128]{3,2,1,0:T(8,128)(2,1)} %bitcast.30, s32[64]{0:T(128)S(1)} %copy-done.2), custom_call_target="tpu_custom_call" | custom-call | bytes 2097152 | tf_op jit(solution)/shard_map/pack_level/pallas_call | solution.py:66
  10.1 1.7 %collective-permute-done = bf16[1,2,128,128]{3,2,1,0:T(8,128)(2,1)S(1)} collective-permute-done((bf16[1,2,128,128]{3,2,1,0:T(8,128)(2,1)S(1)}, bf16[1,2,128,128]{3,2,1,0:T(8,128)(2,1)S(1)}, u32[]{:S(2)}, u32[]{:S(2)}) %collective-permute-start) | collective-permute-done | bytes 65568 | tf_op jit(solution)/shard_map/ppermute | solution.py:146
  11.9 2.5 %collective-permute-start.7 = (bf16[3,2,128,128]{3,2,1,0:T(8,128)(2,1)S(1)}, bf16[3,2,128,128]{3,2,1,0:T(8,128)(2,1)S(1)}, u32[]{:S(2)}, u32[]{:S(2)}) collective-permute-start(bf16[3,2,128,128]{3,2,1,0:T(8,128)(2,1)S(1)} %pad_maximum_fusion.1.refs_0_), channel_id=1, source_target_pairs={{0,6},{1,7},{2,4},{3,5},{4,2},{5,3},{6,0},{7,1},{8,14},{9,15},{10,... | collective-permute-start | bytes 589832 | tf_op jit(solution)/shard_map/ppermute | solution.py:146
  15.4 5.1 %collective-permute-done.7.refs_6_ = bf16[3,2,128,128]{3,2,1,0:T(8,128)(2,1)S(1)} collective-permute-done((bf16[3,2,128,128]{3,2,1,0:T(8,128)(2,1)S(1)}, bf16[3,2,128,128]{3,2,1,0:T(8,128)(2,1)S(1)}, u32[]{:S(2)}, u32[]{:S(2)}) %collective-permute-start.7) | collective-permute-done | bytes 196640 | tf_op jit(solution)/shard_map/ppermute | solution.py:146
  20.5 1.7 %collective-permute-done.5.refs_4_ = bf16[3,2,128,128]{3,2,1,0:T(8,128)(2,1)S(1)} collective-permute-done((bf16[3,2,128,128]{3,2,1,0:T(8,128)(2,1)S(1)}, bf16[3,2,128,128]{3,2,1,0:T(8,128)(2,1)S(1)}, u32[]{:S(2)}, u32[]{:S(2)}) %collective-permute-start.5) | collective-permute-done | bytes 196640 | tf_op jit(solution)/shard_map/ppermute | solution.py:146
  24.7 2.3 %collective-permute-start.11 = (bf16[1,2,128,128]{3,2,1,0:T(8,128)(2,1)S(1)}, bf16[1,2,128,128]{3,2,1,0:T(8,128)(2,1)S(1)}, u32[]{:S(2)}, u32[]{:S(2)}) collective-permute-start(bf16[1,2,128,128]{3,2,1,0:T(8,128)(2,1)S(1)} %bitcast.19), channel_id=1, source_target_pairs={{0,24},{1,25},{2,26},{3,27},{4,28},{5,29},{6,30},{7,31},{8,16},{9,... | collective-permute-start | bytes 196616 | tf_op jit(solution)/shard_map/ppermute | solution.py:146
  27.6 1.6 %collective-permute-start.9 = (bf16[1,2,128,128]{3,2,1,0:T(8,128)(2,1)S(1)}, bf16[1,2,128,128]{3,2,1,0:T(8,128)(2,1)S(1)}, u32[]{:S(2)}, u32[]{:S(2)}) collective-permute-start(bf16[1,2,128,128]{3,2,1,0:T(8,128)(2,1)S(1)} %bitcast.21), channel_id=1, source_target_pairs={{0,8},{1,9},{2,10},{3,11},{4,12},{5,13},{6,14},{7,15},{8,0},{9,1},... | collective-permute-start | bytes 196616 | tf_op jit(solution)/shard_map/ppermute | solution.py:146
  29.4 3.8 %pack_down.1.refs_8_ = bf16[64,128,128]{2,1,0:T(8,128)(2,1)S(1)} custom-call(bf16[96,3,128,128]{3,2,1,0:T(8,128)(2,1)} %bitcast.31, s32[64]{0:T(128)S(1)} %copy-done.3, s32[32]{0:T(128)S(1)} %copy-done.1, s32[5,1]{1,0:T(8,128)S(1)} %copy.9.parent, s32[32,5]{1,0:T(8,128)S(1)} %copy.10.pattern), custom_call_target="tpu_custom_call" | custom-call | bytes 4194304 | tf_op jit(solution)/shard_map/pack_down/pallas_call | solution.py:129
  34.3 1.8 %collective-permute-start.17 = (bf16[4,2,128,128]{3,2,1,0:T(8,128)(2,1)S(1)}, bf16[4,2,128,128]{3,2,1,0:T(8,128)(2,1)S(1)}, u32[]{:S(2)}, u32[]{:S(2)}) collective-permute-start(bf16[4,2,128,128]{3,2,1,0:T(8,128)(2,1)S(1)} %pad_maximum_fusion.refs_0_), channel_id=1, source_target_pairs={{0,6},{1,7},{2,4},{3,5},{4,2},{5,3},{6,0},{7,1},{8,14},{9,15},{10,... | collective-permute-start | bytes 786440 | tf_op jit(solution)/shard_map/ppermute | solution.py:146
  37.8 6.7 %collective-permute-done.17.refs_6_ = bf16[4,2,128,128]{3,2,1,0:T(8,128)(2,1)S(1)} collective-permute-done((bf16[4,2,128,128]{3,2,1,0:T(8,128)(2,1)S(1)}, bf16[4,2,128,128]{3,2,1,0:T(8,128)(2,1)S(1)}, u32[]{:S(2)}, u32[]{:S(2)}) %collective-permute-start.17) | collective-permute-done | bytes 262176 | tf_op jit(solution)/shard_map/ppermute | solution.py:146
  44.5 4.3 %collective-permute-done.15.refs_4_ = bf16[4,2,128,128]{3,2,1,0:T(8,128)(2,1)S(1)} collective-permute-done((bf16[4,2,128,128]{3,2,1,0:T(8,128)(2,1)S(1)}, bf16[4,2,128,128]{3,2,1,0:T(8,128)(2,1)S(1)}, u32[]{:S(2)}, u32[]{:S(2)}) %collective-permute-start.15) | collective-permute-done | bytes 262176 | tf_op jit(solution)/shard_map/ppermute | solution.py:146
  52.5 2.7 %collective-permute-start.19 = (bf16[1,1,128,128]{3,2,1,0:T(8,128)(2,1)S(1)}, bf16[1,1,128,128]{3,2,1,0:T(8,128)(2,1)S(1)}, u32[]{:S(2)}, u32[]{:S(2)}) collective-permute-start(bf16[1,1,128,128]{3,2,1,0:T(8,128)(2,1)S(1)} %bitcast.17), channel_id=1, source_target_pairs={{0,8},{1,9},{2,10},{3,11},{4,12},{5,13},{6,14},{7,15},{8,16},{9,17... | collective-permute-start | bytes 98312 | tf_op jit(solution)/shard_map/ppermute | solution.py:146
  55.2 1.8 %pack_level.5.refs_8_ = bf16[16,128,128]{2,1,0:T(8,128)(2,1)S(1)} custom-call(bf16[96,3,128,128]{3,2,1,0:T(8,128)(2,1)} %bitcast.32, s32[32]{0:T(128)S(1)} %copy-done.1), custom_call_target="tpu_custom_call" | custom-call | bytes 1048576 | tf_op jit(solution)/shard_map/pack_level/pallas_call | solution.py:66
  58.2 1.8 %collective-permute-start.26 = (bf16[3,1,128,128]{3,2,1,0:T(8,128)(2,1)S(1)}, bf16[3,1,128,128]{3,2,1,0:T(8,128)(2,1)S(1)}, u32[]{:S(2)}, u32[]{:S(2)}) collective-permute-start(bf16[3,1,128,128]{3,2,1,0:T(8,128)(2,1)S(1)} %pad_maximum_fusion.4.refs_0_), channel_id=1, source_target_pairs={{0,6},{1,7},{2,4},{3,5},{4,2},{5,3},{6,0},{7,1},{8,14},{9,15},{10,... | collective-permute-start | bytes 294920 | tf_op jit(solution)/shard_map/ppermute | solution.py:146
  61.8 3.1 %collective-permute-done.26.refs_6_ = bf16[3,1,128,128]{3,2,1,0:T(8,128)(2,1)S(1)} collective-permute-done((bf16[3,1,128,128]{3,2,1,0:T(8,128)(2,1)S(1)}, bf16[3,1,128,128]{3,2,1,0:T(8,128)(2,1)S(1)}, u32[]{:S(2)}, u32[]{:S(2)}) %collective-permute-start.26) | collective-permute-done | bytes 98336 | tf_op jit(solution)/shard_map/ppermute | solution.py:146
  68.4 2.6 %collective-permute-start.28 = (bf16[1,1,128,128]{3,2,1,0:T(8,128)(2,1)S(1)}, bf16[1,1,128,128]{3,2,1,0:T(8,128)(2,1)S(1)}, u32[]{:S(2)}, u32[]{:S(2)}) collective-permute-start(bf16[1,1,128,128]{3,2,1,0:T(8,128)(2,1)S(1)} %bitcast.24), channel_id=1, source_target_pairs={{0,24},{1,25},{2,26},{3,27},{4,28},{5,29},{6,30},{7,31},{8,0},{9,1... | collective-permute-start | bytes 98312 | tf_op jit(solution)/shard_map/ppermute | solution.py:146
  71.0 1.8 %pack_level.6.refs_8_ = bf16[16,128,128]{2,1,0:T(8,128)(2,1)S(1)} custom-call(bf16[96,3,128,128]{3,2,1,0:T(8,128)(2,1)} %bitcast.33, s32[32]{0:T(128)S(1)} %copy-done.1), custom_call_target="tpu_custom_call" | custom-call | bytes 1048576 | tf_op jit(solution)/shard_map/pack_level/pallas_call | solution.py:66
  73.0 1.6 %collective-permute-start.35 = (bf16[3,1,128,128]{3,2,1,0:T(8,128)(2,1)S(1)}, bf16[3,1,128,128]{3,2,1,0:T(8,128)(2,1)S(1)}, u32[]{:S(2)}, u32[]{:S(2)}) collective-permute-start(bf16[3,1,128,128]{3,2,1,0:T(8,128)(2,1)S(1)} %pad_maximum_fusion.5.refs_0_), channel_id=1, source_target_pairs={{0,6},{1,7},{2,4},{3,5},{4,2},{5,3},{6,0},{7,1},{8,14},{9,15},{10,... | collective-permute-start | bytes 294920 | tf_op jit(solution)/shard_map/ppermute | solution.py:146
  76.5 3.0 %collective-permute-done.35.refs_6_ = bf16[3,1,128,128]{3,2,1,0:T(8,128)(2,1)S(1)} collective-permute-done((bf16[3,1,128,128]{3,2,1,0:T(8,128)(2,1)S(1)}, bf16[3,1,128,128]{3,2,1,0:T(8,128)(2,1)S(1)}, u32[]{:S(2)}, u32[]{:S(2)}) %collective-permute-start.35) | collective-permute-done | bytes 98336 | tf_op jit(solution)/shard_map/ppermute | solution.py:146
  82.2 3.5 %collective-permute-start.39 = (bf16[1,1,128,128]{3,2,1,0:T(8,128)(2,1)S(1)}, bf16[1,1,128,128]{3,2,1,0:T(8,128)(2,1)S(1)}, u32[]{:S(2)}, u32[]{:S(2)}) collective-permute-start(bf16[1,1,128,128]{3,2,1,0:T(8,128)(2,1)S(1)} %bitcast.26), channel_id=1, source_target_pairs={{0,24},{1,25},{2,26},{3,27},{4,28},{5,29},{6,30},{7,31},{8,16},{9,... | collective-permute-start | bytes 98312 | tf_op jit(solution)/shard_map/ppermute | solution.py:146
  86.6 3.2 %pack_up.1.refs_8_ = bf16[2,32,128,128]{3,2,1,0:T(8,128)(2,1)S(1)} custom-call(bf16[96,3,128,128]{3,2,1,0:T(8,128)(2,1)} %bitcast.34, s32[64]{0:T(128)S(1)} %copy-done.3, s32[32]{0:T(128)S(1)} %copy-done.1, s32[5,1]{1,0:T(8,128)S(1)} %copy.9.parent, s32[32,5]{1,0:T(8,128)S(1)} %copy.10.pattern), custom_call_target="tpu_custom_call" | custom-call | bytes 4194304 | tf_op jit(solution)/shard_map/pack_up/pallas_call | solution.py:129
  90.4 1.5 %collective-permute-start.45 = (bf16[4,1,128,128]{3,2,1,0:T(8,128)(2,1)S(1)}, bf16[4,1,128,128]{3,2,1,0:T(8,128)(2,1)S(1)}, u32[]{:S(2)}, u32[]{:S(2)}) collective-permute-start(bf16[4,1,128,128]{3,2,1,0:T(8,128)(2,1)S(1)} %pad_maximum_fusion.3.refs_0_), channel_id=1, source_target_pairs={{0,6},{1,7},{2,4},{3,5},{4,2},{5,3},{6,0},{7,1},{8,14},{9,15},{10,... | collective-permute-start | bytes 393224 | tf_op jit(solution)/shard_map/ppermute | solution.py:146
  94.0 3.3 %collective-permute-done.45.refs_6_ = bf16[4,1,128,128]{3,2,1,0:T(8,128)(2,1)S(1)} collective-permute-done((bf16[4,1,128,128]{3,2,1,0:T(8,128)(2,1)S(1)}, bf16[4,1,128,128]{3,2,1,0:T(8,128)(2,1)S(1)}, u32[]{:S(2)}, u32[]{:S(2)}) %collective-permute-start.45) | collective-permute-done | bytes 131104 | tf_op jit(solution)/shard_map/ppermute | solution.py:146
  101.1 2.3 %collective-permute-start.48 = (bf16[1,2,128,128]{3,2,1,0:T(8,128)(2,1)S(1)}, bf16[1,2,128,128]{3,2,1,0:T(8,128)(2,1)S(1)}, u32[]{:S(2)}, u32[]{:S(2)}) collective-permute-start(bf16[1,2,128,128]{3,2,1,0:T(8,128)(2,1)S(1)} %bitcast.13), channel_id=1, source_target_pairs={{0,16},{1,17},{2,18},{3,19},{4,20},{5,21},{6,22},{7,23},{8,24},{9,... | collective-permute-start | bytes 196616 | tf_op jit(solution)/shard_map/ppermute | solution.py:146
  103.4 1.5 %collective-permute-start.47 = (bf16[1,2,128,128]{3,2,1,0:T(8,128)(2,1)S(1)}, bf16[1,2,128,128]{3,2,1,0:T(8,128)(2,1)S(1)}, u32[]{:S(2)}, u32[]{:S(2)}) collective-permute-start(bf16[1,2,128,128]{3,2,1,0:T(8,128)(2,1)S(1)} %bitcast.14), channel_id=1, source_target_pairs={{0,24},{1,25},{2,26},{3,27},{4,28},{5,29},{6,30},{7,31},{8,0},{9,1... | collective-permute-start | bytes 196616 | tf_op jit(solution)/shard_map/ppermute | solution.py:146
  104.8 1.9 %pack_level.7.refs_8_ = bf16[32,128,128]{2,1,0:T(8,128)(2,1)S(1)} custom-call(bf16[96,3,128,128]{3,2,1,0:T(8,128)(2,1)} %bitcast.35, s32[64]{0:T(128)S(1)} %copy-done.3), custom_call_target="tpu_custom_call" | custom-call | bytes 2097152 | tf_op jit(solution)/shard_map/pack_level/pallas_call | solution.py:66
  108.1 1.6 %collective-permute-start.54 = (bf16[3,2,128,128]{3,2,1,0:T(8,128)(2,1)S(1)}, bf16[3,2,128,128]{3,2,1,0:T(8,128)(2,1)S(1)}, u32[]{:S(2)}, u32[]{:S(2)}) collective-permute-start(bf16[3,2,128,128]{3,2,1,0:T(8,128)(2,1)S(1)} %pad_maximum_fusion.2.refs_0_), channel_id=1, source_target_pairs={{0,6},{1,7},{2,4},{3,5},{4,2},{5,3},{6,0},{7,1},{8,14},{9,15},{10,... | collective-permute-start | bytes 589832 | tf_op jit(solution)/shard_map/ppermute | solution.py:146
  111.7 5.1 %collective-permute-done.54.refs_6_ = bf16[3,2,128,128]{3,2,1,0:T(8,128)(2,1)S(1)} collective-permute-done((bf16[3,2,128,128]{3,2,1,0:T(8,128)(2,1)S(1)}, bf16[3,2,128,128]{3,2,1,0:T(8,128)(2,1)S(1)}, u32[]{:S(2)}, u32[]{:S(2)}) %collective-permute-start.54) | collective-permute-done | bytes 196640 | tf_op jit(solution)/shard_map/ppermute | solution.py:146
  116.8 2.0 %collective-permute-done.52.refs_4_ = bf16[3,2,128,128]{3,2,1,0:T(8,128)(2,1)S(1)} collective-permute-done((bf16[3,2,128,128]{3,2,1,0:T(8,128)(2,1)S(1)}, bf16[3,2,128,128]{3,2,1,0:T(8,128)(2,1)S(1)}, u32[]{:S(2)}, u32[]{:S(2)}) %collective-permute-start.52) | collective-permute-done | bytes 196640 | tf_op jit(solution)/shard_map/ppermute | solution.py:146
  120.6 1.6 %backward_lower.1 = f32[3,1,128,128]{3,2,1,0:T(8,128)} custom-call(bf16[3,2,128,128]{3,2,1,0:T(8,128)(2,1)S(1)} %pad_maximum_fusion.2.refs_0_, bf16[3,2,128,128]{3,2,1,0:T(8,128)(2,1)S(1)} %collective-permute-done.49.refs_1_, bf16[3,2,128,128]{3,2,1,0:T(8,128)(2,1)S(1)} %collective-permute-done.50.refs_2_, ...), custom_call_target="tpu_custom_call" | custom-call | bytes 1048576 | tf_op jit(solution)/shard_map/backward_lower/pallas_call | solution.py:269
  (115 shorter events, 36.2 us)
Async XLA Ops:
  1.7 8.5 %collective-permute-start.1 = (bf16[1,2,128,128]{3,2,1,0:T(8,128)(2,1)S(1)}, bf16[1,2,128,128]{3,2,1,0:T(8,128)(2,1)S(1)}, u32[]{:S(2)}, u32[]{:S(2)}) collective-permute-start(bf16[1,2,128,128]{3,2,1,0:T(8,128)(2,1)S(1)} %slice_bitcast_fusion), channel_id=1, source_target_pairs={{0,16},{1,17},{2,18},{3,19},{4,20},{5,21},{6,22},{7,23},{8,24},{9,... | collective-permute-start | bytes 196616 | tf_op jit(solution)/shard_map/ppermute | solution.py:146
  5.8 6.1 %collective-permute-start = (bf16[1,2,128,128]{3,2,1,0:T(8,128)(2,1)S(1)}, bf16[1,2,128,128]{3,2,1,0:T(8,128)(2,1)S(1)}, u32[]{:S(2)}, u32[]{:S(2)}) collective-permute-start(bf16[1,2,128,128]{3,2,1,0:T(8,128)(2,1)S(1)} %slice_bitcast_fusion), channel_id=1, source_target_pairs={{0,8},{1,9},{2,10},{3,11},{4,12},{5,13},{6,14},{7,15},{8,16},{9,17... | collective-permute-start | bytes 196616 | tf_op jit(solution)/shard_map/ppermute | solution.py:146
  11.9 8.6 %collective-permute-start.7 = (bf16[3,2,128,128]{3,2,1,0:T(8,128)(2,1)S(1)}, bf16[3,2,128,128]{3,2,1,0:T(8,128)(2,1)S(1)}, u32[]{:S(2)}, u32[]{:S(2)}) collective-permute-start(bf16[3,2,128,128]{3,2,1,0:T(8,128)(2,1)S(1)} %pad_maximum_fusion.1.refs_0_), channel_id=1, source_target_pairs={{0,6},{1,7},{2,4},{3,5},{4,2},{5,3},{6,0},{7,1},{8,14},{9,15},{10,... | collective-permute-start | bytes 589832 | tf_op jit(solution)/shard_map/ppermute | solution.py:146
  14.4 7.9 %collective-permute-start.5 = (bf16[3,2,128,128]{3,2,1,0:T(8,128)(2,1)S(1)}, bf16[3,2,128,128]{3,2,1,0:T(8,128)(2,1)S(1)}, u32[]{:S(2)}, u32[]{:S(2)}) collective-permute-start(bf16[3,2,128,128]{3,2,1,0:T(8,128)(2,1)S(1)} %pad_maximum_fusion.1.refs_0_), channel_id=1, source_target_pairs={{0,4},{1,5},{2,6},{3,7},{4,0},{5,1},{6,2},{7,3},{8,12},{9,13},{10,... | collective-permute-start | bytes 589832 | tf_op jit(solution)/shard_map/ppermute | solution.py:146
  14.9 7.5 %collective-permute-start.3 = (bf16[3,2,128,128]{3,2,1,0:T(8,128)(2,1)S(1)}, bf16[3,2,128,128]{3,2,1,0:T(8,128)(2,1)S(1)}, u32[]{:S(2)}, u32[]{:S(2)}) collective-permute-start(bf16[3,2,128,128]{3,2,1,0:T(8,128)(2,1)S(1)} %pad_maximum_fusion.1.refs_0_), channel_id=1, source_target_pairs={{0,2},{1,3},{2,0},{3,1},{4,6},{5,7},{6,4},{7,5},{8,10},{9,11},{10,... | collective-permute-start | bytes 589832 | tf_op jit(solution)/shard_map/ppermute | solution.py:146
  15.4 7.4 %collective-permute-start.2 = (bf16[3,2,128,128]{3,2,1,0:T(8,128)(2,1)S(1)}, bf16[3,2,128,128]{3,2,1,0:T(8,128)(2,1)S(1)}, u32[]{:S(2)}, u32[]{:S(2)}) collective-permute-start(bf16[3,2,128,128]{3,2,1,0:T(8,128)(2,1)S(1)} %pad_maximum_fusion.1.refs_0_), channel_id=1, source_target_pairs={{0,1},{1,0},{2,3},{3,2},{4,5},{5,4},{6,7},{7,6},{8,9},{9,8},{10,11... | collective-permute-start | bytes 589832 | tf_op jit(solution)/shard_map/ppermute | solution.py:146
  24.7 8.4 %collective-permute-start.11 = (bf16[1,2,128,128]{3,2,1,0:T(8,128)(2,1)S(1)}, bf16[1,2,128,128]{3,2,1,0:T(8,128)(2,1)S(1)}, u32[]{:S(2)}, u32[]{:S(2)}) collective-permute-start(bf16[1,2,128,128]{3,2,1,0:T(8,128)(2,1)S(1)} %bitcast.19), channel_id=1, source_target_pairs={{0,24},{1,25},{2,26},{3,27},{4,28},{5,29},{6,30},{7,31},{8,16},{9,... | collective-permute-start | bytes 196616 | tf_op jit(solution)/shard_map/ppermute | solution.py:146
  27.0 7.2 %collective-permute-start.10 = (bf16[1,2,128,128]{3,2,1,0:T(8,128)(2,1)S(1)}, bf16[1,2,128,128]{3,2,1,0:T(8,128)(2,1)S(1)}, u32[]{:S(2)}, u32[]{:S(2)}) collective-permute-start(bf16[1,2,128,128]{3,2,1,0:T(8,128)(2,1)S(1)} %bitcast.20), channel_id=1, source_target_pairs={{0,16},{1,17},{2,18},{3,19},{4,20},{5,21},{6,22},{7,23},{8,24},{9,... | collective-permute-start | bytes 196616 | tf_op jit(solution)/shard_map/ppermute | solution.py:146
  27.6 6.6 %collective-permute-start.9 = (bf16[1,2,128,128]{3,2,1,0:T(8,128)(2,1)S(1)}, bf16[1,2,128,128]{3,2,1,0:T(8,128)(2,1)S(1)}, u32[]{:S(2)}, u32[]{:S(2)}) collective-permute-start(bf16[1,2,128,128]{3,2,1,0:T(8,128)(2,1)S(1)} %bitcast.21), channel_id=1, source_target_pairs={{0,8},{1,9},{2,10},{3,11},{4,12},{5,13},{6,14},{7,15},{8,0},{9,1},... | collective-permute-start | bytes 196616 | tf_op jit(solution)/shard_map/ppermute | solution.py:146
  34.3 10.2 %collective-permute-start.17 = (bf16[4,2,128,128]{3,2,1,0:T(8,128)(2,1)S(1)}, bf16[4,2,128,128]{3,2,1,0:T(8,128)(2,1)S(1)}, u32[]{:S(2)}, u32[]{:S(2)}) collective-permute-start(bf16[4,2,128,128]{3,2,1,0:T(8,128)(2,1)S(1)} %pad_maximum_fusion.refs_0_), channel_id=1, source_target_pairs={{0,6},{1,7},{2,4},{3,5},{4,2},{5,3},{6,0},{7,1},{8,14},{9,15},{10,... | collective-permute-start | bytes 786440 | tf_op jit(solution)/shard_map/ppermute | solution.py:146
  36.1 12.7 %collective-permute-start.15 = (bf16[4,2,128,128]{3,2,1,0:T(8,128)(2,1)S(1)}, bf16[4,2,128,128]{3,2,1,0:T(8,128)(2,1)S(1)}, u32[]{:S(2)}, u32[]{:S(2)}) collective-permute-start(bf16[4,2,128,128]{3,2,1,0:T(8,128)(2,1)S(1)} %pad_maximum_fusion.refs_0_), channel_id=1, source_target_pairs={{0,4},{1,5},{2,6},{3,7},{4,0},{5,1},{6,2},{7,3},{8,12},{9,13},{10,... | collective-permute-start | bytes 786440 | tf_op jit(solution)/shard_map/ppermute | solution.py:146
  37.3 11.6 %collective-permute-start.13 = (bf16[4,2,128,128]{3,2,1,0:T(8,128)(2,1)S(1)}, bf16[4,2,128,128]{3,2,1,0:T(8,128)(2,1)S(1)}, u32[]{:S(2)}, u32[]{:S(2)}) collective-permute-start(bf16[4,2,128,128]{3,2,1,0:T(8,128)(2,1)S(1)} %pad_maximum_fusion.refs_0_), channel_id=1, source_target_pairs={{0,2},{1,3},{2,0},{3,1},{4,6},{5,7},{6,4},{7,5},{8,10},{9,11},{10,... | collective-permute-start | bytes 786440 | tf_op jit(solution)/shard_map/ppermute | solution.py:146
  37.8 11.5 %collective-permute-start.12 = (bf16[4,2,128,128]{3,2,1,0:T(8,128)(2,1)S(1)}, bf16[4,2,128,128]{3,2,1,0:T(8,128)(2,1)S(1)}, u32[]{:S(2)}, u32[]{:S(2)}) collective-permute-start(bf16[4,2,128,128]{3,2,1,0:T(8,128)(2,1)S(1)} %pad_maximum_fusion.refs_0_), channel_id=1, source_target_pairs={{0,1},{1,0},{2,3},{3,2},{4,5},{5,4},{6,7},{7,6},{8,9},{9,8},{10,11... | collective-permute-start | bytes 786440 | tf_op jit(solution)/shard_map/ppermute | solution.py:146
  44.5 4.8 %collective-permute-start.18 = (bf16[4,2,128,128]{3,2,1,0:T(8,128)(2,1)S(1)}, bf16[4,2,128,128]{3,2,1,0:T(8,128)(2,1)S(1)}, u32[]{:S(2)}, u32[]{:S(2)}) collective-permute-start(bf16[4,2,128,128]{3,2,1,0:T(8,128)(2,1)S(1)} %collective-permute-done.17.refs_6_), channel_id=1, source_target_pairs={{0,1},{1,0},{2,3},{3,2},{4,5},{5,4},{6,7},{7,6},{8,9},{9,8},{10,11... | collective-permute-start | bytes 786440 | tf_op jit(solution)/shard_map/ppermute | solution.py:146
  52.0 5.4 %collective-permute-start.20 = (bf16[1,1,128,128]{3,2,1,0:T(8,128)(2,1)S(1)}, bf16[1,1,128,128]{3,2,1,0:T(8,128)(2,1)S(1)}, u32[]{:S(2)}, u32[]{:S(2)}) collective-permute-start(bf16[1,1,128,128]{3,2,1,0:T(8,128)(2,1)S(1)} %bitcast.16), channel_id=1, source_target_pairs={{0,16},{1,17},{2,18},{3,19},{4,20},{5,21},{6,22},{7,23},{8,24},{9,... | collective-permute-start | bytes 98312 | tf_op jit(solution)/shard_map/ppermute | solution.py:146
  52.5 5.7 %collective-permute-start.19 = (bf16[1,1,128,128]{3,2,1,0:T(8,128)(2,1)S(1)}, bf16[1,1,128,128]{3,2,1,0:T(8,128)(2,1)S(1)}, u32[]{:S(2)}, u32[]{:S(2)}) collective-permute-start(bf16[1,1,128,128]{3,2,1,0:T(8,128)(2,1)S(1)} %bitcast.17), channel_id=1, source_target_pairs={{0,8},{1,9},{2,10},{3,11},{4,12},{5,13},{6,14},{7,15},{8,16},{9,17... | collective-permute-start | bytes 98312 | tf_op jit(solution)/shard_map/ppermute | solution.py:146
  58.2 6.6 %collective-permute-start.26 = (bf16[3,1,128,128]{3,2,1,0:T(8,128)(2,1)S(1)}, bf16[3,1,128,128]{3,2,1,0:T(8,128)(2,1)S(1)}, u32[]{:S(2)}, u32[]{:S(2)}) collective-permute-start(bf16[3,1,128,128]{3,2,1,0:T(8,128)(2,1)S(1)} %pad_maximum_fusion.4.refs_0_), channel_id=1, source_target_pairs={{0,6},{1,7},{2,4},{3,5},{4,2},{5,3},{6,0},{7,1},{8,14},{9,15},{10,... | collective-permute-start | bytes 294920 | tf_op jit(solution)/shard_map/ppermute | solution.py:146
  60.0 5.2 %collective-permute-start.24 = (bf16[3,1,128,128]{3,2,1,0:T(8,128)(2,1)S(1)}, bf16[3,1,128,128]{3,2,1,0:T(8,128)(2,1)S(1)}, u32[]{:S(2)}, u32[]{:S(2)}) collective-permute-start(bf16[3,1,128,128]{3,2,1,0:T(8,128)(2,1)S(1)} %pad_maximum_fusion.4.refs_0_), channel_id=1, source_target_pairs={{0,4},{1,5},{2,6},{3,7},{4,0},{5,1},{6,2},{7,3},{8,12},{9,13},{10,... | collective-permute-start | bytes 294920 | tf_op jit(solution)/shard_map/ppermute | solution.py:146
  67.6 5.3 %collective-permute-start.29 = (bf16[1,1,128,128]{3,2,1,0:T(8,128)(2,1)S(1)}, bf16[1,1,128,128]{3,2,1,0:T(8,128)(2,1)S(1)}, u32[]{:S(2)}, u32[]{:S(2)}) collective-permute-start(bf16[1,1,128,128]{3,2,1,0:T(8,128)(2,1)S(1)} %bitcast.23), channel_id=1, source_target_pairs={{0,16},{1,17},{2,18},{3,19},{4,20},{5,21},{6,22},{7,23},{8,24},{9,... | collective-permute-start | bytes 98312 | tf_op jit(solution)/shard_map/ppermute | solution.py:146
  73.0 6.5 %collective-permute-start.35 = (bf16[3,1,128,128]{3,2,1,0:T(8,128)(2,1)S(1)}, bf16[3,1,128,128]{3,2,1,0:T(8,128)(2,1)S(1)}, u32[]{:S(2)}, u32[]{:S(2)}) collective-permute-start(bf16[3,1,128,128]{3,2,1,0:T(8,128)(2,1)S(1)} %pad_maximum_fusion.5.refs_0_), channel_id=1, source_target_pairs={{0,6},{1,7},{2,4},{3,5},{4,2},{5,3},{6,0},{7,1},{8,14},{9,15},{10,... | collective-permute-start | bytes 294920 | tf_op jit(solution)/shard_map/ppermute | solution.py:146
  74.6 5.6 %collective-permute-start.33 = (bf16[3,1,128,128]{3,2,1,0:T(8,128)(2,1)S(1)}, bf16[3,1,128,128]{3,2,1,0:T(8,128)(2,1)S(1)}, u32[]{:S(2)}, u32[]{:S(2)}) collective-permute-start(bf16[3,1,128,128]{3,2,1,0:T(8,128)(2,1)S(1)} %pad_maximum_fusion.5.refs_0_), channel_id=1, source_target_pairs={{0,4},{1,5},{2,6},{3,7},{4,0},{5,1},{6,2},{7,3},{8,12},{9,13},{10,... | collective-permute-start | bytes 294920 | tf_op jit(solution)/shard_map/ppermute | solution.py:146
  82.2 7.7 %collective-permute-start.39 = (bf16[1,1,128,128]{3,2,1,0:T(8,128)(2,1)S(1)}, bf16[1,1,128,128]{3,2,1,0:T(8,128)(2,1)S(1)}, u32[]{:S(2)}, u32[]{:S(2)}) collective-permute-start(bf16[1,1,128,128]{3,2,1,0:T(8,128)(2,1)S(1)} %bitcast.26), channel_id=1, source_target_pairs={{0,24},{1,25},{2,26},{3,27},{4,28},{5,29},{6,30},{7,31},{8,16},{9,... | collective-permute-start | bytes 98312 | tf_op jit(solution)/shard_map/ppermute | solution.py:146
  85.6 4.8 %collective-permute-start.38 = (bf16[1,1,128,128]{3,2,1,0:T(8,128)(2,1)S(1)}, bf16[1,1,128,128]{3,2,1,0:T(8,128)(2,1)S(1)}, u32[]{:S(2)}, u32[]{:S(2)}) collective-permute-start(bf16[1,1,128,128]{3,2,1,0:T(8,128)(2,1)S(1)} %bitcast.27), channel_id=1, source_target_pairs={{0,16},{1,17},{2,18},{3,19},{4,20},{5,21},{6,22},{7,23},{8,24},{9,... | collective-permute-start | bytes 98312 | tf_op jit(solution)/shard_map/ppermute | solution.py:146
  90.4 6.8 %collective-permute-start.45 = (bf16[4,1,128,128]{3,2,1,0:T(8,128)(2,1)S(1)}, bf16[4,1,128,128]{3,2,1,0:T(8,128)(2,1)S(1)}, u32[]{:S(2)}, u32[]{:S(2)}) collective-permute-start(bf16[4,1,128,128]{3,2,1,0:T(8,128)(2,1)S(1)} %pad_maximum_fusion.3.refs_0_), channel_id=1, source_target_pairs={{0,6},{1,7},{2,4},{3,5},{4,2},{5,3},{6,0},{7,1},{8,14},{9,15},{10,... | collective-permute-start | bytes 393224 | tf_op jit(solution)/shard_map/ppermute | solution.py:146
  92.0 6.6 %collective-permute-start.43 = (bf16[4,1,128,128]{3,2,1,0:T(8,128)(2,1)S(1)}, bf16[4,1,128,128]{3,2,1,0:T(8,128)(2,1)S(1)}, u32[]{:S(2)}, u32[]{:S(2)}) collective-permute-start(bf16[4,1,128,128]{3,2,1,0:T(8,128)(2,1)S(1)} %pad_maximum_fusion.3.refs_0_), channel_id=1, source_target_pairs={{0,4},{1,5},{2,6},{3,7},{4,0},{5,1},{6,2},{7,3},{8,12},{9,13},{10,... | collective-permute-start | bytes 393224 | tf_op jit(solution)/shard_map/ppermute | solution.py:146
  93.1 5.5 %collective-permute-start.41 = (bf16[4,1,128,128]{3,2,1,0:T(8,128)(2,1)S(1)}, bf16[4,1,128,128]{3,2,1,0:T(8,128)(2,1)S(1)}, u32[]{:S(2)}, u32[]{:S(2)}) collective-permute-start(bf16[4,1,128,128]{3,2,1,0:T(8,128)(2,1)S(1)} %pad_maximum_fusion.3.refs_0_), channel_id=1, source_target_pairs={{0,2},{1,3},{2,0},{3,1},{4,6},{5,7},{6,4},{7,5},{8,10},{9,11},{10,... | collective-permute-start | bytes 393224 | tf_op jit(solution)/shard_map/ppermute | solution.py:146
  94.0 5.1 %collective-permute-start.40 = (bf16[4,1,128,128]{3,2,1,0:T(8,128)(2,1)S(1)}, bf16[4,1,128,128]{3,2,1,0:T(8,128)(2,1)S(1)}, u32[]{:S(2)}, u32[]{:S(2)}) collective-permute-start(bf16[4,1,128,128]{3,2,1,0:T(8,128)(2,1)S(1)} %pad_maximum_fusion.3.refs_0_), channel_id=1, source_target_pairs={{0,1},{1,0},{2,3},{3,2},{4,5},{5,4},{6,7},{7,6},{8,9},{9,8},{10,11... | collective-permute-start | bytes 393224 | tf_op jit(solution)/shard_map/ppermute | solution.py:146
  101.1 7.0 %collective-permute-start.48 = (bf16[1,2,128,128]{3,2,1,0:T(8,128)(2,1)S(1)}, bf16[1,2,128,128]{3,2,1,0:T(8,128)(2,1)S(1)}, u32[]{:S(2)}, u32[]{:S(2)}) collective-permute-start(bf16[1,2,128,128]{3,2,1,0:T(8,128)(2,1)S(1)} %bitcast.13), channel_id=1, source_target_pairs={{0,16},{1,17},{2,18},{3,19},{4,20},{5,21},{6,22},{7,23},{8,24},{9,... | collective-permute-start | bytes 196616 | tf_op jit(solution)/shard_map/ppermute | solution.py:146
  108.1 8.7 %collective-permute-start.54 = (bf16[3,2,128,128]{3,2,1,0:T(8,128)(2,1)S(1)}, bf16[3,2,128,128]{3,2,1,0:T(8,128)(2,1)S(1)}, u32[]{:S(2)}, u32[]{:S(2)}) collective-permute-start(bf16[3,2,128,128]{3,2,1,0:T(8,128)(2,1)S(1)} %pad_maximum_fusion.2.refs_0_), channel_id=1, source_target_pairs={{0,6},{1,7},{2,4},{3,5},{4,2},{5,3},{6,0},{7,1},{8,14},{9,15},{10,... | collective-permute-start | bytes 589832 | tf_op jit(solution)/shard_map/ppermute | solution.py:146
  109.7 9.1 %collective-permute-start.52 = (bf16[3,2,128,128]{3,2,1,0:T(8,128)(2,1)S(1)}, bf16[3,2,128,128]{3,2,1,0:T(8,128)(2,1)S(1)}, u32[]{:S(2)}, u32[]{:S(2)}) collective-permute-start(bf16[3,2,128,128]{3,2,1,0:T(8,128)(2,1)S(1)} %pad_maximum_fusion.2.refs_0_), channel_id=1, source_target_pairs={{0,4},{1,5},{2,6},{3,7},{4,0},{5,1},{6,2},{7,3},{8,12},{9,13},{10,... | collective-permute-start | bytes 589832 | tf_op jit(solution)/shard_map/ppermute | solution.py:146
  110.7 8.1 %collective-permute-start.50 = (bf16[3,2,128,128]{3,2,1,0:T(8,128)(2,1)S(1)}, bf16[3,2,128,128]{3,2,1,0:T(8,128)(2,1)S(1)}, u32[]{:S(2)}, u32[]{:S(2)}) collective-permute-start(bf16[3,2,128,128]{3,2,1,0:T(8,128)(2,1)S(1)} %pad_maximum_fusion.2.refs_0_), channel_id=1, source_target_pairs={{0,2},{1,3},{2,0},{3,1},{4,6},{5,7},{6,4},{7,5},{8,10},{9,11},{10,... | collective-permute-start | bytes 589832 | tf_op jit(solution)/shard_map/ppermute | solution.py:146
  111.7 8.5 %collective-permute-start.49 = (bf16[3,2,128,128]{3,2,1,0:T(8,128)(2,1)S(1)}, bf16[3,2,128,128]{3,2,1,0:T(8,128)(2,1)S(1)}, u32[]{:S(2)}, u32[]{:S(2)}) collective-permute-start(bf16[3,2,128,128]{3,2,1,0:T(8,128)(2,1)S(1)} %pad_maximum_fusion.2.refs_0_), channel_id=1, source_target_pairs={{0,1},{1,0},{2,3},{3,2},{4,5},{5,4},{6,7},{7,6},{8,9},{9,8},{10,11... | collective-permute-start | bytes 589832 | tf_op jit(solution)/shard_map/ppermute | solution.py:146
  (30 other events, 172.0 us)

commit v3 on v0

--- a/solution.py
+++ b/solution.py
@@ -1,7 +1,359 @@
+import functools
+import math
 import jax
 import jax.numpy as jnp
 from jax import lax
+from jax.experimental import pallas as pl
+from jax.experimental.pallas import tpu as pltpu
 from jax.sharding import PartitionSpec as P
+
+SPAN = 16
+PLANE = 8
+PLANES = 4
+VMEM_BYTES = 48 * 1024 * 1024
+
+
+def window_start(block, direction, count):
+    if direction > 0:
+        return jnp.maximum(block - (SPAN - 1), 0)
+    return jnp.minimum(block, count - SPAN)
+
+
+def first_pair(start, parity):
+    return (start + 1 - parity) // 2
+
+
+def pack_level_kernel(direction, base, rows, row_first, count, factor, snode, mine, other, sems):
+    me = lax.axis_index("prow")
+    core = me & 1
+    half = SPAN // 2
+    copies = []
+    for row in range(rows):
+        block = row * PLANE * PLANES + me
+        start = window_start(block, direction, count)
+        for side, out in ((0, mine), (1, other)):
+            parity = core ^ side
+            pair = first_pair(start, parity)
+            copy = pltpu.make_async_copy(
+                factor.at[pl.ds(base // 2 + pair, half), parity, row_first + row],
+                out.at[pl.ds(row * half, half)],
+                sems.at[2 * row + side],
+            )
+            copy.start()
+            copies.append((copy, row, block, pair, parity, out))
+    for copy, row, block, pair, parity, out in copies:
+        copy.wait()
+        own = snode[block]
+        for step in range(half):
+            column = 2 * (pair + step) + parity
+            if direction > 0:
+                kept = (snode[column] == own) & (column <= block)
+            else:
+                kept = (snode[column] == own) & (column >= block)
+
+            @pl.when(jnp.logical_not(kept))
+            def _():
+                out[row * half + step] = jnp.zeros(out.shape[1:], out.dtype)
+
+        if out is mine:
+            size = out.shape[1]
+            col = lax.broadcasted_iota(jnp.int32, (size, size), 0)
+            line = lax.broadcasted_iota(jnp.int32, (size, size), 1)
+            tri = line >= col if direction > 0 else line <= col
+            at = row * half + block // 2 - pair
+            diagonal = out[at]
+            out[at] = jnp.where(tri, diagonal, jnp.zeros_like(diagonal))
+
+
+def pack_down_kernel(factor, lower_snode, upper_snode, parent, pattern, mine, other, sems):
+    me = lax.axis_index("prow")
+    core = me & 1
+    count = mine.shape[0]
+    copies = []
+    for side, out in ((0, mine), (1, other)):
+        copy = pltpu.make_async_copy(
+            factor.at[pl.ds(0, count), core ^ side, 2], out, sems.at[side]
+        )
+        copy.start()
+        copies.append(copy)
+    for side, out in ((0, mine), (1, other)):
+        copies[side].wait()
+
+        def clear(pair, carry):
+            child = lower_snode[2 * pair + (core ^ side)]
+            linked = (parent[child, 0] == upper_snode[me]) & (pattern[me, child] == 1)
+
+            @pl.when(jnp.logical_not(linked))
+            def _():
+                out[pair] = jnp.zeros(out.shape[1:], out.dtype)
+
+            return carry
+
+        lax.fori_loop(0, count, clear, 0)
+
+
+def pack_up_kernel(factor, lower_snode, upper_snode, parent, pattern, mine, other, sems):
+    me = lax.axis_index("prow")
+    core = me & 1
+    count = mine.shape[1]
+    copies = []
+    for side, out in ((0, mine), (1, other)):
+        for row in range(2):
+            copy = pltpu.make_async_copy(
+                factor.at[pl.ds(2 * count, count), core ^ side, row],
+                out.at[row],
+                sems.at[2 * side + row],
+            )
+            copy.start()
+            copies.append(copy)
+    for side, out in ((0, mine), (1, other)):
+        for row in range(2):
+            copies[2 * side + row].wait()
+            child = lower_snode[row * PLANE * PLANES + me]
+            above = parent[child, 0]
+
+            def clear(pair, carry):
+                block = 2 * pair + (core ^ side)
+                linked = (above == upper_snode[block]) & (pattern[block, child] == 1)
+
+                @pl.when(jnp.logical_not(linked))
+                def _():
+                    out[row, pair] = jnp.zeros(out.shape[2:], out.dtype)
+
+                return carry
+
+            lax.fori_loop(0, count, clear, 0)
+
+
+def pack_call(kernel, name, shape, copies, factor, *tables):
+    return pl.pallas_call(
+        kernel,
+        out_shape=[jax.ShapeDtypeStruct(shape, factor.dtype)] * 2,
+        in_specs=[pl.BlockSpec(memory_space=pl.ANY)]
+        + [pl.BlockSpec(memory_space=pltpu.SMEM)] * len(tables),
+        out_specs=[pl.BlockSpec(memory_space=pltpu.VMEM)] * 2,
+        scratch_shapes=[pltpu.SemaphoreType.DMA((copies,))],
+        compiler_params=pltpu.CompilerParams(vmem_limit_bytes=VMEM_BYTES),
+        cost_estimate=pl.CostEstimate(
+            flops=0, bytes_accessed=4 * factor.dtype.itemsize * math.prod(shape), transcendentals=0
+        ),
+        name=name,
+    )(factor, *tables)
+
+
+def swap(value, distance):
+    return lax.ppermute(
+        value, "prow", [(i, i ^ distance) for i in range(PLANE * PLANES)]
+    )
+
+
+def gather(block, direction, table, pack):
+    total = PLANE * PLANES
+    parts = [block[None]]
+    if direction == 0:
+        parts += [swap(block[None], PLANE * step) for step in range(1, PLANES)]
+    else:
+        for step in (1, 2):
+            pairs = [(i, (i + direction * step * PLANE) % total) for i in range(total)]
+            parts.append(lax.ppermute(block[None], "prow", pairs))
+    mine, other = pack(lax.optimization_barrier((table, block))[0])
+    parts, mine, other = lax.optimization_barrier((parts, mine, other))
+    pieces = [jnp.concatenate(parts, 0)]
+    me = lax.axis_index("prow")
+    for k in (2, 4, 6):
+        if direction == 0:
+            sent = pieces[0]
+        else:
+            near, far = jnp.concatenate(parts[:2], 0), jnp.concatenate(parts[1:], 0)
+            after = (me & (2 if k == 2 else 4)) != 0
+            sent = jnp.where(after if direction > 0 else jnp.logical_not(after), far, near)
+        pieces.append(swap(sent, k))
+    return pieces, mine, swap(other, 1)
+
+
+def copy_window(pieces, xs, block, start, direction):
+    me = lax.axis_index("prow")
+    offset, core = me & (PLANE - 1), me & 1
+    size = xs.shape[0]
+    lines = PLANE // 2
+    pair = first_pair(start, core)
+    for k, piece in zip((0, 2, 4, 6), pieces, strict=True):
+        other = offset ^ k
+        first = (other // 2 - pair) & (lines - 1)
+        if k == 0:
+            skipped = 0
+        elif direction > 0:
+            skipped = (other > offset).astype(jnp.int32)
+        else:
+            skipped = (other < offset).astype(jnp.int32)
+        for half in range(2):
+            slot = first + half * lines
+            source = 2 * (pair + slot) + core
+            apart = direction * (block // PLANE - source // PLANE) - skipped
+            apart = jnp.clip(apart, 0, piece.shape[0] - 1)
+            level = source // (PLANE * PLANES) if piece.shape[1] > 1 else 0
+            at = pl.multiple_of(slot * size, size)
+            xs[:, pl.ds(at, size)] = piece[apart, level]
+
+
+def copy_all(pieces, xs):
+    me = lax.axis_index("prow")
+    offset, plane = me & (PLANE - 1), me // PLANE
+    size = xs.shape[0]
+    for k, piece in zip((0, 2, 4, 6), pieces, strict=True):
+        for along in range(PLANES):
+            for row in range(piece.shape[1]):
+                pair = (row * PLANES + (plane ^ along)) * (PLANE // 2) + (offset ^ k) // 2
+                xs[:, pl.ds(pl.multiple_of(pair * size, size), size)] = piece[along, row]
+
+
+def dot(left, right):
+    return jnp.dot(left, right, preferred_element_type=jnp.float32)
+
+
+def window_kernel(direction, flip, *refs):
+    pieces, (factor, out, xs) = refs[:4], refs[4:]
+    me = lax.axis_index("prow") ^ flip
+    size = xs.shape[0]
+    rows, half = out.shape[0], SPAN // 2
+    for row in range(rows):
+        block = row * PLANE * PLANES + me
+        start = window_start(block, direction, rows * PLANE * PLANES)
+        copy_window(pieces, xs, block, start, direction)
+        out[row] = dot(xs[...], factor[row * half : (row + 1) * half].reshape(half * size, size))
+
+
+def down_kernel(*refs):
+    pieces, (factor, out, xs) = refs[:4], refs[4:]
+    copy_all(pieces, xs)
+    out[0] = dot(xs[...], factor[...].reshape(xs.shape[1], xs.shape[0]))
+
+
+def up_kernel(*refs):
+    pieces, (factor, out, xs) = refs[:4], refs[4:]
+    copy_all(pieces, xs)
+    for row in range(out.shape[0]):
+        out[row] = dot(xs[...], factor[row].reshape(xs.shape[1], xs.shape[0]))
+
+
+def backward_out_kernel(mine, brought, upper, out):
+    for row in range(2):
+        out[row, 0] = (mine[row] + brought[row]).T
+    out[2, 0] = upper[0].T
+
+
+def turn_kernel(value, out):
+    for row in range(3):
+        out[row] = value[row, 0].astype(jnp.float32).T.astype(out.dtype)
+
+
+def forward_out_kernel(lower, upper, out):
+    for row in range(2):
+        out[row, 0] = lower[row].T
+    out[2, 0] = upper[0].T
+
+
+def local_call(kernel, name, shape, dtype, operands, width=0):
+    scratch = [pltpu.VMEM((shape[-2], width), jnp.bfloat16)] if width else []
+    return pl.pallas_call(
+        kernel,
+        out_shape=jax.ShapeDtypeStruct(shape, dtype),
+        in_specs=[pl.BlockSpec(memory_space=pltpu.VMEM)] * len(operands),
+        out_specs=pl.BlockSpec(memory_space=pltpu.VMEM),
+        scratch_shapes=scratch,
+        compiler_params=pltpu.CompilerParams(vmem_limit_bytes=VMEM_BYTES),
+        cost_estimate=pl.CostEstimate(flops=0, bytes_accessed=1 << 20, transcendentals=0),
+        name=name,
+    )(*operands)
+
+
+def fast_device(rhs, lower_factor_t, upper_factor_t, lower_snode, upper_snode, parent, pattern):
+    rows, _, size, width = rhs.shape
+    total = PLANE * PLANES
+    half = SPAN // 2
+    f32, bf16 = jnp.float32, jnp.bfloat16
+
+    def blocks(factor):
+        return jnp.transpose(factor, (0, 1, 3, 4, 2, 5)).reshape(
+            rows * total // 2, 2, rows, size, size
+        )
+
+    lower, upper = blocks(lower_factor_t), blocks(upper_factor_t)
+    own = local_call(turn_kernel, "turn", (rows, width, size), bf16, [rhs])
+
+    def level(factor, direction, count):
+        first, base = (0, 0) if count == 2 else (2, 2 * total)
+        kernel = functools.partial(
+            pack_level_kernel, direction, base, count, first, count * total
+        )
+        return lambda table: pack_call(
+            kernel, "pack_level", (count * half, size, size), 2 * count, factor, table
+        )
+
+    def pack_down(table):
+        return pack_call(
+            pack_down_kernel, "pack_down", (total, size, size), 2, lower, table, upper_snode, parent, pattern
+        )
+
+    def pack_up(table):
+        return pack_call(
+            pack_up_kernel, "pack_up", (2, total // 2, size, size), 4, upper, table, upper_snode, parent, pattern
+        )
+
+    def halves(kernels, name, count, width_in, block, direction, table, pack):
+        pieces, mine, theirs = gather(block, direction, table, pack)
+        shape = (count, width, size)
+        sent = local_call(kernels[1], name + "_other", shape, f32, [*pieces, theirs], width_in)
+        brought = swap(sent, 1)
+        kept = local_call(kernels[0], name, shape, f32, [*pieces, mine], width_in)
+        return kept, brought
+
+    def window(name, count, block, direction, table, factor):
+        kernels = [functools.partial(window_kernel, direction, flip) for flip in (0, 1)]
+        return halves(
+            kernels, name, count, half * size, block, direction, table, level(factor, direction, count)
+        )
+
+    kept, brought = window("forward_lower", 2, own[:2], 1, lower_snode, lower)
+    forward_lower = kept + brought
+    known = forward_lower.astype(bf16)
+    kept, brought = halves(
+        [down_kernel] * 2, "coupling", 1, total * size, known, 0, lower_snode, pack_down
+    )
+    coupling = (kept + brought).astype(bf16).astype(f32)
+    difference = (own[2:].astype(f32) - coupling).astype(bf16)
+    kept, brought = window("forward_upper", 1, difference, 1, upper_snode, lower)
+    forward_upper = kept + brought
+    kept, brought = window("backward_upper", 1, forward_upper.astype(bf16), -1, upper_snode, upper)
+    backward_upper = kept + brought
+    forward_solution = local_call(
+        forward_out_kernel,
+        "forward_out",
+        (rows, 1, size, width),
+        f32,
+        [forward_lower, forward_upper],
+    )
+    kept, brought = halves(
+        [up_kernel] * 2,
+        "correction",
+        2,
+        total // 2 * size,
+        backward_upper.astype(bf16),
+        0,
+        lower_snode,
+        pack_up,
+    )
+    correction = (kept + brought).astype(bf16).astype(f32)
+    remainder = (known.astype(f32) - correction).astype(bf16)
+    kept, brought = window("backward_lower", 2, remainder, -1, lower_snode, upper)
+    backward_solution = local_call(
+        backward_out_kernel,
+        "backward_out",
+        (rows, 1, size, width),
+        f32,
+        [kept, brought, backward_upper],
+    )
+    return forward_solution, backward_solution
 
 
 def block_masks(lower_snode, upper_snode, parent, pattern):
@@ -134,8 +486,10 @@
         P("parts", None),
         P("parts", None),
     )
+    total = PLANE * PLANES
+    simple = mesh.shape["prow"] == total and mesh.shape["pcol"] == 1
     return jax.shard_map(
-        on_device,
+        fast_device if simple else on_device,
         mesh=mesh,
         in_specs=placed,
         out_specs=(P("parts", "prow", "pcol", None), P("parts", "prow", "pcol", None)),

time: 402 us -> 122 us (0.30)
  waiting for transfers between devices: 313 us -> 53.6 us
  starting transfers between devices: 0.43 us -> 43.4 us
  matrix products: 39.1 us -> 0 us
  Pallas kernels: 0 us -> 21.1 us
  other arithmetic: 21 us -> 0.17 us
  between operations: 14.3 us -> 1.08 us
  local copies, waits for them, and re-layouts: 13 us -> 2.08 us
    all_gather x6 -> x0, waiting for transfers between devices: 313 us -> none  [apply_factor(): pieces_in = lax.all_gather(vector, 'prow', axis=1, tiled=True)]
    ppermute x0 -> x44, waiting for transfers between devices: none -> 53.6 us  [the longest x36 42.5 us: swap(): lax.ppermute(value, 'prow', [(i, i ^ distance) for i in range(PLANE * PLA...]
    ppermute x0 -> x44, starting transfers between devices: none -> 43.4 us  [the longest x36 30.8 us: swap(): lax.ppermute(value, 'prow', [(i, i ^ distance) for i in range(PLANE * PLA...]
    dot_general x12 -> x0, matrix products: 39.1 us -> none  [the longest x6 22.2 us: apply_factor(): lax.dot_general(window, picked, (((0, 1, 2), (0, 1, 2)), ((), ())), prefe...]
    pallas_call x0 -> x21, Pallas kernels: none -> 21.1 us  [the longest x6 13.5 us: pack_call(): pl.pallas_call(kernel, out_shape=[jax.ShapeDtypeStruct(shape, factor.dtyp...]
    select_n x1 -> x4, other arithmetic: 14.9 us -> 0.09 us  [gather(): jnp.where(after if direction > 0 else jnp.logical_not(after), far, near)]
  transfers between devices with their start and end apart: 6 -> 44, of which waited for: 6 -> 30; matrix products, arithmetic and copies ran while one was open for 6% -> 0% of each run, Pallas kernels for 0% -> 14%
where the time goes in v3:
time: 122 us; the launch traced here: 121 us
  waiting for transfers between devices  53.6 us (44%)
  starting transfers between devices  43.4 us (36%)
  Pallas kernels  21.1 us (17%)
  local copies, waits for them, and re-layouts  2.08 us (2%)
    ppermute x36, waiting for transfers between devices, swap(): lax.ppermute(value, 'prow', [(i, i ^ distance) for i in range(PLANE * PLA...  42.5 us
    ppermute x36, starting transfers between devices, swap(): lax.ppermute(value, 'prow', [(i, i ^ distance) for i in range(PLANE * PLA...  30.8 us
    pallas_call x6, Pallas kernels, pack_call(): pl.pallas_call(kernel, out_shape=[jax.ShapeDtypeStruct(shape, factor.dtyp...  13.5 us
    ppermute x8, starting transfers between devices, gather(): parts.append(lax.ppermute(block[None], 'prow', pairs))  12.6 us
    ppermute x8, waiting for transfers between devices, gather(): parts.append(lax.ppermute(block[None], 'prow', pairs))  11 us
    pallas_call x15, Pallas kernels, local_call(): pl.pallas_call(kernel, out_shape=jax.ShapeDtypeStruct(shape, dtype), in_s...  7.58 us
  transfers between devices with their start and end apart: 44, of which 30 were waited for; matrix products, arithmetic and copies ran while one was open for 0% of the time, Pallas kernels for 14%

profile of v3, /device:TPU:0, one launch (start us, length us, event | category | flops | bytes accessed | tf_op | source)
XLA Modules:
  0.0 121.4 jit_solution(11909606825619203998)
XLA Ops:
  1.7 3.1 %collective-permute-start = (bf16[1,2,128,128]{3,2,1,0:T(8,128)(2,1)S(1)}, bf16[1,2,128,128]{3,2,1,0:T(8,128)(2,1)S(1)}, u32[]{:S(2)}, u32[]{:S(2)}) collective-permute-start(bf16[1,2,128,128]{3,2,1,0:T(8,128)(2,1)S(1)} %slice_bitcast_fusion), channel_id=1, source_target_pairs={{0,8},{1,9},{2,10},{3,11},{4,12},{5,13},{6,14},{7,15},{8,16},{9,17... | collective-permute-start | bytes 196616 | tf_op jit(solution)/shard_map/ppermute | solution.py:158
  4.7 2.6 %collective-permute-start.1 = (bf16[1,2,128,128]{3,2,1,0:T(8,128)(2,1)S(1)}, bf16[1,2,128,128]{3,2,1,0:T(8,128)(2,1)S(1)}, u32[]{:S(2)}, u32[]{:S(2)}) collective-permute-start(bf16[1,2,128,128]{3,2,1,0:T(8,128)(2,1)S(1)} %slice_bitcast_fusion), channel_id=1, source_target_pairs={{0,16},{1,17},{2,18},{3,19},{4,20},{5,21},{6,22},{7,23},{8,24},{9,... | collective-permute-start | bytes 196616 | tf_op jit(solution)/shard_map/ppermute | solution.py:158
  8.0 1.9 %pack_level.4 = (bf16[16,128,128]{2,1,0:T(8,128)(2,1)S(1)}, bf16[16,128,128]{2,1,0:T(8,128)(2,1)S(1)}) custom-call(bf16[48,2,3,128,128]{4,3,2,1,0:T(8,128)(2,1)} %bitcast.13, s32[64]{0:T(128)S(1)} %copy-done.2), custom_call_target="tpu_custom_call" | custom-call | bytes 2097152 | tf_op jit(solution)/shard_map/pack_level/pallas_call | solution.py:129
  9.9 1.8 %collective-permute-done.1 = bf16[1,2,128,128]{3,2,1,0:T(8,128)(2,1)S(1)} collective-permute-done((bf16[1,2,128,128]{3,2,1,0:T(8,128)(2,1)S(1)}, bf16[1,2,128,128]{3,2,1,0:T(8,128)(2,1)S(1)}, u32[]{:S(2)}, u32[]{:S(2)}) %collective-permute-start.1) | collective-permute-done | bytes 65568 | tf_op jit(solution)/shard_map/ppermute | solution.py:158
  11.9 1.6 %collective-permute-start.2 = (bf16[2,2,128,128]{3,2,1,0:T(8,128)(2,1)S(1)}, bf16[2,2,128,128]{3,2,1,0:T(8,128)(2,1)S(1)}, u32[]{:S(2)}, u32[]{:S(2)}) collective-permute-start(bf16[2,2,128,128]{3,2,1,0:T(8,128)(2,1)S(1)} %get-tuple-element.111), channel_id=1, source_target_pairs={{0,2},{1,3},{2,0},{3,1},{4,6},{5,7},{6,4},{7,5},{8,10},{9,11},{10,... | collective-permute-start | bytes 393224 | tf_op jit(solution)/shard_map/ppermute | solution.py:145
  15.4 2.8 %collective-permute-done.2.refs_1_ = bf16[2,2,128,128]{3,2,1,0:T(8,128)(2,1)S(1)} collective-permute-done((bf16[2,2,128,128]{3,2,1,0:T(8,128)(2,1)S(1)}, bf16[2,2,128,128]{3,2,1,0:T(8,128)(2,1)S(1)}, u32[]{:S(2)}, u32[]{:S(2)}) %collective-permute-start.2) | collective-permute-done | bytes 131104 | tf_op jit(solution)/shard_map/ppermute | solution.py:145
  18.2 3.6 %collective-permute-done.3.refs_2_ = bf16[2,2,128,128]{3,2,1,0:T(8,128)(2,1)S(1)} collective-permute-done((bf16[2,2,128,128]{3,2,1,0:T(8,128)(2,1)S(1)}, bf16[2,2,128,128]{3,2,1,0:T(8,128)(2,1)S(1)}, u32[]{:S(2)}, u32[]{:S(2)}) %collective-permute-start.3) | collective-permute-done | bytes 131104 | tf_op jit(solution)/shard_map/ppermute | solution.py:145
  23.9 2.6 %collective-permute-start.8 = (bf16[1,2,128,128]{3,2,1,0:T(8,128)(2,1)S(1)}, bf16[1,2,128,128]{3,2,1,0:T(8,128)(2,1)S(1)}, u32[]{:S(2)}, u32[]{:S(2)}) collective-permute-start(bf16[1,2,128,128]{3,2,1,0:T(8,128)(2,1)S(1)} %bitcast.20), channel_id=1, source_target_pairs={{0,16},{1,17},{2,18},{3,19},{4,20},{5,21},{6,22},{7,23},{8,24},{9,... | collective-permute-start | bytes 196616 | tf_op jit(solution)/shard_map/ppermute | solution.py:145
  26.5 1.8 %collective-permute-start.9 = (bf16[1,2,128,128]{3,2,1,0:T(8,128)(2,1)S(1)}, bf16[1,2,128,128]{3,2,1,0:T(8,128)(2,1)S(1)}, u32[]{:S(2)}, u32[]{:S(2)}) collective-permute-start(bf16[1,2,128,128]{3,2,1,0:T(8,128)(2,1)S(1)} %bitcast.21), channel_id=1, source_target_pairs={{0,24},{1,25},{2,26},{3,27},{4,28},{5,29},{6,30},{7,31},{8,16},{9,... | collective-permute-start | bytes 196616 | tf_op jit(solution)/shard_map/ppermute | solution.py:145
  28.5 3.4 %pack_down.1 = (bf16[32,128,128]{2,1,0:T(8,128)(2,1)S(1)}, bf16[32,128,128]{2,1,0:T(8,128)(2,1)S(1)}) custom-call(bf16[48,2,3,128,128]{4,3,2,1,0:T(8,128)(2,1)} %bitcast.14, s32[64]{0:T(128)S(1)} %copy-done.3, s32[32]{0:T(128)S(1)} %copy-done.1, s32[5,1]{1,0:T(8,128)S(1)} %copy.9.parent, s32[32,5]{1,0:T(8,128)S(1)} %copy.10.pattern), custom_call_target="tpu_custom_call" | custom-call | bytes 4194304 | tf_op jit(solution)/shard_map/pack_down/pallas_call | solution.py:129
  36.3 5.6 %collective-permute-done.10.refs_1_ = bf16[4,2,128,128]{3,2,1,0:T(8,128)(2,1)S(1)} collective-permute-done((bf16[4,2,128,128]{3,2,1,0:T(8,128)(2,1)S(1)}, bf16[4,2,128,128]{3,2,1,0:T(8,128)(2,1)S(1)}, u32[]{:S(2)}, u32[]{:S(2)}) %collective-permute-start.10) | collective-permute-done | bytes 262176 | tf_op jit(solution)/shard_map/ppermute | solution.py:145
  41.9 4.5 %collective-permute-done.11.refs_2_ = bf16[4,2,128,128]{3,2,1,0:T(8,128)(2,1)S(1)} collective-permute-done((bf16[4,2,128,128]{3,2,1,0:T(8,128)(2,1)S(1)}, bf16[4,2,128,128]{3,2,1,0:T(8,128)(2,1)S(1)}, u32[]{:S(2)}, u32[]{:S(2)}) %collective-permute-start.11) | collective-permute-done | bytes 262176 | tf_op jit(solution)/shard_map/ppermute | solution.py:145
  46.4 1.6 %collective-permute-done.12.refs_3_ = bf16[4,2,128,128]{3,2,1,0:T(8,128)(2,1)S(1)} collective-permute-done((bf16[4,2,128,128]{3,2,1,0:T(8,128)(2,1)S(1)}, bf16[4,2,128,128]{3,2,1,0:T(8,128)(2,1)S(1)}, u32[]{:S(2)}, u32[]{:S(2)}) %collective-permute-start.12) | collective-permute-done | bytes 262176 | tf_op jit(solution)/shard_map/ppermute | solution.py:145
  52.7 1.7 %pack_level.5 = (bf16[8,128,128]{2,1,0:T(8,128)(2,1)S(1)}, bf16[8,128,128]{2,1,0:T(8,128)(2,1)S(1)}) custom-call(bf16[48,2,3,128,128]{4,3,2,1,0:T(8,128)(2,1)} %bitcast.15, s32[32]{0:T(128)S(1)} %copy-done.1), custom_call_target="tpu_custom_call" | custom-call | bytes 1048576 | tf_op jit(solution)/shard_map/pack_level/pallas_call | solution.py:129
  54.3 1.6 %collective-permute-done.15 = bf16[1,1,128,128]{3,2,1,0:T(8,128)(2,1)S(1)} collective-permute-done((bf16[1,1,128,128]{3,2,1,0:T(8,128)(2,1)S(1)}, bf16[1,1,128,128]{3,2,1,0:T(8,128)(2,1)S(1)}, u32[]{:S(2)}, u32[]{:S(2)}) %collective-permute-start.15) | collective-permute-done | bytes 32800 | tf_op jit(solution)/shard_map/ppermute | solution.py:158
  62.0 2.4 %collective-permute-done.19.refs_3_ = bf16[2,1,128,128]{3,2,1,0:T(8,128)(2,1)S(1)} collective-permute-done((bf16[2,1,128,128]{3,2,1,0:T(8,128)(2,1)S(1)}, bf16[2,1,128,128]{3,2,1,0:T(8,128)(2,1)S(1)}, u32[]{:S(2)}, u32[]{:S(2)}) %collective-permute-start.19) | collective-permute-done | bytes 65568 | tf_op jit(solution)/shard_map/ppermute | solution.py:145
  66.1 2.0 %collective-permute-start.22 = (bf16[1,1,128,128]{3,2,1,0:T(8,128)(2,1)S(1)}, bf16[1,1,128,128]{3,2,1,0:T(8,128)(2,1)S(1)}, u32[]{:S(2)}, u32[]{:S(2)}) collective-permute-start(bf16[1,1,128,128]{3,2,1,0:T(8,128)(2,1)S(1)} %bitcast.26), channel_id=1, source_target_pairs={{0,24},{1,25},{2,26},{3,27},{4,28},{5,29},{6,30},{7,31},{8,0},{9,1... | collective-permute-start | bytes 98312 | tf_op jit(solution)/shard_map/ppermute | solution.py:158
  68.1 1.7 %pack_level.6 = (bf16[8,128,128]{2,1,0:T(8,128)(2,1)S(1)}, bf16[8,128,128]{2,1,0:T(8,128)(2,1)S(1)}) custom-call(bf16[48,2,3,128,128]{4,3,2,1,0:T(8,128)(2,1)} %bitcast.16, s32[32]{0:T(128)S(1)} %copy-done.1), custom_call_target="tpu_custom_call" | custom-call | bytes 1048576 | tf_op jit(solution)/shard_map/pack_level/pallas_call | solution.py:129
  70.1 2.9 %collective-permute-done.23 = bf16[1,1,128,128]{3,2,1,0:T(8,128)(2,1)S(1)} collective-permute-done((bf16[1,1,128,128]{3,2,1,0:T(8,128)(2,1)S(1)}, bf16[1,1,128,128]{3,2,1,0:T(8,128)(2,1)S(1)}, u32[]{:S(2)}, u32[]{:S(2)}) %collective-permute-start.23) | collective-permute-done | bytes 32800 | tf_op jit(solution)/shard_map/ppermute | solution.py:158
  74.8 1.8 %collective-permute-start.26 = (bf16[2,1,128,128]{3,2,1,0:T(8,128)(2,1)S(1)}, bf16[2,1,128,128]{3,2,1,0:T(8,128)(2,1)S(1)}, u32[]{:S(2)}, u32[]{:S(2)}) collective-permute-start(bf16[2,1,128,128]{3,2,1,0:T(8,128)(2,1)S(1)} %get-tuple-element.112), channel_id=1, source_target_pairs={{0,6},{1,7},{2,4},{3,5},{4,2},{5,3},{6,0},{7,1},{8,14},{9,15},{10,... | collective-permute-start | bytes 196616 | tf_op jit(solution)/shard_map/ppermute | solution.py:145
  77.9 2.1 %collective-permute-done.26.refs_3_ = bf16[2,1,128,128]{3,2,1,0:T(8,128)(2,1)S(1)} collective-permute-done((bf16[2,1,128,128]{3,2,1,0:T(8,128)(2,1)S(1)}, bf16[2,1,128,128]{3,2,1,0:T(8,128)(2,1)S(1)}, u32[]{:S(2)}, u32[]{:S(2)}) %collective-permute-start.26) | collective-permute-done | bytes 65568 | tf_op jit(solution)/shard_map/ppermute | solution.py:145
  81.8 2.0 %collective-permute-start.30 = (bf16[1,1,128,128]{3,2,1,0:T(8,128)(2,1)S(1)}, bf16[1,1,128,128]{3,2,1,0:T(8,128)(2,1)S(1)}, u32[]{:S(2)}, u32[]{:S(2)}) collective-permute-start(bf16[1,1,128,128]{3,2,1,0:T(8,128)(2,1)S(1)} %bitcast.30), channel_id=1, source_target_pairs={{0,16},{1,17},{2,18},{3,19},{4,20},{5,21},{6,22},{7,23},{8,24},{9,... | collective-permute-start | bytes 98312 | tf_op jit(solution)/shard_map/ppermute | solution.py:145
  83.8 2.3 %collective-permute-start.31 = (bf16[1,1,128,128]{3,2,1,0:T(8,128)(2,1)S(1)}, bf16[1,1,128,128]{3,2,1,0:T(8,128)(2,1)S(1)}, u32[]{:S(2)}, u32[]{:S(2)}) collective-permute-start(bf16[1,1,128,128]{3,2,1,0:T(8,128)(2,1)S(1)} %bitcast.31), channel_id=1, source_target_pairs={{0,24},{1,25},{2,26},{3,27},{4,28},{5,29},{6,30},{7,31},{8,16},{9,... | collective-permute-start | bytes 98312 | tf_op jit(solution)/shard_map/ppermute | solution.py:145
  86.1 3.1 %pack_up.1 = (bf16[2,16,128,128]{3,2,1,0:T(8,128)(2,1)S(1)}, bf16[2,16,128,128]{3,2,1,0:T(8,128)(2,1)S(1)}) custom-call(bf16[48,2,3,128,128]{4,3,2,1,0:T(8,128)(2,1)} %bitcast.17, s32[64]{0:T(128)S(1)} %copy-done.3, s32[32]{0:T(128)S(1)} %copy-done.1, s32[5,1]{1,0:T(8,128)S(1)} %copy.9.parent, s32[32,5]{1,0:T(8,128)S(1)} %copy.10.pattern), custom_call_target="tpu_custom_call" | custom-call | bytes 4194304 | tf_op jit(solution)/shard_map/pack_up/pallas_call | solution.py:129
  93.1 2.8 %collective-permute-done.32.refs_1_ = bf16[4,1,128,128]{3,2,1,0:T(8,128)(2,1)S(1)} collective-permute-done((bf16[4,1,128,128]{3,2,1,0:T(8,128)(2,1)S(1)}, bf16[4,1,128,128]{3,2,1,0:T(8,128)(2,1)S(1)}, u32[]{:S(2)}, u32[]{:S(2)}) %collective-permute-start.32) | collective-permute-done | bytes 131104 | tf_op jit(solution)/shard_map/ppermute | solution.py:145
  95.9 2.9 %collective-permute-done.33.refs_2_ = bf16[4,1,128,128]{3,2,1,0:T(8,128)(2,1)S(1)} collective-permute-done((bf16[4,1,128,128]{3,2,1,0:T(8,128)(2,1)S(1)}, bf16[4,1,128,128]{3,2,1,0:T(8,128)(2,1)S(1)}, u32[]{:S(2)}, u32[]{:S(2)}) %collective-permute-start.33) | collective-permute-done | bytes 131104 | tf_op jit(solution)/shard_map/ppermute | solution.py:145
  100.9 2.4 %collective-permute-start.37 = (bf16[1,2,128,128]{3,2,1,0:T(8,128)(2,1)S(1)}, bf16[1,2,128,128]{3,2,1,0:T(8,128)(2,1)S(1)}, u32[]{:S(2)}, u32[]{:S(2)}) collective-permute-start(bf16[1,2,128,128]{3,2,1,0:T(8,128)(2,1)S(1)} %bitcast.23), channel_id=1, source_target_pairs={{0,24},{1,25},{2,26},{3,27},{4,28},{5,29},{6,30},{7,31},{8,0},{9,1... | collective-permute-start | bytes 196616 | tf_op jit(solution)/shard_map/ppermute | solution.py:158
  103.3 1.8 %pack_level.7 = (bf16[16,128,128]{2,1,0:T(8,128)(2,1)S(1)}, bf16[16,128,128]{2,1,0:T(8,128)(2,1)S(1)}) custom-call(bf16[48,2,3,128,128]{4,3,2,1,0:T(8,128)(2,1)} %bitcast.18, s32[64]{0:T(128)S(1)} %copy-done.3), custom_call_target="tpu_custom_call" | custom-call | bytes 2097152 | tf_op jit(solution)/shard_map/pack_level/pallas_call | solution.py:129
  105.7 3.1 %collective-permute-done.38 = bf16[1,2,128,128]{3,2,1,0:T(8,128)(2,1)S(1)} collective-permute-done((bf16[1,2,128,128]{3,2,1,0:T(8,128)(2,1)S(1)}, bf16[1,2,128,128]{3,2,1,0:T(8,128)(2,1)S(1)}, u32[]{:S(2)}, u32[]{:S(2)}) %collective-permute-start.38) | collective-permute-done | bytes 65568 | tf_op jit(solution)/shard_map/ppermute | solution.py:158
  112.5 2.8 %collective-permute-done.39.refs_1_ = bf16[2,2,128,128]{3,2,1,0:T(8,128)(2,1)S(1)} collective-permute-done((bf16[2,2,128,128]{3,2,1,0:T(8,128)(2,1)S(1)}, bf16[2,2,128,128]{3,2,1,0:T(8,128)(2,1)S(1)}, u32[]{:S(2)}, u32[]{:S(2)}) %collective-permute-start.39) | collective-permute-done | bytes 131104 | tf_op jit(solution)/shard_map/ppermute | solution.py:145
  115.3 1.7 %collective-permute-done.40.refs_2_ = bf16[2,2,128,128]{3,2,1,0:T(8,128)(2,1)S(1)} collective-permute-done((bf16[2,2,128,128]{3,2,1,0:T(8,128)(2,1)S(1)}, bf16[2,2,128,128]{3,2,1,0:T(8,128)(2,1)S(1)}, u32[]{:S(2)}, u32[]{:S(2)}) %collective-permute-start.40) | collective-permute-done | bytes 131104 | tf_op jit(solution)/shard_map/ppermute | solution.py:145
  117.0 1.6 %collective-permute-done.41.refs_3_ = bf16[2,2,128,128]{3,2,1,0:T(8,128)(2,1)S(1)} collective-permute-done((bf16[2,2,128,128]{3,2,1,0:T(8,128)(2,1)S(1)}, bf16[2,2,128,128]{3,2,1,0:T(8,128)(2,1)S(1)}, u32[]{:S(2)}, u32[]{:S(2)}) %collective-permute-start.41) | collective-permute-done | bytes 131104 | tf_op jit(solution)/shard_map/ppermute | solution.py:145
  (121 shorter events, 40.7 us)
Async XLA Ops:
  1.7 8.2 %collective-permute-start = (bf16[1,2,128,128]{3,2,1,0:T(8,128)(2,1)S(1)}, bf16[1,2,128,128]{3,2,1,0:T(8,128)(2,1)S(1)}, u32[]{:S(2)}, u32[]{:S(2)}) collective-permute-start(bf16[1,2,128,128]{3,2,1,0:T(8,128)(2,1)S(1)} %slice_bitcast_fusion), channel_id=1, source_target_pairs={{0,8},{1,9},{2,10},{3,11},{4,12},{5,13},{6,14},{7,15},{8,16},{9,17... | collective-permute-start | bytes 196616 | tf_op jit(solution)/shard_map/ppermute | solution.py:158
  4.7 6.9 %collective-permute-start.1 = (bf16[1,2,128,128]{3,2,1,0:T(8,128)(2,1)S(1)}, bf16[1,2,128,128]{3,2,1,0:T(8,128)(2,1)S(1)}, u32[]{:S(2)}, u32[]{:S(2)}) collective-permute-start(bf16[1,2,128,128]{3,2,1,0:T(8,128)(2,1)S(1)} %slice_bitcast_fusion), channel_id=1, source_target_pairs={{0,16},{1,17},{2,18},{3,19},{4,20},{5,21},{6,22},{7,23},{8,24},{9,... | collective-permute-start | bytes 196616 | tf_op jit(solution)/shard_map/ppermute | solution.py:158
  11.7 10.2 %collective-permute-start.5 = (bf16[16,128,128]{2,1,0:T(8,128)(2,1)S(1)}, bf16[16,128,128]{2,1,0:T(8,128)(2,1)S(1)}, u32[]{:S(2)}, u32[]{:S(2)}) collective-permute-start(bf16[16,128,128]{2,1,0:T(8,128)(2,1)S(1)} %get-tuple-element.59), channel_id=1, source_target_pairs={{0,1},{1,0},{2,3},{3,2},{4,5},{5,4},{6,7},{7,6},{8,9},{9,8},{10,11... | collective-permute-start | bytes 1572872 | tf_op jit(solution)/shard_map/ppermute | solution.py:145
  11.9 6.4 %collective-permute-start.2 = (bf16[2,2,128,128]{3,2,1,0:T(8,128)(2,1)S(1)}, bf16[2,2,128,128]{3,2,1,0:T(8,128)(2,1)S(1)}, u32[]{:S(2)}, u32[]{:S(2)}) collective-permute-start(bf16[2,2,128,128]{3,2,1,0:T(8,128)(2,1)S(1)} %get-tuple-element.111), channel_id=1, source_target_pairs={{0,2},{1,3},{2,0},{3,1},{4,6},{5,7},{6,4},{7,5},{8,10},{9,11},{10,... | collective-permute-start | bytes 393224 | tf_op jit(solution)/shard_map/ppermute | solution.py:145
  13.4 8.4 %collective-permute-start.3 = (bf16[2,2,128,128]{3,2,1,0:T(8,128)(2,1)S(1)}, bf16[2,2,128,128]{3,2,1,0:T(8,128)(2,1)S(1)}, u32[]{:S(2)}, u32[]{:S(2)}) collective-permute-start(bf16[2,2,128,128]{3,2,1,0:T(8,128)(2,1)S(1)} %get-tuple-element.110), channel_id=1, source_target_pairs={{0,4},{1,5},{2,6},{3,7},{4,0},{5,1},{6,2},{7,3},{8,12},{9,13},{10,... | collective-permute-start | bytes 393224 | tf_op jit(solution)/shard_map/ppermute | solution.py:145
  15.0 6.9 %collective-permute-start.4 = (bf16[2,2,128,128]{3,2,1,0:T(8,128)(2,1)S(1)}, bf16[2,2,128,128]{3,2,1,0:T(8,128)(2,1)S(1)}, u32[]{:S(2)}, u32[]{:S(2)}) collective-permute-start(bf16[2,2,128,128]{3,2,1,0:T(8,128)(2,1)S(1)} %get-tuple-element.110), channel_id=1, source_target_pairs={{0,6},{1,7},{2,4},{3,5},{4,2},{5,3},{6,0},{7,1},{8,14},{9,15},{10,... | collective-permute-start | bytes 393224 | tf_op jit(solution)/shard_map/ppermute | solution.py:145
  23.8 8.1 %collective-permute-start.7 = (bf16[1,2,128,128]{3,2,1,0:T(8,128)(2,1)S(1)}, bf16[1,2,128,128]{3,2,1,0:T(8,128)(2,1)S(1)}, u32[]{:S(2)}, u32[]{:S(2)}) collective-permute-start(bf16[1,2,128,128]{3,2,1,0:T(8,128)(2,1)S(1)} %bitcast.19), channel_id=1, source_target_pairs={{0,8},{1,9},{2,10},{3,11},{4,12},{5,13},{6,14},{7,15},{8,0},{9,1},... | collective-permute-start | bytes 196616 | tf_op jit(solution)/shard_map/ppermute | solution.py:145
  23.9 8.0 %collective-permute-start.8 = (bf16[1,2,128,128]{3,2,1,0:T(8,128)(2,1)S(1)}, bf16[1,2,128,128]{3,2,1,0:T(8,128)(2,1)S(1)}, u32[]{:S(2)}, u32[]{:S(2)}) collective-permute-start(bf16[1,2,128,128]{3,2,1,0:T(8,128)(2,1)S(1)} %bitcast.20), channel_id=1, source_target_pairs={{0,16},{1,17},{2,18},{3,19},{4,20},{5,21},{6,22},{7,23},{8,24},{9,... | collective-permute-start | bytes 196616 | tf_op jit(solution)/shard_map/ppermute | solution.py:145
  26.5 6.2 %collective-permute-start.9 = (bf16[1,2,128,128]{3,2,1,0:T(8,128)(2,1)S(1)}, bf16[1,2,128,128]{3,2,1,0:T(8,128)(2,1)S(1)}, u32[]{:S(2)}, u32[]{:S(2)}) collective-permute-start(bf16[1,2,128,128]{3,2,1,0:T(8,128)(2,1)S(1)} %bitcast.21), channel_id=1, source_target_pairs={{0,24},{1,25},{2,26},{3,27},{4,28},{5,29},{6,30},{7,31},{8,16},{9,... | collective-permute-start | bytes 196616 | tf_op jit(solution)/shard_map/ppermute | solution.py:145
  32.6 15.4 %collective-permute-start.13 = (bf16[32,128,128]{2,1,0:T(8,128)(2,1)S(1)}, bf16[32,128,128]{2,1,0:T(8,128)(2,1)S(1)}, u32[]{:S(2)}, u32[]{:S(2)}) collective-permute-start(bf16[32,128,128]{2,1,0:T(8,128)(2,1)S(1)} %get-tuple-element.68), channel_id=1, source_target_pairs={{0,1},{1,0},{2,3},{3,2},{4,5},{5,4},{6,7},{7,6},{8,9},{9,8},{10,11... | collective-permute-start | bytes 3145736 | tf_op jit(solution)/shard_map/ppermute | solution.py:145
  32.7 9.2 %collective-permute-start.10 = (bf16[4,2,128,128]{3,2,1,0:T(8,128)(2,1)S(1)}, bf16[4,2,128,128]{3,2,1,0:T(8,128)(2,1)S(1)}, u32[]{:S(2)}, u32[]{:S(2)}) collective-permute-start(bf16[4,2,128,128]{3,2,1,0:T(8,128)(2,1)S(1)} %constant_dynamic-update-slice_fusion.7.refs_0_), channel_id=1, source_target_pairs={{0,2},{1,3},{2,0},{3,1},{4,6},{5,7},{6,4},{7,5},{8,10},{9,11},{10,... | collective-permute-start | bytes 786440 | tf_op jit(solution)/shard_map/ppermute | solution.py:145
  34.0 12.4 %collective-permute-start.11 = (bf16[4,2,128,128]{3,2,1,0:T(8,128)(2,1)S(1)}, bf16[4,2,128,128]{3,2,1,0:T(8,128)(2,1)S(1)}, u32[]{:S(2)}, u32[]{:S(2)}) collective-permute-start(bf16[4,2,128,128]{3,2,1,0:T(8,128)(2,1)S(1)} %constant_dynamic-update-slice_fusion.7.refs_0_), channel_id=1, source_target_pairs={{0,4},{1,5},{2,6},{3,7},{4,0},{5,1},{6,2},{7,3},{8,12},{9,13},{10,... | collective-permute-start | bytes 786440 | tf_op jit(solution)/shard_map/ppermute | solution.py:145
  34.8 13.2 %collective-permute-start.12 = (bf16[4,2,128,128]{3,2,1,0:T(8,128)(2,1)S(1)}, bf16[4,2,128,128]{3,2,1,0:T(8,128)(2,1)S(1)}, u32[]{:S(2)}, u32[]{:S(2)}) collective-permute-start(bf16[4,2,128,128]{3,2,1,0:T(8,128)(2,1)S(1)} %constant_dynamic-update-slice_fusion.7.refs_0_), channel_id=1, source_target_pairs={{0,6},{1,7},{2,4},{3,5},{4,2},{5,3},{6,0},{7,1},{8,14},{9,15},{10,... | collective-permute-start | bytes 786440 | tf_op jit(solution)/shard_map/ppermute | solution.py:145
  50.1 5.9 %collective-permute-start.15 = (bf16[1,1,128,128]{3,2,1,0:T(8,128)(2,1)S(1)}, bf16[1,1,128,128]{3,2,1,0:T(8,128)(2,1)S(1)}, u32[]{:S(2)}, u32[]{:S(2)}) collective-permute-start(bf16[1,1,128,128]{3,2,1,0:T(8,128)(2,1)S(1)} %bitcast.33), channel_id=1, source_target_pairs={{0,8},{1,9},{2,10},{3,11},{4,12},{5,13},{6,14},{7,15},{8,16},{9,17... | collective-permute-start | bytes 98312 | tf_op jit(solution)/shard_map/ppermute | solution.py:158
  51.4 5.4 %collective-permute-start.16 = (bf16[1,1,128,128]{3,2,1,0:T(8,128)(2,1)S(1)}, bf16[1,1,128,128]{3,2,1,0:T(8,128)(2,1)S(1)}, u32[]{:S(2)}, u32[]{:S(2)}) collective-permute-start(bf16[1,1,128,128]{3,2,1,0:T(8,128)(2,1)S(1)} %bitcast.34), channel_id=1, source_target_pairs={{0,16},{1,17},{2,18},{3,19},{4,20},{5,21},{6,22},{7,23},{8,24},{9,... | collective-permute-start | bytes 98312 | tf_op jit(solution)/shard_map/ppermute | solution.py:158
  56.8 7.6 %collective-permute-start.20 = (bf16[8,128,128]{2,1,0:T(8,128)(2,1)S(1)}, bf16[8,128,128]{2,1,0:T(8,128)(2,1)S(1)}, u32[]{:S(2)}, u32[]{:S(2)}) collective-permute-start(bf16[8,128,128]{2,1,0:T(8,128)(2,1)S(1)} %get-tuple-element.76), channel_id=1, source_target_pairs={{0,1},{1,0},{2,3},{3,2},{4,5},{5,4},{6,7},{7,6},{8,9},{9,8},{10,11... | collective-permute-start | bytes 786440 | tf_op jit(solution)/shard_map/ppermute | solution.py:145
  59.3 5.2 %collective-permute-start.19 = (bf16[2,1,128,128]{3,2,1,0:T(8,128)(2,1)S(1)}, bf16[2,1,128,128]{3,2,1,0:T(8,128)(2,1)S(1)}, u32[]{:S(2)}, u32[]{:S(2)}) collective-permute-start(bf16[2,1,128,128]{3,2,1,0:T(8,128)(2,1)S(1)} %get-tuple-element.114), channel_id=1, source_target_pairs={{0,6},{1,7},{2,4},{3,5},{4,2},{5,3},{6,0},{7,1},{8,14},{9,15},{10,... | collective-permute-start | bytes 196616 | tf_op jit(solution)/shard_map/ppermute | solution.py:145
  68.1 4.8 %collective-permute-start.23 = (bf16[1,1,128,128]{3,2,1,0:T(8,128)(2,1)S(1)}, bf16[1,1,128,128]{3,2,1,0:T(8,128)(2,1)S(1)}, u32[]{:S(2)}, u32[]{:S(2)}) collective-permute-start(bf16[1,1,128,128]{3,2,1,0:T(8,128)(2,1)S(1)} %bitcast.27), channel_id=1, source_target_pairs={{0,16},{1,17},{2,18},{3,19},{4,20},{5,21},{6,22},{7,23},{8,24},{9,... | collective-permute-start | bytes 98312 | tf_op jit(solution)/shard_map/ppermute | solution.py:158
  73.0 7.1 %collective-permute-start.27 = (bf16[8,128,128]{2,1,0:T(8,128)(2,1)S(1)}, bf16[8,128,128]{2,1,0:T(8,128)(2,1)S(1)}, u32[]{:S(2)}, u32[]{:S(2)}) collective-permute-start(bf16[8,128,128]{2,1,0:T(8,128)(2,1)S(1)} %get-tuple-element.84), channel_id=1, source_target_pairs={{0,1},{1,0},{2,3},{3,2},{4,5},{5,4},{6,7},{7,6},{8,9},{9,8},{10,11... | collective-permute-start | bytes 786440 | tf_op jit(solution)/shard_map/ppermute | solution.py:145
  74.8 5.2 %collective-permute-start.26 = (bf16[2,1,128,128]{3,2,1,0:T(8,128)(2,1)S(1)}, bf16[2,1,128,128]{3,2,1,0:T(8,128)(2,1)S(1)}, u32[]{:S(2)}, u32[]{:S(2)}) collective-permute-start(bf16[2,1,128,128]{3,2,1,0:T(8,128)(2,1)S(1)} %get-tuple-element.112), channel_id=1, source_target_pairs={{0,6},{1,7},{2,4},{3,5},{4,2},{5,3},{6,0},{7,1},{8,14},{9,15},{10,... | collective-permute-start | bytes 196616 | tf_op jit(solution)/shard_map/ppermute | solution.py:145
  81.7 7.5 %collective-permute-start.29 = (bf16[1,1,128,128]{3,2,1,0:T(8,128)(2,1)S(1)}, bf16[1,1,128,128]{3,2,1,0:T(8,128)(2,1)S(1)}, u32[]{:S(2)}, u32[]{:S(2)}) collective-permute-start(bf16[1,1,128,128]{3,2,1,0:T(8,128)(2,1)S(1)} %bitcast.29), channel_id=1, source_target_pairs={{0,8},{1,9},{2,10},{3,11},{4,12},{5,13},{6,14},{7,15},{8,0},{9,1},... | collective-permute-start | bytes 98312 | tf_op jit(solution)/shard_map/ppermute | solution.py:145
  81.8 7.4 %collective-permute-start.30 = (bf16[1,1,128,128]{3,2,1,0:T(8,128)(2,1)S(1)}, bf16[1,1,128,128]{3,2,1,0:T(8,128)(2,1)S(1)}, u32[]{:S(2)}, u32[]{:S(2)}) collective-permute-start(bf16[1,1,128,128]{3,2,1,0:T(8,128)(2,1)S(1)} %bitcast.30), channel_id=1, source_target_pairs={{0,16},{1,17},{2,18},{3,19},{4,20},{5,21},{6,22},{7,23},{8,24},{9,... | collective-permute-start | bytes 98312 | tf_op jit(solution)/shard_map/ppermute | solution.py:145
  83.8 5.7 %collective-permute-start.31 = (bf16[1,1,128,128]{3,2,1,0:T(8,128)(2,1)S(1)}, bf16[1,1,128,128]{3,2,1,0:T(8,128)(2,1)S(1)}, u32[]{:S(2)}, u32[]{:S(2)}) collective-permute-start(bf16[1,1,128,128]{3,2,1,0:T(8,128)(2,1)S(1)} %bitcast.31), channel_id=1, source_target_pairs={{0,24},{1,25},{2,26},{3,27},{4,28},{5,29},{6,30},{7,31},{8,16},{9,... | collective-permute-start | bytes 98312 | tf_op jit(solution)/shard_map/ppermute | solution.py:145
  89.5 9.4 %collective-permute-start.35 = (bf16[2,16,128,128]{3,2,1,0:T(8,128)(2,1)S(1)}, bf16[2,16,128,128]{3,2,1,0:T(8,128)(2,1)S(1)}, u32[]{:S(2)}, u32[]{:S(2)}) collective-permute-start(bf16[2,16,128,128]{3,2,1,0:T(8,128)(2,1)S(1)} %get-tuple-element.93), channel_id=1, source_target_pairs={{0,1},{1,0},{2,3},{3,2},{4,5},{5,4},{6,7},{7,6},{8,9},{9,8},{10,11... | collective-permute-start | bytes 3145736 | tf_op jit(solution)/shard_map/ppermute | solution.py:145
  89.6 6.4 %collective-permute-start.32 = (bf16[4,1,128,128]{3,2,1,0:T(8,128)(2,1)S(1)}, bf16[4,1,128,128]{3,2,1,0:T(8,128)(2,1)S(1)}, u32[]{:S(2)}, u32[]{:S(2)}) collective-permute-start(bf16[4,1,128,128]{3,2,1,0:T(8,128)(2,1)S(1)} %constant_dynamic-update-slice_fusion.25.refs_0_), channel_id=1, source_target_pairs={{0,2},{1,3},{2,0},{3,1},{4,6},{5,7},{6,4},{7,5},{8,10},{9,11},{10,... | collective-permute-start | bytes 393224 | tf_op jit(solution)/shard_map/ppermute | solution.py:145
  90.4 8.4 %collective-permute-start.33 = (bf16[4,1,128,128]{3,2,1,0:T(8,128)(2,1)S(1)}, bf16[4,1,128,128]{3,2,1,0:T(8,128)(2,1)S(1)}, u32[]{:S(2)}, u32[]{:S(2)}) collective-permute-start(bf16[4,1,128,128]{3,2,1,0:T(8,128)(2,1)S(1)} %constant_dynamic-update-slice_fusion.25.refs_0_), channel_id=1, source_target_pairs={{0,4},{1,5},{2,6},{3,7},{4,0},{5,1},{6,2},{7,3},{8,12},{9,13},{10,... | collective-permute-start | bytes 393224 | tf_op jit(solution)/shard_map/ppermute | solution.py:145
  91.9 6.9 %collective-permute-start.34 = (bf16[4,1,128,128]{3,2,1,0:T(8,128)(2,1)S(1)}, bf16[4,1,128,128]{3,2,1,0:T(8,128)(2,1)S(1)}, u32[]{:S(2)}, u32[]{:S(2)}) collective-permute-start(bf16[4,1,128,128]{3,2,1,0:T(8,128)(2,1)S(1)} %constant_dynamic-update-slice_fusion.25.refs_0_), channel_id=1, source_target_pairs={{0,6},{1,7},{2,4},{3,5},{4,2},{5,3},{6,0},{7,1},{8,14},{9,15},{10,... | collective-permute-start | bytes 393224 | tf_op jit(solution)/shard_map/ppermute | solution.py:145
  103.3 5.5 %collective-permute-start.38 = (bf16[1,2,128,128]{3,2,1,0:T(8,128)(2,1)S(1)}, bf16[1,2,128,128]{3,2,1,0:T(8,128)(2,1)S(1)}, u32[]{:S(2)}, u32[]{:S(2)}) collective-permute-start(bf16[1,2,128,128]{3,2,1,0:T(8,128)(2,1)S(1)} %bitcast.24), channel_id=1, source_target_pairs={{0,16},{1,17},{2,18},{3,19},{4,20},{5,21},{6,22},{7,23},{8,24},{9,... | collective-permute-start | bytes 196616 | tf_op jit(solution)/shard_map/ppermute | solution.py:158
  108.7 9.9 %collective-permute-start.42 = (bf16[16,128,128]{2,1,0:T(8,128)(2,1)S(1)}, bf16[16,128,128]{2,1,0:T(8,128)(2,1)S(1)}, u32[]{:S(2)}, u32[]{:S(2)}) collective-permute-start(bf16[16,128,128]{2,1,0:T(8,128)(2,1)S(1)} %get-tuple-element.101), channel_id=1, source_target_pairs={{0,1},{1,0},{2,3},{3,2},{4,5},{5,4},{6,7},{7,6},{8,9},{9,8},{10,11... | collective-permute-start | bytes 1572872 | tf_op jit(solution)/shard_map/ppermute | solution.py:145
  108.9 6.4 %collective-permute-start.39 = (bf16[2,2,128,128]{3,2,1,0:T(8,128)(2,1)S(1)}, bf16[2,2,128,128]{3,2,1,0:T(8,128)(2,1)S(1)}, u32[]{:S(2)}, u32[]{:S(2)}) collective-permute-start(bf16[2,2,128,128]{3,2,1,0:T(8,128)(2,1)S(1)} %get-tuple-element.109), channel_id=1, source_target_pairs={{0,2},{1,3},{2,0},{3,1},{4,6},{5,7},{6,4},{7,5},{8,10},{9,11},{10,... | collective-permute-start | bytes 393224 | tf_op jit(solution)/shard_map/ppermute | solution.py:145
  110.2 6.8 %collective-permute-start.40 = (bf16[2,2,128,128]{3,2,1,0:T(8,128)(2,1)S(1)}, bf16[2,2,128,128]{3,2,1,0:T(8,128)(2,1)S(1)}, u32[]{:S(2)}, u32[]{:S(2)}) collective-permute-start(bf16[2,2,128,128]{3,2,1,0:T(8,128)(2,1)S(1)} %get-tuple-element.108), channel_id=1, source_target_pairs={{0,4},{1,5},{2,6},{3,7},{4,0},{5,1},{6,2},{7,3},{8,12},{9,13},{10,... | collective-permute-start | bytes 393224 | tf_op jit(solution)/shard_map/ppermute | solution.py:145
  111.1 7.6 %collective-permute-start.41 = (bf16[2,2,128,128]{3,2,1,0:T(8,128)(2,1)S(1)}, bf16[2,2,128,128]{3,2,1,0:T(8,128)(2,1)S(1)}, u32[]{:S(2)}, u32[]{:S(2)}) collective-permute-start(bf16[2,2,128,128]{3,2,1,0:T(8,128)(2,1)S(1)} %get-tuple-element.108), channel_id=1, source_target_pairs={{0,6},{1,7},{2,4},{3,5},{4,2},{5,3},{6,0},{7,1},{8,14},{9,15},{10,... | collective-permute-start | bytes 393224 | tf_op jit(solution)/shard_map/ppermute | solution.py:145
  (18 other events, 143.6 us)

commit v4 on v2

--- a/solution.py
+++ b/solution.py
@@ -139,26 +139,37 @@
     )(factor, *tables)
 
 
-def gather(block, shifts, table, pack):
+def gather(block, direction, table, pack):
     total = PLANE * PLANES
 
-    def move(value, pairs):
-        return lax.ppermute(value, "prow", pairs)
+    def swap(value, distance):
+        return lax.ppermute(value, "prow", [(i, i ^ distance) for i in range(total)])
 
     parts = [block[None]]
-    for shift in shifts:
-        if shift[0] == "xor":
-            pairs = [(i, i ^ (PLANE * shift[1])) for i in range(total)]
-        else:
-            pairs = [(i, (i + PLANE * shift[1]) % total) for i in range(total)]
-        parts.append(move(block[None], pairs))
+    if direction == 0:
+        parts += [swap(block[None], PLANE * step) for step in range(1, PLANES)]
+    else:
+        for step in (1, 2):
+            pairs = [(i, (i + direction * step * PLANE) % total) for i in range(total)]
+            parts.append(lax.ppermute(block[None], "prow", pairs))
     packed = pack(lax.optimization_barrier((table, block))[0])
-    stacked, packed = lax.optimization_barrier((jnp.concatenate(parts, 0), packed))
+    parts, packed = lax.optimization_barrier((parts, packed))
+    stacked = jnp.concatenate(parts, 0)
     pieces = {0: stacked}
+    if direction == 0:
+        sent = {1: stacked, 2: stacked, 4: stacked}
+    else:
+        near, far = jnp.concatenate(parts[:2], 0), jnp.concatenate(parts[1:], 0)
+        me = lax.axis_index("prow")
+        sent = {}
+        for bit in (1, 2, 4):
+            after = (me & bit) != 0
+            sent[bit] = jnp.where(after if direction > 0 else jnp.logical_not(after), far, near)
     for k in (6, 2, 4):
-        pieces[k] = move(pieces[0], [(i, i ^ k) for i in range(total)])
-    for k in (0, 6, 2, 4):
-        pieces[k + 1] = move(pieces[k], [(i, i ^ 1) for i in range(total)])
+        pieces[k] = swap(sent[2 if k == 2 else 4], k)
+    pieces[1] = swap(sent[1], 1)
+    for k in (6, 2, 4):
+        pieces[k + 1] = swap(pieces[k], 1)
     return [pieces[k] for k in range(PLANE)], packed
 
 
@@ -169,11 +180,14 @@
     for k in range(PLANE):
         other = offset ^ k
         first = (other - start) & (PLANE - 1)
+        skipped = jnp.int32(0)
+        if k > 0:
+            skipped = (other > offset if direction > 0 else other < offset).astype(jnp.int32)
         for half in range(SPAN // PLANE):
             slot = first + half * PLANE
             source = start + slot
             apart = direction * (block // PLANE - source // PLANE)
-            apart = jnp.clip(apart, 0, 2)
+            apart = jnp.clip(apart - skipped, 0, pieces[k].shape[0] - 1)
             level = source // (PLANE * PLANES) if pieces[k].shape[1] > 1 else 0
             at = pl.multiple_of(slot * size, size)
             xs[:, pl.ds(at, size)] = pieces[k][apart, level]
@@ -290,9 +304,7 @@
     tables = (lower_snode, upper_snode, parent, pattern)
     own = local_call(turn_kernel, "turn", [((rows, width, size), bf16)], [rhs])[0]
 
-    forward = (("shift", 1), ("shift", 2))
-    backward = (("shift", -1), ("shift", -2))
-    whole = (("xor", 1), ("xor", 2), ("xor", 3))
+    forward, backward, whole = 1, -1, 0
 
     def pack_l1(table):
         return pack_level(lower, table, 1, 0, 2, 0, 2 * total)

time: 123 us -> 120 us (0.976)
  starting transfers between devices: 48.6 us -> 43.6 us
  waiting for transfers between devices: 49.8 us -> 51.7 us
    ppermute x56, starting transfers between devices: 48.6 us -> 43.6 us  [the longest x48 32.2 us: swap(): lax.ppermute(value, 'prow', [(i, i ^ distance) for i in range(total)])]
    ppermute x56, waiting for transfers between devices: 49.8 us -> 51.7 us  [the longest x48 40 us: swap(): lax.ppermute(value, 'prow', [(i, i ^ distance) for i in range(total)])]
  transfers between devices with their start and end apart: 56 -> 56, of which waited for: 37 -> 32; matrix products, arithmetic and copies ran while one was open for 0% -> 0% of each run, Pallas kernels for 13% -> 13%
where the time goes in v4:
time: 120 us
  waiting for transfers between devices  51.7 us (43%)
  starting transfers between devices  43.6 us (36%)
  Pallas kernels  21 us (18%)
  local copies, waits for them, and re-layouts  1.96 us (2%)
    ppermute x48, waiting for transfers between devices, swap(): lax.ppermute(value, 'prow', [(i, i ^ distance) for i in range(total)])  40 us
    ppermute x48, starting transfers between devices, swap(): lax.ppermute(value, 'prow', [(i, i ^ distance) for i in range(total)])  32.2 us
    ppermute x8, waiting for transfers between devices, gather(): parts.append(lax.ppermute(block[None], 'prow', pairs))  11.7 us
    ppermute x8, starting transfers between devices, gather(): parts.append(lax.ppermute(block[None], 'prow', pairs))  11.4 us
    pallas_call x4, Pallas kernels, pack_level(): pl.pallas_call(functools.partial(pack_level_kernel, direction, base, rows...  7.63 us
    pallas_call x2, Pallas kernels, pack_coupling(): pl.pallas_call(kernel, out_shape=jax.ShapeDtypeStruct(shape, factor.dtype...  6.96 us
    pallas_call x8, Pallas kernels, local_call(): pl.pallas_call(kernel, out_shape=outs, in_specs=[pl.BlockSpec(memory_spac...  6.39 us
  transfers between devices with their start and end apart: 56, of which 32 were waited for; matrix products, arithmetic and copies ran while one was open for 0% of the time, Pallas kernels for 13%

profile of v4, /device:TPU:0, one launch (start us, length us, event | category | flops | bytes accessed | tf_op | source)
XLA Modules:
  0.0 119.5 jit_solution(1705510471123268922)
XLA Ops:
  1.7 3.1 %collective-permute-start = (bf16[1,2,128,128]{3,2,1,0:T(8,128)(2,1)S(1)}, bf16[1,2,128,128]{3,2,1,0:T(8,128)(2,1)S(1)}, u32[]{:S(2)}, u32[]{:S(2)}) collective-permute-start(bf16[1,2,128,128]{3,2,1,0:T(8,128)(2,1)S(1)} %slice_bitcast_fusion), channel_id=1, source_target_pairs={{0,8},{1,9},{2,10},{3,11},{4,12},{5,13},{6,14},{7,15},{8,16},{9,17... | collective-permute-start | bytes 196616 | tf_op jit(solution)/shard_map/ppermute | solution.py:154
  4.7 2.6 %collective-permute-start.1 = (bf16[1,2,128,128]{3,2,1,0:T(8,128)(2,1)S(1)}, bf16[1,2,128,128]{3,2,1,0:T(8,128)(2,1)S(1)}, u32[]{:S(2)}, u32[]{:S(2)}) collective-permute-start(bf16[1,2,128,128]{3,2,1,0:T(8,128)(2,1)S(1)} %slice_bitcast_fusion), channel_id=1, source_target_pairs={{0,16},{1,17},{2,18},{3,19},{4,20},{5,21},{6,22},{7,23},{8,24},{9,... | collective-permute-start | bytes 196616 | tf_op jit(solution)/shard_map/ppermute | solution.py:154
  8.0 2.1 %pack_level.4.refs_8_ = bf16[32,128,128]{2,1,0:T(8,128)(2,1)S(1)} custom-call(bf16[96,3,128,128]{3,2,1,0:T(8,128)(2,1)} %bitcast.33, s32[64]{0:T(128)S(1)} %copy-done.2), custom_call_target="tpu_custom_call" | custom-call | bytes 2097152 | tf_op jit(solution)/shard_map/pack_level/pallas_call | solution.py:66
  11.8 1.6 %collective-permute-start.3 = (bf16[2,2,128,128]{3,2,1,0:T(8,128)(2,1)S(1)}, bf16[2,2,128,128]{3,2,1,0:T(8,128)(2,1)S(1)}, u32[]{:S(2)}, u32[]{:S(2)}) collective-permute-start(bf16[2,2,128,128]{3,2,1,0:T(8,128)(2,1)S(1)} %get-tuple-element.82), channel_id=1, source_target_pairs={{0,2},{1,3},{2,0},{3,1},{4,6},{5,7},{6,4},{7,5},{8,10},{9,11},{10,... | collective-permute-start | bytes 393224 | tf_op jit(solution)/shard_map/ppermute | solution.py:146
  15.3 2.5 %collective-permute-done.3.refs_2_ = bf16[2,2,128,128]{3,2,1,0:T(8,128)(2,1)S(1)} collective-permute-done((bf16[2,2,128,128]{3,2,1,0:T(8,128)(2,1)S(1)}, bf16[2,2,128,128]{3,2,1,0:T(8,128)(2,1)S(1)}, u32[]{:S(2)}, u32[]{:S(2)}) %collective-permute-start.3) | collective-permute-done | bytes 131104 | tf_op jit(solution)/shard_map/ppermute | solution.py:146
  17.9 3.2 %collective-permute-done.5.refs_4_ = bf16[2,2,128,128]{3,2,1,0:T(8,128)(2,1)S(1)} collective-permute-done((bf16[2,2,128,128]{3,2,1,0:T(8,128)(2,1)S(1)}, bf16[2,2,128,128]{3,2,1,0:T(8,128)(2,1)S(1)}, u32[]{:S(2)}, u32[]{:S(2)}) %collective-permute-start.5) | collective-permute-done | bytes 131104 | tf_op jit(solution)/shard_map/ppermute | solution.py:146
  23.4 2.0 %collective-permute-start.10 = (bf16[1,2,128,128]{3,2,1,0:T(8,128)(2,1)S(1)}, bf16[1,2,128,128]{3,2,1,0:T(8,128)(2,1)S(1)}, u32[]{:S(2)}, u32[]{:S(2)}) collective-permute-start(bf16[1,2,128,128]{3,2,1,0:T(8,128)(2,1)S(1)} %bitcast.26), channel_id=1, source_target_pairs={{0,16},{1,17},{2,18},{3,19},{4,20},{5,21},{6,22},{7,23},{8,24},{9,... | collective-permute-start | bytes 196616 | tf_op jit(solution)/shard_map/ppermute | solution.py:146
  25.4 2.4 %collective-permute-start.11 = (bf16[1,2,128,128]{3,2,1,0:T(8,128)(2,1)S(1)}, bf16[1,2,128,128]{3,2,1,0:T(8,128)(2,1)S(1)}, u32[]{:S(2)}, u32[]{:S(2)}) collective-permute-start(bf16[1,2,128,128]{3,2,1,0:T(8,128)(2,1)S(1)} %bitcast.27), channel_id=1, source_target_pairs={{0,24},{1,25},{2,26},{3,27},{4,28},{5,29},{6,30},{7,31},{8,16},{9,... | collective-permute-start | bytes 196616 | tf_op jit(solution)/shard_map/ppermute | solution.py:146
  28.0 3.8 %pack_down.1.refs_8_ = bf16[64,128,128]{2,1,0:T(8,128)(2,1)S(1)} custom-call(bf16[96,3,128,128]{3,2,1,0:T(8,128)(2,1)} %bitcast.34, s32[64]{0:T(128)S(1)} %copy-done.3, s32[32]{0:T(128)S(1)} %copy-done.1, s32[5,1]{1,0:T(8,128)S(1)} %copy.9.parent, s32[32,5]{1,0:T(8,128)S(1)} %copy.10.pattern), custom_call_target="tpu_custom_call" | custom-call | bytes 4194304 | tf_op jit(solution)/shard_map/pack_down/pallas_call | solution.py:129
  35.8 5.8 %collective-permute-done.13.refs_2_ = bf16[4,2,128,128]{3,2,1,0:T(8,128)(2,1)S(1)} collective-permute-done((bf16[4,2,128,128]{3,2,1,0:T(8,128)(2,1)S(1)}, bf16[4,2,128,128]{3,2,1,0:T(8,128)(2,1)S(1)}, u32[]{:S(2)}, u32[]{:S(2)}) %collective-permute-start.13) | collective-permute-done | bytes 262176 | tf_op jit(solution)/shard_map/ppermute | solution.py:146
  42.0 4.0 %collective-permute-done.17.refs_6_ = bf16[4,2,128,128]{3,2,1,0:T(8,128)(2,1)S(1)} collective-permute-done((bf16[4,2,128,128]{3,2,1,0:T(8,128)(2,1)S(1)}, bf16[4,2,128,128]{3,2,1,0:T(8,128)(2,1)S(1)}, u32[]{:S(2)}, u32[]{:S(2)}) %collective-permute-start.17) | collective-permute-done | bytes 262176 | tf_op jit(solution)/shard_map/ppermute | solution.py:146
  48.9 1.8 %collective-permute-start.19 = (bf16[1,1,128,128]{3,2,1,0:T(8,128)(2,1)S(1)}, bf16[1,1,128,128]{3,2,1,0:T(8,128)(2,1)S(1)}, u32[]{:S(2)}, u32[]{:S(2)}) collective-permute-start(bf16[1,1,128,128]{3,2,1,0:T(8,128)(2,1)S(1)} %bitcast.17), channel_id=1, source_target_pairs={{0,8},{1,9},{2,10},{3,11},{4,12},{5,13},{6,14},{7,15},{8,16},{9,17... | collective-permute-start | bytes 98312 | tf_op jit(solution)/shard_map/ppermute | solution.py:154
  50.9 1.8 %pack_level.5.refs_8_ = bf16[16,128,128]{2,1,0:T(8,128)(2,1)S(1)} custom-call(bf16[96,3,128,128]{3,2,1,0:T(8,128)(2,1)} %bitcast.35, s32[32]{0:T(128)S(1)} %copy-done.1), custom_call_target="tpu_custom_call" | custom-call | bytes 1048576 | tf_op jit(solution)/shard_map/pack_level/pallas_call | solution.py:66
  52.8 2.2 %collective-permute-done.19 = bf16[1,1,128,128]{3,2,1,0:T(8,128)(2,1)S(1)} collective-permute-done((bf16[1,1,128,128]{3,2,1,0:T(8,128)(2,1)S(1)}, bf16[1,1,128,128]{3,2,1,0:T(8,128)(2,1)S(1)}, u32[]{:S(2)}, u32[]{:S(2)}) %collective-permute-start.19) | collective-permute-done | bytes 32800 | tf_op jit(solution)/shard_map/ppermute | solution.py:154
  60.5 1.7 %collective-permute-done.24.refs_4_ = bf16[2,1,128,128]{3,2,1,0:T(8,128)(2,1)S(1)} collective-permute-done((bf16[2,1,128,128]{3,2,1,0:T(8,128)(2,1)S(1)}, bf16[2,1,128,128]{3,2,1,0:T(8,128)(2,1)S(1)}, u32[]{:S(2)}, u32[]{:S(2)}) %collective-permute-start.24) | collective-permute-done | bytes 65568 | tf_op jit(solution)/shard_map/ppermute | solution.py:146
  62.2 1.6 %collective-permute-done.26.refs_6_ = bf16[2,1,128,128]{3,2,1,0:T(8,128)(2,1)S(1)} collective-permute-done((bf16[2,1,128,128]{3,2,1,0:T(8,128)(2,1)S(1)}, bf16[2,1,128,128]{3,2,1,0:T(8,128)(2,1)S(1)}, u32[]{:S(2)}, u32[]{:S(2)}) %collective-permute-start.26) | collective-permute-done | bytes 65568 | tf_op jit(solution)/shard_map/ppermute | solution.py:146
  65.5 1.8 %collective-permute-start.28 = (bf16[1,1,128,128]{3,2,1,0:T(8,128)(2,1)S(1)}, bf16[1,1,128,128]{3,2,1,0:T(8,128)(2,1)S(1)}, u32[]{:S(2)}, u32[]{:S(2)}) collective-permute-start(bf16[1,1,128,128]{3,2,1,0:T(8,128)(2,1)S(1)} %bitcast.21), channel_id=1, source_target_pairs={{0,24},{1,25},{2,26},{3,27},{4,28},{5,29},{6,30},{7,31},{8,0},{9,1... | collective-permute-start | bytes 98312 | tf_op jit(solution)/shard_map/ppermute | solution.py:154
  67.4 1.8 %pack_level.6.refs_8_ = bf16[16,128,128]{2,1,0:T(8,128)(2,1)S(1)} custom-call(bf16[96,3,128,128]{3,2,1,0:T(8,128)(2,1)} %bitcast.36, s32[32]{0:T(128)S(1)} %copy-done.1), custom_call_target="tpu_custom_call" | custom-call | bytes 1048576 | tf_op jit(solution)/shard_map/pack_level/pallas_call | solution.py:66
  69.5 2.7 %collective-permute-done.29 = bf16[1,1,128,128]{3,2,1,0:T(8,128)(2,1)S(1)} collective-permute-done((bf16[1,1,128,128]{3,2,1,0:T(8,128)(2,1)S(1)}, bf16[1,1,128,128]{3,2,1,0:T(8,128)(2,1)S(1)}, u32[]{:S(2)}, u32[]{:S(2)}) %collective-permute-start.29) | collective-permute-done | bytes 32800 | tf_op jit(solution)/shard_map/ppermute | solution.py:154
  73.7 2.1 %collective-permute-start.35 = (bf16[2,1,128,128]{3,2,1,0:T(8,128)(2,1)S(1)}, bf16[2,1,128,128]{3,2,1,0:T(8,128)(2,1)S(1)}, u32[]{:S(2)}, u32[]{:S(2)}) collective-permute-start(bf16[2,1,128,128]{3,2,1,0:T(8,128)(2,1)S(1)} %get-tuple-element.84), channel_id=1, source_target_pairs={{0,6},{1,7},{2,4},{3,5},{4,2},{5,3},{6,0},{7,1},{8,14},{9,15},{10,... | collective-permute-start | bytes 196616 | tf_op jit(solution)/shard_map/ppermute | solution.py:146
  77.1 1.7 %collective-permute-done.35.refs_6_ = bf16[2,1,128,128]{3,2,1,0:T(8,128)(2,1)S(1)} collective-permute-done((bf16[2,1,128,128]{3,2,1,0:T(8,128)(2,1)S(1)}, bf16[2,1,128,128]{3,2,1,0:T(8,128)(2,1)S(1)}, u32[]{:S(2)}, u32[]{:S(2)}) %collective-permute-start.35) | collective-permute-done | bytes 65568 | tf_op jit(solution)/shard_map/ppermute | solution.py:146
  80.9 1.8 %collective-permute-start.38 = (bf16[1,1,128,128]{3,2,1,0:T(8,128)(2,1)S(1)}, bf16[1,1,128,128]{3,2,1,0:T(8,128)(2,1)S(1)}, u32[]{:S(2)}, u32[]{:S(2)}) collective-permute-start(bf16[1,1,128,128]{3,2,1,0:T(8,128)(2,1)S(1)} %bitcast.30), channel_id=1, source_target_pairs={{0,16},{1,17},{2,18},{3,19},{4,20},{5,21},{6,22},{7,23},{8,24},{9,... | collective-permute-start | bytes 98312 | tf_op jit(solution)/shard_map/ppermute | solution.py:146
  82.6 2.4 %collective-permute-start.39 = (bf16[1,1,128,128]{3,2,1,0:T(8,128)(2,1)S(1)}, bf16[1,1,128,128]{3,2,1,0:T(8,128)(2,1)S(1)}, u32[]{:S(2)}, u32[]{:S(2)}) collective-permute-start(bf16[1,1,128,128]{3,2,1,0:T(8,128)(2,1)S(1)} %bitcast.31), channel_id=1, source_target_pairs={{0,24},{1,25},{2,26},{3,27},{4,28},{5,29},{6,30},{7,31},{8,16},{9,... | collective-permute-start | bytes 98312 | tf_op jit(solution)/shard_map/ppermute | solution.py:146
  85.0 3.2 %pack_up.1.refs_8_ = bf16[2,32,128,128]{3,2,1,0:T(8,128)(2,1)S(1)} custom-call(bf16[96,3,128,128]{3,2,1,0:T(8,128)(2,1)} %bitcast.37, s32[64]{0:T(128)S(1)} %copy-done.3, s32[32]{0:T(128)S(1)} %copy-done.1, s32[5,1]{1,0:T(8,128)S(1)} %copy.9.parent, s32[32,5]{1,0:T(8,128)S(1)} %copy.10.pattern), custom_call_target="tpu_custom_call" | custom-call | bytes 4194304 | tf_op jit(solution)/shard_map/pack_up/pallas_call | solution.py:129
  91.9 2.4 %collective-permute-done.41.refs_2_ = bf16[4,1,128,128]{3,2,1,0:T(8,128)(2,1)S(1)} collective-permute-done((bf16[4,1,128,128]{3,2,1,0:T(8,128)(2,1)S(1)}, bf16[4,1,128,128]{3,2,1,0:T(8,128)(2,1)S(1)}, u32[]{:S(2)}, u32[]{:S(2)}) %collective-permute-start.41) | collective-permute-done | bytes 131104 | tf_op jit(solution)/shard_map/ppermute | solution.py:146
  94.4 3.2 %collective-permute-done.43.refs_4_ = bf16[4,1,128,128]{3,2,1,0:T(8,128)(2,1)S(1)} collective-permute-done((bf16[4,1,128,128]{3,2,1,0:T(8,128)(2,1)S(1)}, bf16[4,1,128,128]{3,2,1,0:T(8,128)(2,1)S(1)}, u32[]{:S(2)}, u32[]{:S(2)}) %collective-permute-start.43) | collective-permute-done | bytes 131104 | tf_op jit(solution)/shard_map/ppermute | solution.py:146
  100.1 1.8 %collective-permute-start.47 = (bf16[1,2,128,128]{3,2,1,0:T(8,128)(2,1)S(1)}, bf16[1,2,128,128]{3,2,1,0:T(8,128)(2,1)S(1)}, u32[]{:S(2)}, u32[]{:S(2)}) collective-permute-start(bf16[1,2,128,128]{3,2,1,0:T(8,128)(2,1)S(1)} %bitcast.13), channel_id=1, source_target_pairs={{0,24},{1,25},{2,26},{3,27},{4,28},{5,29},{6,30},{7,31},{8,0},{9,1... | collective-permute-start | bytes 196616 | tf_op jit(solution)/shard_map/ppermute | solution.py:154
  101.9 1.9 %pack_level.7.refs_8_ = bf16[32,128,128]{2,1,0:T(8,128)(2,1)S(1)} custom-call(bf16[96,3,128,128]{3,2,1,0:T(8,128)(2,1)} %bitcast.38, s32[64]{0:T(128)S(1)} %copy-done.3), custom_call_target="tpu_custom_call" | custom-call | bytes 2097152 | tf_op jit(solution)/shard_map/pack_level/pallas_call | solution.py:66
  104.5 3.5 %collective-permute-done.48 = bf16[1,2,128,128]{3,2,1,0:T(8,128)(2,1)S(1)} collective-permute-done((bf16[1,2,128,128]{3,2,1,0:T(8,128)(2,1)S(1)}, bf16[1,2,128,128]{3,2,1,0:T(8,128)(2,1)S(1)}, u32[]{:S(2)}, u32[]{:S(2)}) %collective-permute-start.48) | collective-permute-done | bytes 65568 | tf_op jit(solution)/shard_map/ppermute | solution.py:154
  109.5 2.1 %collective-permute-start.54 = (bf16[2,2,128,128]{3,2,1,0:T(8,128)(2,1)S(1)}, bf16[2,2,128,128]{3,2,1,0:T(8,128)(2,1)S(1)}, u32[]{:S(2)}, u32[]{:S(2)}) collective-permute-start(bf16[2,2,128,128]{3,2,1,0:T(8,128)(2,1)S(1)} %get-tuple-element.78), channel_id=1, source_target_pairs={{0,6},{1,7},{2,4},{3,5},{4,2},{5,3},{6,0},{7,1},{8,14},{9,15},{10,... | collective-permute-start | bytes 393224 | tf_op jit(solution)/shard_map/ppermute | solution.py:146
  111.6 2.9 %collective-permute-done.50.refs_2_ = bf16[2,2,128,128]{3,2,1,0:T(8,128)(2,1)S(1)} collective-permute-done((bf16[2,2,128,128]{3,2,1,0:T(8,128)(2,1)S(1)}, bf16[2,2,128,128]{3,2,1,0:T(8,128)(2,1)S(1)}, u32[]{:S(2)}, u32[]{:S(2)}) %collective-permute-start.50) | collective-permute-done | bytes 131104 | tf_op jit(solution)/shard_map/ppermute | solution.py:146
  115.0 1.6 %collective-permute-done.54.refs_6_ = bf16[2,2,128,128]{3,2,1,0:T(8,128)(2,1)S(1)} collective-permute-done((bf16[2,2,128,128]{3,2,1,0:T(8,128)(2,1)S(1)}, bf16[2,2,128,128]{3,2,1,0:T(8,128)(2,1)S(1)}, u32[]{:S(2)}, u32[]{:S(2)}) %collective-permute-start.54) | collective-permute-done | bytes 131104 | tf_op jit(solution)/shard_map/ppermute | solution.py:146
  (137 shorter events, 39.5 us)
Async XLA Ops:
  1.7 8.4 %collective-permute-start = (bf16[1,2,128,128]{3,2,1,0:T(8,128)(2,1)S(1)}, bf16[1,2,128,128]{3,2,1,0:T(8,128)(2,1)S(1)}, u32[]{:S(2)}, u32[]{:S(2)}) collective-permute-start(bf16[1,2,128,128]{3,2,1,0:T(8,128)(2,1)S(1)} %slice_bitcast_fusion), channel_id=1, source_target_pairs={{0,8},{1,9},{2,10},{3,11},{4,12},{5,13},{6,14},{7,15},{8,16},{9,17... | collective-permute-start | bytes 196616 | tf_op jit(solution)/shard_map/ppermute | solution.py:154
  4.7 6.9 %collective-permute-start.1 = (bf16[1,2,128,128]{3,2,1,0:T(8,128)(2,1)S(1)}, bf16[1,2,128,128]{3,2,1,0:T(8,128)(2,1)S(1)}, u32[]{:S(2)}, u32[]{:S(2)}) collective-permute-start(bf16[1,2,128,128]{3,2,1,0:T(8,128)(2,1)S(1)} %slice_bitcast_fusion), channel_id=1, source_target_pairs={{0,16},{1,17},{2,18},{3,19},{4,20},{5,21},{6,22},{7,23},{8,24},{9,... | collective-permute-start | bytes 196616 | tf_op jit(solution)/shard_map/ppermute | solution.py:154
  11.8 6.1 %collective-permute-start.3 = (bf16[2,2,128,128]{3,2,1,0:T(8,128)(2,1)S(1)}, bf16[2,2,128,128]{3,2,1,0:T(8,128)(2,1)S(1)}, u32[]{:S(2)}, u32[]{:S(2)}) collective-permute-start(bf16[2,2,128,128]{3,2,1,0:T(8,128)(2,1)S(1)} %get-tuple-element.82), channel_id=1, source_target_pairs={{0,2},{1,3},{2,0},{3,1},{4,6},{5,7},{6,4},{7,5},{8,10},{9,11},{10,... | collective-permute-start | bytes 393224 | tf_op jit(solution)/shard_map/ppermute | solution.py:146
  13.3 7.8 %collective-permute-start.5 = (bf16[2,2,128,128]{3,2,1,0:T(8,128)(2,1)S(1)}, bf16[2,2,128,128]{3,2,1,0:T(8,128)(2,1)S(1)}, u32[]{:S(2)}, u32[]{:S(2)}) collective-permute-start(bf16[2,2,128,128]{3,2,1,0:T(8,128)(2,1)S(1)} %get-tuple-element.81), channel_id=1, source_target_pairs={{0,4},{1,5},{2,6},{3,7},{4,0},{5,1},{6,2},{7,3},{8,12},{9,13},{10,... | collective-permute-start | bytes 393224 | tf_op jit(solution)/shard_map/ppermute | solution.py:146
  14.8 6.3 %collective-permute-start.7 = (bf16[2,2,128,128]{3,2,1,0:T(8,128)(2,1)S(1)}, bf16[2,2,128,128]{3,2,1,0:T(8,128)(2,1)S(1)}, u32[]{:S(2)}, u32[]{:S(2)}) collective-permute-start(bf16[2,2,128,128]{3,2,1,0:T(8,128)(2,1)S(1)} %get-tuple-element.81), channel_id=1, source_target_pairs={{0,6},{1,7},{2,4},{3,5},{4,2},{5,3},{6,0},{7,1},{8,14},{9,15},{10,... | collective-permute-start | bytes 393224 | tf_op jit(solution)/shard_map/ppermute | solution.py:146
  15.3 6.3 %collective-permute-start.2 = (bf16[2,2,128,128]{3,2,1,0:T(8,128)(2,1)S(1)}, bf16[2,2,128,128]{3,2,1,0:T(8,128)(2,1)S(1)}, u32[]{:S(2)}, u32[]{:S(2)}) collective-permute-start(bf16[2,2,128,128]{3,2,1,0:T(8,128)(2,1)S(1)} %get-tuple-element.83), channel_id=1, source_target_pairs={{0,1},{1,0},{2,3},{3,2},{4,5},{5,4},{6,7},{7,6},{8,9},{9,8},{10,11... | collective-permute-start | bytes 393224 | tf_op jit(solution)/shard_map/ppermute | solution.py:146
  23.4 8.4 %collective-permute-start.9 = (bf16[1,2,128,128]{3,2,1,0:T(8,128)(2,1)S(1)}, bf16[1,2,128,128]{3,2,1,0:T(8,128)(2,1)S(1)}, u32[]{:S(2)}, u32[]{:S(2)}) collective-permute-start(bf16[1,2,128,128]{3,2,1,0:T(8,128)(2,1)S(1)} %bitcast.25), channel_id=1, source_target_pairs={{0,8},{1,9},{2,10},{3,11},{4,12},{5,13},{6,14},{7,15},{8,0},{9,1},... | collective-permute-start | bytes 196616 | tf_op jit(solution)/shard_map/ppermute | solution.py:146
  23.4 8.7 %collective-permute-start.10 = (bf16[1,2,128,128]{3,2,1,0:T(8,128)(2,1)S(1)}, bf16[1,2,128,128]{3,2,1,0:T(8,128)(2,1)S(1)}, u32[]{:S(2)}, u32[]{:S(2)}) collective-permute-start(bf16[1,2,128,128]{3,2,1,0:T(8,128)(2,1)S(1)} %bitcast.26), channel_id=1, source_target_pairs={{0,16},{1,17},{2,18},{3,19},{4,20},{5,21},{6,22},{7,23},{8,24},{9,... | collective-permute-start | bytes 196616 | tf_op jit(solution)/shard_map/ppermute | solution.py:146
  25.4 6.7 %collective-permute-start.11 = (bf16[1,2,128,128]{3,2,1,0:T(8,128)(2,1)S(1)}, bf16[1,2,128,128]{3,2,1,0:T(8,128)(2,1)S(1)}, u32[]{:S(2)}, u32[]{:S(2)}) collective-permute-start(bf16[1,2,128,128]{3,2,1,0:T(8,128)(2,1)S(1)} %bitcast.27), channel_id=1, source_target_pairs={{0,24},{1,25},{2,26},{3,27},{4,28},{5,29},{6,30},{7,31},{8,16},{9,... | collective-permute-start | bytes 196616 | tf_op jit(solution)/shard_map/ppermute | solution.py:146
  32.2 9.3 %collective-permute-start.13 = (bf16[4,2,128,128]{3,2,1,0:T(8,128)(2,1)S(1)}, bf16[4,2,128,128]{3,2,1,0:T(8,128)(2,1)S(1)}, u32[]{:S(2)}, u32[]{:S(2)}) collective-permute-start(bf16[4,2,128,128]{3,2,1,0:T(8,128)(2,1)S(1)} %constant_dynamic-update-slice_fusion.4.refs_0_), channel_id=1, source_target_pairs={{0,2},{1,3},{2,0},{3,1},{4,6},{5,7},{6,4},{7,5},{8,10},{9,11},{10,... | collective-permute-start | bytes 786440 | tf_op jit(solution)/shard_map/ppermute | solution.py:146
  33.1 8.5 %collective-permute-start.15 = (bf16[4,2,128,128]{3,2,1,0:T(8,128)(2,1)S(1)}, bf16[4,2,128,128]{3,2,1,0:T(8,128)(2,1)S(1)}, u32[]{:S(2)}, u32[]{:S(2)}) collective-permute-start(bf16[4,2,128,128]{3,2,1,0:T(8,128)(2,1)S(1)} %constant_dynamic-update-slice_fusion.4.refs_0_), channel_id=1, source_target_pairs={{0,4},{1,5},{2,6},{3,7},{4,0},{5,1},{6,2},{7,3},{8,12},{9,13},{10,... | collective-permute-start | bytes 786440 | tf_op jit(solution)/shard_map/ppermute | solution.py:146
  34.2 11.8 %collective-permute-start.17 = (bf16[4,2,128,128]{3,2,1,0:T(8,128)(2,1)S(1)}, bf16[4,2,128,128]{3,2,1,0:T(8,128)(2,1)S(1)}, u32[]{:S(2)}, u32[]{:S(2)}) collective-permute-start(bf16[4,2,128,128]{3,2,1,0:T(8,128)(2,1)S(1)} %constant_dynamic-update-slice_fusion.4.refs_0_), channel_id=1, source_target_pairs={{0,6},{1,7},{2,4},{3,5},{4,2},{5,3},{6,0},{7,1},{8,14},{9,15},{10,... | collective-permute-start | bytes 786440 | tf_op jit(solution)/shard_map/ppermute | solution.py:146
  35.8 10.3 %collective-permute-start.12 = (bf16[4,2,128,128]{3,2,1,0:T(8,128)(2,1)S(1)}, bf16[4,2,128,128]{3,2,1,0:T(8,128)(2,1)S(1)}, u32[]{:S(2)}, u32[]{:S(2)}) collective-permute-start(bf16[4,2,128,128]{3,2,1,0:T(8,128)(2,1)S(1)} %constant_dynamic-update-slice_fusion.4.refs_0_), channel_id=1, source_target_pairs={{0,1},{1,0},{2,3},{3,2},{4,5},{5,4},{6,7},{7,6},{8,9},{9,8},{10,11... | collective-permute-start | bytes 786440 | tf_op jit(solution)/shard_map/ppermute | solution.py:146
  48.9 6.1 %collective-permute-start.19 = (bf16[1,1,128,128]{3,2,1,0:T(8,128)(2,1)S(1)}, bf16[1,1,128,128]{3,2,1,0:T(8,128)(2,1)S(1)}, u32[]{:S(2)}, u32[]{:S(2)}) collective-permute-start(bf16[1,1,128,128]{3,2,1,0:T(8,128)(2,1)S(1)} %bitcast.17), channel_id=1, source_target_pairs={{0,8},{1,9},{2,10},{3,11},{4,12},{5,13},{6,14},{7,15},{8,16},{9,17... | collective-permute-start | bytes 98312 | tf_op jit(solution)/shard_map/ppermute | solution.py:154
  50.7 5.2 %collective-permute-start.20 = (bf16[1,1,128,128]{3,2,1,0:T(8,128)(2,1)S(1)}, bf16[1,1,128,128]{3,2,1,0:T(8,128)(2,1)S(1)}, u32[]{:S(2)}, u32[]{:S(2)}) collective-permute-start(bf16[1,1,128,128]{3,2,1,0:T(8,128)(2,1)S(1)} %bitcast.18), channel_id=1, source_target_pairs={{0,16},{1,17},{2,18},{3,19},{4,20},{5,21},{6,22},{7,23},{8,24},{9,... | collective-permute-start | bytes 98312 | tf_op jit(solution)/shard_map/ppermute | solution.py:154
  55.9 4.6 %collective-permute-start.22 = (bf16[2,1,128,128]{3,2,1,0:T(8,128)(2,1)S(1)}, bf16[2,1,128,128]{3,2,1,0:T(8,128)(2,1)S(1)}, u32[]{:S(2)}, u32[]{:S(2)}) collective-permute-start(bf16[2,1,128,128]{3,2,1,0:T(8,128)(2,1)S(1)} %get-tuple-element.88), channel_id=1, source_target_pairs={{0,2},{1,3},{2,0},{3,1},{4,6},{5,7},{6,4},{7,5},{8,10},{9,11},{10,... | collective-permute-start | bytes 196616 | tf_op jit(solution)/shard_map/ppermute | solution.py:146
  57.3 4.9 %collective-permute-start.24 = (bf16[2,1,128,128]{3,2,1,0:T(8,128)(2,1)S(1)}, bf16[2,1,128,128]{3,2,1,0:T(8,128)(2,1)S(1)}, u32[]{:S(2)}, u32[]{:S(2)}) collective-permute-start(bf16[2,1,128,128]{3,2,1,0:T(8,128)(2,1)S(1)} %get-tuple-element.87), channel_id=1, source_target_pairs={{0,4},{1,5},{2,6},{3,7},{4,0},{5,1},{6,2},{7,3},{8,12},{9,13},{10,... | collective-permute-start | bytes 196616 | tf_op jit(solution)/shard_map/ppermute | solution.py:146
  58.7 5.2 %collective-permute-start.26 = (bf16[2,1,128,128]{3,2,1,0:T(8,128)(2,1)S(1)}, bf16[2,1,128,128]{3,2,1,0:T(8,128)(2,1)S(1)}, u32[]{:S(2)}, u32[]{:S(2)}) collective-permute-start(bf16[2,1,128,128]{3,2,1,0:T(8,128)(2,1)S(1)} %get-tuple-element.87), channel_id=1, source_target_pairs={{0,6},{1,7},{2,4},{3,5},{4,2},{5,3},{6,0},{7,1},{8,14},{9,15},{10,... | collective-permute-start | bytes 196616 | tf_op jit(solution)/shard_map/ppermute | solution.py:146
  67.3 4.9 %collective-permute-start.29 = (bf16[1,1,128,128]{3,2,1,0:T(8,128)(2,1)S(1)}, bf16[1,1,128,128]{3,2,1,0:T(8,128)(2,1)S(1)}, u32[]{:S(2)}, u32[]{:S(2)}) collective-permute-start(bf16[1,1,128,128]{3,2,1,0:T(8,128)(2,1)S(1)} %bitcast.22), channel_id=1, source_target_pairs={{0,16},{1,17},{2,18},{3,19},{4,20},{5,21},{6,22},{7,23},{8,24},{9,... | collective-permute-start | bytes 98312 | tf_op jit(solution)/shard_map/ppermute | solution.py:154
  73.7 5.2 %collective-permute-start.35 = (bf16[2,1,128,128]{3,2,1,0:T(8,128)(2,1)S(1)}, bf16[2,1,128,128]{3,2,1,0:T(8,128)(2,1)S(1)}, u32[]{:S(2)}, u32[]{:S(2)}) collective-permute-start(bf16[2,1,128,128]{3,2,1,0:T(8,128)(2,1)S(1)} %get-tuple-element.84), channel_id=1, source_target_pairs={{0,6},{1,7},{2,4},{3,5},{4,2},{5,3},{6,0},{7,1},{8,14},{9,15},{10,... | collective-permute-start | bytes 196616 | tf_op jit(solution)/shard_map/ppermute | solution.py:146
  80.6 7.7 %collective-permute-start.37 = (bf16[1,1,128,128]{3,2,1,0:T(8,128)(2,1)S(1)}, bf16[1,1,128,128]{3,2,1,0:T(8,128)(2,1)S(1)}, u32[]{:S(2)}, u32[]{:S(2)}) collective-permute-start(bf16[1,1,128,128]{3,2,1,0:T(8,128)(2,1)S(1)} %bitcast.29), channel_id=1, source_target_pairs={{0,8},{1,9},{2,10},{3,11},{4,12},{5,13},{6,14},{7,15},{8,0},{9,1},... | collective-permute-start | bytes 98312 | tf_op jit(solution)/shard_map/ppermute | solution.py:146
  80.9 7.4 %collective-permute-start.38 = (bf16[1,1,128,128]{3,2,1,0:T(8,128)(2,1)S(1)}, bf16[1,1,128,128]{3,2,1,0:T(8,128)(2,1)S(1)}, u32[]{:S(2)}, u32[]{:S(2)}) collective-permute-start(bf16[1,1,128,128]{3,2,1,0:T(8,128)(2,1)S(1)} %bitcast.30), channel_id=1, source_target_pairs={{0,16},{1,17},{2,18},{3,19},{4,20},{5,21},{6,22},{7,23},{8,24},{9,... | collective-permute-start | bytes 98312 | tf_op jit(solution)/shard_map/ppermute | solution.py:146
  82.6 5.7 %collective-permute-start.39 = (bf16[1,1,128,128]{3,2,1,0:T(8,128)(2,1)S(1)}, bf16[1,1,128,128]{3,2,1,0:T(8,128)(2,1)S(1)}, u32[]{:S(2)}, u32[]{:S(2)}) collective-permute-start(bf16[1,1,128,128]{3,2,1,0:T(8,128)(2,1)S(1)} %bitcast.31), channel_id=1, source_target_pairs={{0,24},{1,25},{2,26},{3,27},{4,28},{5,29},{6,30},{7,31},{8,16},{9,... | collective-permute-start | bytes 98312 | tf_op jit(solution)/shard_map/ppermute | solution.py:146
  88.4 6.0 %collective-permute-start.41 = (bf16[4,1,128,128]{3,2,1,0:T(8,128)(2,1)S(1)}, bf16[4,1,128,128]{3,2,1,0:T(8,128)(2,1)S(1)}, u32[]{:S(2)}, u32[]{:S(2)}) collective-permute-start(bf16[4,1,128,128]{3,2,1,0:T(8,128)(2,1)S(1)} %constant_dynamic-update-slice_fusion.16.refs_0_), channel_id=1, source_target_pairs={{0,2},{1,3},{2,0},{3,1},{4,6},{5,7},{6,4},{7,5},{8,10},{9,11},{10,... | collective-permute-start | bytes 393224 | tf_op jit(solution)/shard_map/ppermute | solution.py:146
  89.8 7.8 %collective-permute-start.43 = (bf16[4,1,128,128]{3,2,1,0:T(8,128)(2,1)S(1)}, bf16[4,1,128,128]{3,2,1,0:T(8,128)(2,1)S(1)}, u32[]{:S(2)}, u32[]{:S(2)}) collective-permute-start(bf16[4,1,128,128]{3,2,1,0:T(8,128)(2,1)S(1)} %constant_dynamic-update-slice_fusion.16.refs_0_), channel_id=1, source_target_pairs={{0,4},{1,5},{2,6},{3,7},{4,0},{5,1},{6,2},{7,3},{8,12},{9,13},{10,... | collective-permute-start | bytes 393224 | tf_op jit(solution)/shard_map/ppermute | solution.py:146
  91.1 6.4 %collective-permute-start.45 = (bf16[4,1,128,128]{3,2,1,0:T(8,128)(2,1)S(1)}, bf16[4,1,128,128]{3,2,1,0:T(8,128)(2,1)S(1)}, u32[]{:S(2)}, u32[]{:S(2)}) collective-permute-start(bf16[4,1,128,128]{3,2,1,0:T(8,128)(2,1)S(1)} %constant_dynamic-update-slice_fusion.16.refs_0_), channel_id=1, source_target_pairs={{0,6},{1,7},{2,4},{3,5},{4,2},{5,3},{6,0},{7,1},{8,14},{9,15},{10,... | collective-permute-start | bytes 393224 | tf_op jit(solution)/shard_map/ppermute | solution.py:146
  91.9 6.1 %collective-permute-start.40 = (bf16[4,1,128,128]{3,2,1,0:T(8,128)(2,1)S(1)}, bf16[4,1,128,128]{3,2,1,0:T(8,128)(2,1)S(1)}, u32[]{:S(2)}, u32[]{:S(2)}) collective-permute-start(bf16[4,1,128,128]{3,2,1,0:T(8,128)(2,1)S(1)} %constant_dynamic-update-slice_fusion.16.refs_0_), channel_id=1, source_target_pairs={{0,1},{1,0},{2,3},{3,2},{4,5},{5,4},{6,7},{7,6},{8,9},{9,8},{10,11... | collective-permute-start | bytes 393224 | tf_op jit(solution)/shard_map/ppermute | solution.py:146
  101.9 6.1 %collective-permute-start.48 = (bf16[1,2,128,128]{3,2,1,0:T(8,128)(2,1)S(1)}, bf16[1,2,128,128]{3,2,1,0:T(8,128)(2,1)S(1)}, u32[]{:S(2)}, u32[]{:S(2)}) collective-permute-start(bf16[1,2,128,128]{3,2,1,0:T(8,128)(2,1)S(1)} %bitcast.14), channel_id=1, source_target_pairs={{0,16},{1,17},{2,18},{3,19},{4,20},{5,21},{6,22},{7,23},{8,24},{9,... | collective-permute-start | bytes 196616 | tf_op jit(solution)/shard_map/ppermute | solution.py:154
  108.0 6.4 %collective-permute-start.50 = (bf16[2,2,128,128]{3,2,1,0:T(8,128)(2,1)S(1)}, bf16[2,2,128,128]{3,2,1,0:T(8,128)(2,1)S(1)}, u32[]{:S(2)}, u32[]{:S(2)}) collective-permute-start(bf16[2,2,128,128]{3,2,1,0:T(8,128)(2,1)S(1)} %get-tuple-element.79), channel_id=1, source_target_pairs={{0,2},{1,3},{2,0},{3,1},{4,6},{5,7},{6,4},{7,5},{8,10},{9,11},{10,... | collective-permute-start | bytes 393224 | tf_op jit(solution)/shard_map/ppermute | solution.py:146
  108.3 6.2 %collective-permute-start.52 = (bf16[2,2,128,128]{3,2,1,0:T(8,128)(2,1)S(1)}, bf16[2,2,128,128]{3,2,1,0:T(8,128)(2,1)S(1)}, u32[]{:S(2)}, u32[]{:S(2)}) collective-permute-start(bf16[2,2,128,128]{3,2,1,0:T(8,128)(2,1)S(1)} %get-tuple-element.78), channel_id=1, source_target_pairs={{0,4},{1,5},{2,6},{3,7},{4,0},{5,1},{6,2},{7,3},{8,12},{9,13},{10,... | collective-permute-start | bytes 393224 | tf_op jit(solution)/shard_map/ppermute | solution.py:146
  109.5 7.1 %collective-permute-start.54 = (bf16[2,2,128,128]{3,2,1,0:T(8,128)(2,1)S(1)}, bf16[2,2,128,128]{3,2,1,0:T(8,128)(2,1)S(1)}, u32[]{:S(2)}, u32[]{:S(2)}) collective-permute-start(bf16[2,2,128,128]{3,2,1,0:T(8,128)(2,1)S(1)} %get-tuple-element.78), channel_id=1, source_target_pairs={{0,6},{1,7},{2,4},{3,5},{4,2},{5,3},{6,0},{7,1},{8,14},{9,15},{10,... | collective-permute-start | bytes 393224 | tf_op jit(solution)/shard_map/ppermute | solution.py:146
  111.6 5.9 %collective-permute-start.49 = (bf16[2,2,128,128]{3,2,1,0:T(8,128)(2,1)S(1)}, bf16[2,2,128,128]{3,2,1,0:T(8,128)(2,1)S(1)}, u32[]{:S(2)}, u32[]{:S(2)}) collective-permute-start(bf16[2,2,128,128]{3,2,1,0:T(8,128)(2,1)S(1)} %get-tuple-element.80), channel_id=1, source_target_pairs={{0,1},{1,0},{2,3},{3,2},{4,5},{5,4},{6,7},{7,6},{8,9},{9,8},{10,11... | collective-permute-start | bytes 393224 | tf_op jit(solution)/shard_map/ppermute | solution.py:146
  (30 other events, 174.3 us)

commit v5 on v0

--- a/solution.py
+++ b/solution.py
@@ -1,7 +1,492 @@
+import functools
 import jax
 import jax.numpy as jnp
 from jax import lax
+from jax.experimental import pallas as pl
+from jax.experimental.pallas import tpu as pltpu
 from jax.sharding import PartitionSpec as P
+
+SPAN = 16
+PLANE = 8
+PLANES = 4
+VMEM_BYTES = 48 * 1024 * 1024
+
+
+def window_start(block, direction, count):
+    if direction > 0:
+        return jnp.maximum(block - (SPAN - 1), 0)
+    return jnp.minimum(block, count - SPAN)
+
+
+def first_pair(start, parity):
+    return (start + 1 - parity) // 2
+
+
+def start_window(direction, base, rows, row_first, count, factor, out, sems):
+    me = lax.axis_index("prow")
+    half = SPAN // 2
+    copies = []
+    for row in range(rows):
+        block = row * PLANE * PLANES + me
+        start = window_start(block, direction, count)
+        for side in range(2):
+            parity = (me & 1) ^ side
+            pair = first_pair(start, parity)
+            at = row * SPAN + side * half
+            copy = pltpu.make_async_copy(
+                factor.at[pl.ds(base // 2 + pair, half), parity, row_first + row],
+                out.at[pl.ds(at, half)],
+                sems.at[2 * row + side],
+            )
+            copy.start()
+            copies.append((copy, block, pair, side, at))
+    return copies
+
+
+def keep_window(direction, copies, snode, out):
+    me = lax.axis_index("prow")
+    half, size = SPAN // 2, out.shape[1]
+    col = lax.broadcasted_iota(jnp.int32, (size, size), 0)
+    line = lax.broadcasted_iota(jnp.int32, (size, size), 1)
+    tri = line >= col if direction > 0 else line <= col
+    zero = jnp.zeros((size, size), out.dtype)
+    for copy, block, pair, side, at in copies:
+        copy.wait()
+        own = snode[block]
+        for step in range(half):
+            column = 2 * (pair + step) + ((me & 1) ^ side)
+            kept = snode[column] == own
+            kept = kept & (column <= block if direction > 0 else column >= block)
+            out[at + step] = jnp.where(kept, out[at + step], zero)
+        if side == 0:
+            diagonal = at + block // 2 - pair
+            out[diagonal] = jnp.where(tri, out[diagonal], zero)
+
+
+def pack_level_kernel(direction, base, rows, row_first, count, factor, after, rules, out, sems):
+    copies = start_window(direction, base, rows, row_first, count, factor, out, sems)
+    keep_window(direction, copies, rules.at[0 if rows == 2 else 1], out)
+
+
+def pack_up_kernel(factor, after, rules, out, sems):
+    me = lax.axis_index("prow")
+    total = PLANE * PLANES
+    many, size = total // 2, out.shape[1]
+    copies = []
+    for row in range(2):
+        for side in range(2):
+            at = (2 * row + side) * many
+            copy = pltpu.make_async_copy(
+                factor.at[pl.ds(total, many), (me & 1) ^ side, row],
+                out.at[pl.ds(at, many)],
+                sems.at[2 * row + side],
+            )
+            copy.start()
+            copies.append((copy, row, side, at))
+    zero = jnp.zeros((size, size), out.dtype)
+    for copy, row, side, at in copies:
+        child = rules[0, row * total + me]
+        above = rules[2, child]
+        copy.wait()
+        for pair in range(many):
+            block = 2 * pair + ((me & 1) ^ side)
+            linked = (above == rules[1, block]) & (rules[3 + child, block] == 1)
+            out[at + pair] = jnp.where(linked, out[at + pair], zero)
+
+
+def pack_call(kernel, name, blocks, copies, factor, after, rules):
+    size, dtype = factor.shape[-1], factor.dtype
+    return pl.pallas_call(
+        kernel,
+        out_shape=jax.ShapeDtypeStruct((blocks, size, size), dtype),
+        in_specs=[pl.BlockSpec(memory_space=pl.ANY)] * 2
+        + [pl.BlockSpec(memory_space=pltpu.SMEM)],
+        out_specs=pl.BlockSpec(memory_space=pltpu.VMEM),
+        scratch_shapes=[pltpu.SemaphoreType.DMA((copies,))],
+        compiler_params=pltpu.CompilerParams(vmem_limit_bytes=VMEM_BYTES),
+        cost_estimate=pl.CostEstimate(
+            flops=0, bytes_accessed=2 * blocks * size * size * dtype.itemsize, transcendentals=0
+        ),
+        name=name,
+    )(factor, after, rules)
+
+
+def first_pack_kernel(
+    factor, after, rules, mine, even, odd, table, kids, sems
+):
+    me = lax.axis_index("prow")
+    offset, plane = me & (PLANE - 1), me // PLANE
+    total = PLANE * PLANES
+    count, children = 2 * total, rules.shape[0] - 3
+    lower_snode, upper_snode, parent = rules.at[0], rules.at[1], rules.at[2]
+    size = mine.shape[1]
+    windows = start_window(1, 0, 2, 0, count, factor, mine, sems)
+    begins = []
+    for child in range(children):
+        found = jnp.int32(0)
+        for bit in reversed(range(count.bit_length() - 1)):
+            ahead = found + (1 << bit)
+            found = jnp.where(lower_snode[ahead - 1] < child, ahead, found)
+        begins.append(found)
+    parents = [parent[child] for child in range(children)]
+
+    def children_of(above):
+        first, first_at = jnp.int32(0), jnp.int32(0)
+        last, last_at = jnp.int32(0), jnp.int32(0)
+        for child in range(children):
+            match = parents[child] == above
+            last, last_at = jnp.where(match, child, last), jnp.where(match, begins[child], last_at)
+        for child in reversed(range(children)):
+            match = parents[child] == above
+            first, first_at = jnp.where(match, child, first), jnp.where(match, begins[child], first_at)
+        return (first, first_at), (last, last_at)
+
+    def column(start, place, step):
+        return start + ((place - start) & (PLANE - 1)) + step * PLANE
+
+    low, high = children_of(upper_snode[me])
+    copies = []
+    for side, (child, start) in enumerate((low, high)):
+        at = jnp.minimum(start, count - SPAN - 2)
+        copy = pltpu.make_async_copy(
+            factor.at[pl.ds(at // 2, SPAN // 2 + 1), :, 2], kids.at[side], sems.at[4 + side]
+        )
+        copy.start()
+        linked = rules[3 + child, me] == 1
+        if side:
+            linked = linked & (low[0] != high[0])
+        copies.append((copy, child, start, at, linked))
+    for k in range(PLANE):
+        pair = children_of(upper_snode[plane * PLANE + (offset ^ k)])
+        for slot in range(4):
+            found = column(pair[slot // 2][1], offset, slot % 2)
+            table[4 * k + slot] = jnp.minimum(found, count - 1)
+    keep_window(1, windows, lower_snode, mine)
+    zero = jnp.zeros((size, size), mine.dtype)
+    for side, (copy, child, start, at, linked) in enumerate(copies):
+        copy.wait()
+        for k in range(PLANE):
+            for step in range(2):
+                found = column(start, offset ^ k, step)
+                source = jnp.minimum(found, count - 1)
+                kept = linked & (found < count) & (lower_snode[source] == child)
+                out = odd if k % 2 else even
+                near = jnp.minimum(source // 2 - at // 2, SPAN // 2)
+                value = kids[side, near, source % 2]
+                out[4 * (k // 2) + 2 * side + step] = jnp.where(kept, value, zero)
+
+
+def first_pack(factor, after, rules):
+    size, dtype = factor.shape[-1], factor.dtype
+    counts = (2 * SPAN, SPAN, SPAN)
+    vmem, smem = (pl.BlockSpec(memory_space=space) for space in (pltpu.VMEM, pltpu.SMEM))
+    return pl.pallas_call(
+        first_pack_kernel,
+        out_shape=[jax.ShapeDtypeStruct((count, size, size), dtype) for count in counts]
+        + [jax.ShapeDtypeStruct((4 * PLANE,), jnp.int32)],
+        in_specs=[pl.BlockSpec(memory_space=pl.ANY)] * 2 + [smem],
+        out_specs=[vmem] * 3 + [smem],
+        scratch_shapes=[
+            pltpu.VMEM((2, SPAN // 2 + 1, 2, size, size), dtype),
+            pltpu.SemaphoreType.DMA((6,)),
+        ],
+        compiler_params=pltpu.CompilerParams(vmem_limit_bytes=VMEM_BYTES),
+        cost_estimate=pl.CostEstimate(
+            flops=0, bytes_accessed=2 * sum(counts) * size * size * dtype.itemsize, transcendentals=0
+        ),
+        name="first_pack",
+    )(factor, after, rules)
+
+
+def swap(value, distance):
+    return lax.ppermute(value, "prow", [(i, i ^ distance) for i in range(PLANE * PLANES)])
+
+
+def along_z(block, direction):
+    total = PLANE * PLANES
+    parts = [block[None]]
+    if direction == 0:
+        return parts + [swap(block[None], PLANE * step) for step in range(1, PLANES)]
+    for step in (1, 2):
+        pairs = [(i, (i + direction * step * PLANE) % total) for i in range(total)]
+        parts.append(lax.ppermute(block[None], "prow", pairs))
+    return parts
+
+
+def in_plane(parts, direction):
+    stacked = jnp.concatenate(parts, 0)
+    pieces = {0: stacked}
+    if direction == 0:
+        sent = {1: stacked, 2: stacked, 4: stacked}
+    else:
+        near, far = jnp.concatenate(parts[:2], 0), jnp.concatenate(parts[1:], 0)
+        me = lax.axis_index("prow")
+        sent = {}
+        for bit in (1, 2, 4):
+            after = (me & bit) != 0
+            sent[bit] = jnp.where(after if direction > 0 else jnp.logical_not(after), far, near)
+    for k in (2, 4, 6):
+        pieces[k] = swap(sent[2 if k == 2 else 4], k)
+    pieces[1] = swap(sent[1], 1)
+    for k in (2, 4, 6):
+        pieces[k + 1] = swap(pieces[k], 1)
+    return [pieces[k] for k in range(PLANE)]
+
+
+def gather(block, direction, pack):
+    parts = along_z(block, direction)
+    parts, packed = lax.optimization_barrier((parts, pack(block)))
+    return in_plane(parts, direction), packed
+
+
+def copy_window(side, pieces, xs, block, start, direction):
+    me = lax.axis_index("prow")
+    offset, parity = me & (PLANE - 1), (me & 1) ^ side
+    size, lines = xs.shape[0], PLANE // 2
+    pair = first_pair(start, parity)
+    for k, piece in zip(range(side, PLANE, 2), pieces, strict=True):
+        other = offset ^ k
+        first = (other // 2 - pair) & (lines - 1)
+        skipped = jnp.int32(0)
+        if k > 0:
+            skipped = (other > offset if direction > 0 else other < offset).astype(jnp.int32)
+        for half in range(2):
+            slot = first + half * lines
+            source = 2 * (pair + slot) + parity
+            apart = direction * (block // PLANE - source // PLANE)
+            apart = jnp.clip(apart - skipped, 0, piece.shape[0] - 1)
+            level = source // (PLANE * PLANES) if piece.shape[1] > 1 else 0
+            at = pl.multiple_of(slot * size, size)
+            xs[:, pl.ds(at, size)] = piece[apart, level]
+
+
+def dot(left, right):
+    return jnp.dot(left, right, preferred_element_type=jnp.float32)
+
+
+def window_part(side, direction, row, rows, pieces, factor, xs):
+    me = lax.axis_index("prow")
+    size, half = xs.shape[0], SPAN // 2
+    block = row * PLANE * PLANES + me
+    start = window_start(block, direction, rows * PLANE * PLANES)
+    copy_window(side, pieces, xs, block, start, direction)
+    at = row * SPAN + side * half
+    return dot(xs[...], factor[at : at + half].reshape(half * size, size))
+
+
+def window_own_kernel(direction, *refs):
+    pieces, (factor, part, xs) = refs[:4], refs[4:]
+    for row in range(part.shape[0]):
+        part[row] = window_part(0, direction, row, part.shape[0], pieces, factor, xs)
+
+
+def window_other_kernel(direction, *refs):
+    pieces, (factor, part, solved, known, xs) = refs[:4], refs[4:]
+    for row in range(part.shape[0]):
+        other = window_part(1, direction, row, part.shape[0], pieces, factor, xs)
+        result = part[row] + other
+        solved[row] = result
+        known[row] = result.astype(known.dtype)
+
+
+def backward_lower_kernel(*refs):
+    pieces, (factor, part, upper, out, xs) = refs[:4], refs[4:]
+    out[2, 0] = upper[0].T
+    for row in range(2):
+        out[row, 0] = (part[row] + window_part(1, -1, row, 2, pieces, factor, xs)).T
+
+
+def down_kernel(odd, known, own, brought, near, level, far, table, out, xs):
+    me = lax.axis_index("prow")
+    plane = me // PLANE
+    size = xs.shape[0]
+    sources = ((own, 0, brought, 0), (near, 0, near, 4), (level, 0, level, 4), (far, 0, far, 4))
+    for m in range(4):
+        for slot in range(4):
+            block = table[4 * (2 * m + odd) + slot]
+            along = (block // PLANE) % PLANES ^ plane
+            xs[:, slot * size : (slot + 1) * size] = known[along, block // (PLANE * PLANES)]
+        factor, at = sources[m][2 * odd : 2 * odd + 2]
+        out[m] = dot(xs[...], factor[at : at + 4].reshape(4 * size, size))
+
+
+def correction_part(side, row, pieces, factor, xs):
+    me = lax.axis_index("prow")
+    offset, plane = me & (PLANE - 1), me // PLANE
+    size = xs.shape[0]
+    many = xs.shape[1] // size
+    if row == 0:
+        for k, piece in zip(range(side, PLANE, 2), pieces, strict=True):
+            for along in range(PLANES):
+                pair = (plane ^ along) * (PLANE // 2) + (offset ^ k) // 2
+                xs[:, pl.ds(pl.multiple_of(pair * size, size), size)] = piece[along, 0]
+    at = (2 * row + side) * many
+    return dot(xs[...], factor[at : at + many].reshape(many * size, size))
+
+
+def correction_own_kernel(*refs):
+    pieces, (factor, part, xs) = refs[:4], refs[4:]
+    for row in range(2):
+        part[row] = correction_part(0, row, pieces, factor, xs)
+
+
+def correction_kernel(*refs):
+    pieces, (factor, part, solved, out, xs) = refs[:4], refs[4:]
+    for row in range(2):
+        result = part[row] + correction_part(1, row, pieces, factor, xs)
+        known = solved[row].astype(out.dtype).astype(jnp.float32)
+        rounded = result.astype(out.dtype).astype(jnp.float32)
+        out[row] = (known - rounded).astype(out.dtype)
+
+
+def turn_kernel(value, out):
+    for row in range(3):
+        out[row] = value[row, 0].astype(jnp.float32).T.astype(out.dtype)
+
+
+def forward_out_kernel(lower, upper, out):
+    for row in range(2):
+        out[row, 0] = lower[row].T
+    out[2, 0] = upper[0].T
+
+
+def local_call(kernel, name, shapes, operands, width=0, tables=0):
+    size = 128
+    scratch = [pltpu.VMEM((size, width), jnp.bfloat16)] if width else []
+    outs = [jax.ShapeDtypeStruct(*shape) for shape in shapes]
+    return pl.pallas_call(
+        kernel,
+        out_shape=outs,
+        in_specs=[pl.BlockSpec(memory_space=pltpu.VMEM)] * (len(operands) - tables)
+        + [pl.BlockSpec(memory_space=pltpu.SMEM)] * tables,
+        out_specs=[pl.BlockSpec(memory_space=pltpu.VMEM)] * len(outs),
+        scratch_shapes=scratch,
+        compiler_params=pltpu.CompilerParams(vmem_limit_bytes=VMEM_BYTES),
+        cost_estimate=pl.CostEstimate(flops=0, bytes_accessed=1 << 20, transcendentals=0),
+        name=name,
+    )(*operands)
+
+
+def fast_device(rhs, lower_factor_t, upper_factor_t, lower_snode, upper_snode, parent, pattern):
+    rows, _, size, width = rhs.shape
+    total = PLANE * PLANES
+    f32, bf16 = jnp.float32, jnp.bfloat16
+
+    def blocks(factor):
+        return jnp.transpose(factor, (0, 1, 3, 4, 2, 5)).reshape(
+            rows * total // 2, 2, rows, size, size
+        )
+
+    lower, upper = blocks(lower_factor_t), blocks(upper_factor_t)
+
+    def line(values):
+        return jnp.pad(values, ((0, 0), (0, 128 - values.shape[1])))
+
+    rules = jnp.concatenate(
+        [line(lower_snode[None]), line(upper_snode[None]), line(parent.T), line(pattern.T)], 0
+    )
+    own = local_call(turn_kernel, "turn", [((rows, width, size), bf16)], [rhs])[0]
+
+    forward, backward, whole = 1, -1, 0
+    half = SPAN // 2
+
+    def level(factor, direction, count):
+        first, base = (0, 0) if count == 2 else (2, 2 * total)
+        kernel = functools.partial(pack_level_kernel, direction, base, count, first, count * total)
+        return lambda after: pack_call(
+            kernel, "pack_level", count * SPAN, 2 * count, factor, after, rules
+        )
+
+    def pack_up(after):
+        return pack_call(pack_up_kernel, "pack_up", 2 * total, 4, upper, after, rules)
+
+    def window(name, count, direction, pieces, packed):
+        (part,) = local_call(
+            functools.partial(window_own_kernel, direction),
+            name + "_own",
+            [((count, width, size), f32)],
+            [*pieces[0::2], packed],
+            half * size,
+        )
+        return local_call(
+            functools.partial(window_other_kernel, direction),
+            name,
+            [((count, width, size), f32), ((count, width, size), bf16)],
+            [*pieces[1::2], packed, part],
+            half * size,
+        )
+
+    barrier = lax.optimization_barrier
+    rhs_lower = own[:2]
+    parts = along_z(rhs_lower, forward)
+    packed = first_pack(lower, rhs_lower, rules)
+    parts, (l1, even, odd, table) = barrier((parts, packed))
+    pieces = in_plane(parts, forward)
+    brought = swap(odd, 1)
+    even, pieces[6] = barrier((even, pieces[6]))
+    pairs = [
+        jnp.concatenate([even[4 * m : 4 * m + 4], brought[4 * m : 4 * m + 4]], 0) for m in (1, 2, 3)
+    ]
+    down = [swap(pair, 2 * (m + 1)) for m, pair in enumerate(pairs)]
+    solved, known = window("forward_lower", 2, forward, pieces, l1)
+    parts = along_z(known, whole)
+    parts[1], down = barrier((parts[1], down))
+    held = jnp.concatenate(parts, 0)
+    sums = []
+    for group in (1, 0):
+        sums += local_call(
+            functools.partial(down_kernel, group),
+            "coupling_other" if group else "coupling",
+            [((4, width, size), f32)],
+            [held, even, brought, *down, table],
+            4 * size,
+            1,
+        )
+    sums = sums[1] + swap(sums[0], 1)
+    arrived = [swap(sums[m], 2 * m) for m in (1, 2, 3)]
+    coupling = (sums[0] + arrived[0] + arrived[1] + arrived[2]).astype(bf16).astype(f32)
+    difference = (own[2:].astype(f32) - coupling).astype(bf16)
+    pieces, packed = gather(difference, forward, level(lower, forward, 1))
+    forward_upper, upper_known = window("forward_upper", 1, forward, pieces, packed)
+    pieces, packed = gather(upper_known, backward, level(upper, backward, 1))
+    (forward_solution,) = local_call(
+        forward_out_kernel,
+        "forward_out",
+        [((rows, 1, size, width), f32)],
+        [solved, forward_upper],
+    )
+    backward_upper, back_known = window("backward_upper", 1, backward, pieces, packed)
+    pieces, packed = gather(back_known, whole, pack_up)
+    (part,) = local_call(
+        correction_own_kernel,
+        "correction_own",
+        [((2, width, size), f32)],
+        [*pieces[0::2], packed],
+        total // 2 * size,
+    )
+    (remainder,) = local_call(
+        correction_kernel,
+        "correction",
+        [((2, width, size), bf16)],
+        [*pieces[1::2], packed, part, solved],
+        total // 2 * size,
+    )
+    pieces, packed = gather(remainder, backward, level(upper, backward, 2))
+    (part,) = local_call(
+        functools.partial(window_own_kernel, backward),
+        "backward_lower_own",
+        [((2, width, size), f32)],
+        [*pieces[0::2], packed],
+        half * size,
+    )
+    (backward_solution,) = local_call(
+        backward_lower_kernel,
+        "backward_lower",
+        [((rows, 1, size, width), f32)],
+        [*pieces[1::2], packed, part, backward_upper],
+        half * size,
+    )
+    return forward_solution, backward_solution
 
 
 def block_masks(lower_snode, upper_snode, parent, pattern):
@@ -134,8 +619,10 @@
         P("parts", None),
         P("parts", None),
     )
+    total = PLANE * PLANES
+    simple = mesh.shape["prow"] == total and mesh.shape["pcol"] == 1
     return jax.shard_map(
-        on_device,
+        fast_device if simple else on_device,
         mesh=mesh,
         in_specs=placed,
         out_specs=(P("parts", "prow", "pcol", None), P("parts", "prow", "pcol", None)),

time: 402 us -> 115 us (0.29)
  waiting for transfers between devices: 313 us -> 45.8 us
  starting transfers between devices: 0.43 us -> 46.3 us
  matrix products: 39.1 us -> 0 us
  other arithmetic: 21 us -> 1.08 us
  Pallas kernels: 0 us -> 18.7 us
  between operations: 14.3 us -> 1.12 us
  local copies, waits for them, and re-layouts: 13 us -> 1.15 us
    all_gather x6 -> x0, waiting for transfers between devices: 313 us -> none  [apply_factor(): pieces_in = lax.all_gather(vector, 'prow', axis=1, tiled=True)]
    ppermute x0 -> x57, starting transfers between devices: none -> 46.3 us  [the longest x49 34.3 us: swap(): lax.ppermute(value, 'prow', [(i, i ^ distance) for i in range(PLANE * PLA...]
    ppermute x0 -> x57, waiting for transfers between devices: none -> 45.8 us  [the longest x49 38 us: swap(): lax.ppermute(value, 'prow', [(i, i ^ distance) for i in range(PLANE * PLA...]
    dot_general x12 -> x0, matrix products: 39.1 us -> none  [the longest x6 22.2 us: apply_factor(): lax.dot_general(window, picked, (((0, 1, 2), (0, 1, 2)), ((), ())), prefe...]
    pallas_call x0 -> x19, Pallas kernels: none -> 18.7 us  [the longest x14 7.99 us: local_call(): pl.pallas_call(kernel, out_shape=outs, in_specs=[pl.BlockSpec(memory_spac...]
    select_n x1 -> x4, other arithmetic: 14.9 us -> 0.12 us  [in_plane(): jnp.where(after if direction > 0 else jnp.logical_not(after), far, near)]
  transfers between devices with their start and end apart: 6 -> 57, of which waited for: 6 -> 31; matrix products, arithmetic and copies ran while one was open for 6% -> 1% of each run, Pallas kernels for 0% -> 13%
where the time goes in v5:
time: 115 us; the launch traced here: 114 us
  starting transfers between devices  46.3 us (40%)
  waiting for transfers between devices  45.8 us (40%)
  Pallas kernels  18.7 us (16%)
    ppermute x49, waiting for transfers between devices, swap(): lax.ppermute(value, 'prow', [(i, i ^ distance) for i in range(PLANE * PLA...  38 us
    ppermute x49, starting transfers between devices, swap(): lax.ppermute(value, 'prow', [(i, i ^ distance) for i in range(PLANE * PLA...  34.3 us
    ppermute x8, starting transfers between devices, along_z(): parts.append(lax.ppermute(block[None], 'prow', pairs))  12 us
    pallas_call x14, Pallas kernels, local_call(): pl.pallas_call(kernel, out_shape=outs, in_specs=[pl.BlockSpec(memory_spac...  7.99 us
    ppermute x8, waiting for transfers between devices, along_z(): parts.append(lax.ppermute(block[None], 'prow', pairs))  7.78 us
    pallas_call x4, Pallas kernels, pack_call(): pl.pallas_call(kernel, out_shape=jax.ShapeDtypeStruct((blocks, size, size...  7.63 us
    pallas_call x1, Pallas kernels, first_pack(): pl.pallas_call(first_pack_kernel, out_shape=[jax.ShapeDtypeStruct((count,...  3.07 us
  transfers between devices with their start and end apart: 57, of which 31 were waited for; matrix products, arithmetic and copies ran while one was open for 1% of the time, Pallas kernels for 13%

profile of v5, /device:TPU:0, one launch (start us, length us, event | category | flops | bytes accessed | tf_op | source)
XLA Modules:
  0.0 114.2 jit_solution(896107082009851984)
XLA Ops:
  1.7 4.1 %collective-permute-start.1 = (bf16[1,2,128,128]{3,2,1,0:T(8,128)(2,1)S(1)}, bf16[1,2,128,128]{3,2,1,0:T(8,128)(2,1)S(1)}, u32[]{:S(2)}, u32[]{:S(2)}) collective-permute-start(bf16[1,2,128,128]{3,2,1,0:T(8,128)(2,1)S(1)} %get-tuple-element.48), channel_id=1, source_target_pairs={{0,16},{1,17},{2,18},{3,19},{4,20},{5,21},{6,22},{7,23},{8,24},{9,... | collective-permute-start | bytes 196616 | tf_op jit(solution)/shard_map/ppermute | solution.py:212
  5.8 1.6 %collective-permute-start = (bf16[1,2,128,128]{3,2,1,0:T(8,128)(2,1)S(1)}, bf16[1,2,128,128]{3,2,1,0:T(8,128)(2,1)S(1)}, u32[]{:S(2)}, u32[]{:S(2)}) collective-permute-start(bf16[1,2,128,128]{3,2,1,0:T(8,128)(2,1)S(1)} %get-tuple-element.48), channel_id=1, source_target_pairs={{0,8},{1,9},{2,10},{3,11},{4,12},{5,13},{6,14},{7,15},{8,16},{9,17... | collective-permute-start | bytes 196616 | tf_op jit(solution)/shard_map/ppermute | solution.py:212
  8.1 3.1 %first_pack.1 = (bf16[32,128,128]{2,1,0:T(8,128)(2,1)S(1)}, bf16[16,128,128]{2,1,0:T(8,128)(2,1)S(1)}, bf16[16,128,128]{2,1,0:T(8,128)(2,1)S(1)}, s32[32]{0:T(128)S(1)}) custom-call(bf16[48,2,3,128,128]{4,3,2,1,0:T(8,128)(2,1)} %bitcast.65, bf16[2,128,128]{2,1,0:T(8,128)(2,1)S(1)} %get-tuple-element.103.after, s32[8,128]{1,0:T(8,128)S(1)} %pad_add_fusion.rules), custom_call_target="tpu_custom_call" | custom-call | bytes 4194304 | tf_op jit(solution)/shard_map/first_pack/pallas_call | solution.py:183
  11.9 2.5 %collective-permute-start.7 = (bf16[2,2,128,128]{3,2,1,0:T(8,128)(2,1)S(1)}, bf16[2,2,128,128]{3,2,1,0:T(8,128)(2,1)S(1)}, u32[]{:S(2)}, u32[]{:S(2)}) collective-permute-start(bf16[2,2,128,128]{3,2,1,0:T(8,128)(2,1)S(1)} %get-tuple-element.94), channel_id=1, source_target_pairs={{0,6},{1,7},{2,4},{3,5},{4,2},{5,3},{6,0},{7,1},{8,14},{9,15},{10,... | collective-permute-start | bytes 393224 | tf_op jit(solution)/shard_map/ppermute | solution.py:202
  15.5 3.7 %collective-permute-done.7.refs_3_ = bf16[2,2,128,128]{3,2,1,0:T(8,128)(2,1)S(1)} collective-permute-done((bf16[2,2,128,128]{3,2,1,0:T(8,128)(2,1)S(1)}, bf16[2,2,128,128]{3,2,1,0:T(8,128)(2,1)S(1)}, u32[]{:S(2)}, u32[]{:S(2)}) %collective-permute-start.7) | collective-permute-done | bytes 131104 | tf_op jit(solution)/shard_map/ppermute | solution.py:202
  19.2 2.5 %collective-permute-done.3.refs_1_ = bf16[2,2,128,128]{3,2,1,0:T(8,128)(2,1)S(1)} collective-permute-done((bf16[2,2,128,128]{3,2,1,0:T(8,128)(2,1)S(1)}, bf16[2,2,128,128]{3,2,1,0:T(8,128)(2,1)S(1)}, u32[]{:S(2)}, u32[]{:S(2)}) %collective-permute-start.3) | collective-permute-done | bytes 131104 | tf_op jit(solution)/shard_map/ppermute | solution.py:202
  22.3 1.6 %collective-permute-start.11 = (bf16[8,128,128]{2,1,0:T(8,128)(2,1)S(1)}, bf16[8,128,128]{2,1,0:T(8,128)(2,1)S(1)}, u32[]{:S(2)}, u32[]{:S(2)}) collective-permute-start(bf16[8,128,128]{2,1,0:T(8,128)(2,1)S(1)} %pad_maximum_fusion), channel_id=1, source_target_pairs={{0,2},{1,3},{2,0},{3,1},{4,6},{5,7},{6,4},{7,5},{8,10},{9,11},{10,... | collective-permute-start | bytes 786440 | tf_op jit(solution)/shard_map/ppermute | solution.py:202
  27.2 2.9 %collective-permute-start.15 = (bf16[1,2,128,128]{3,2,1,0:T(8,128)(2,1)S(1)}, bf16[1,2,128,128]{3,2,1,0:T(8,128)(2,1)S(1)}, u32[]{:S(2)}, u32[]{:S(2)}) collective-permute-start(bf16[1,2,128,128]{3,2,1,0:T(8,128)(2,1)S(1)} %bitcast.59), channel_id=1, source_target_pairs={{0,24},{1,25},{2,26},{3,27},{4,28},{5,29},{6,30},{7,31},{8,16},{9,... | collective-permute-start | bytes 196616 | tf_op jit(solution)/shard_map/ppermute | solution.py:202
  30.1 2.0 %collective-permute-done.9 = bf16[1,2,128,128]{3,2,1,0:T(8,128)(2,1)S(1)} collective-permute-done((bf16[1,2,128,128]{3,2,1,0:T(8,128)(2,1)S(1)}, bf16[1,2,128,128]{3,2,1,0:T(8,128)(2,1)S(1)}, u32[]{:S(2)}, u32[]{:S(2)}) %collective-permute-start.9) | collective-permute-done | bytes 65568 | tf_op jit(solution)/shard_map/ppermute | solution.py:202
  32.9 4.6 %collective-permute-done.12.level = bf16[8,128,128]{2,1,0:T(8,128)(2,1)S(1)} collective-permute-done((bf16[8,128,128]{2,1,0:T(8,128)(2,1)S(1)}, bf16[8,128,128]{2,1,0:T(8,128)(2,1)S(1)}, u32[]{:S(2)}, u32[]{:S(2)}) %collective-permute-start.12) | collective-permute-done | bytes 262176 | tf_op jit(solution)/shard_map/ppermute | solution.py:202
  41.5 1.6 %collective-permute-start.19 = (f32[128,128]{1,0:T(8,128)S(1)}, f32[128,128]{1,0:T(8,128)S(1)}, u32[]{:S(2)}, u32[]{:S(2)}) collective-permute-start(f32[128,128]{1,0:T(8,128)S(1)} %get-tuple-element.92), channel_id=1, source_target_pairs={{0,6},{1,7},{2,4},{3,5},{4,2},{5,3},{6,0},{7,1},{8,14},{9,15},{10,... | collective-permute-start | bytes 196616 | tf_op jit(solution)/shard_map/ppermute | solution.py:202
  45.0 1.9 %collective-permute-done.19 = f32[128,128]{1,0:T(8,128)S(1)} collective-permute-done((f32[128,128]{1,0:T(8,128)S(1)}, f32[128,128]{1,0:T(8,128)S(1)}, u32[]{:S(2)}, u32[]{:S(2)}) %collective-permute-start.19) | collective-permute-done | bytes 65568 | tf_op jit(solution)/shard_map/ppermute | solution.py:202
  47.9 1.4 %collective-permute-start.21 = (bf16[1,1,128,128]{3,2,1,0:T(8,128)(2,1)S(1)}, bf16[1,1,128,128]{3,2,1,0:T(8,128)(2,1)S(1)}, u32[]{:S(2)}, u32[]{:S(2)}) collective-permute-start(bf16[1,1,128,128]{3,2,1,0:T(8,128)(2,1)S(1)} %bitcast.46), channel_id=1, source_target_pairs={{0,16},{1,17},{2,18},{3,19},{4,20},{5,21},{6,22},{7,23},{8,24},{9,... | collective-permute-start | bytes 98312 | tf_op jit(solution)/shard_map/ppermute | solution.py:212
  50.1 1.7 %pack_level.3.refs_4_ = bf16[16,128,128]{2,1,0:T(8,128)(2,1)S(1)} custom-call(bf16[48,2,3,128,128]{4,3,2,1,0:T(8,128)(2,1)} %bitcast.66, bf16[1,128,128]{2,1,0:T(8,128)(2,1)S(1)} %fusion.4.after, s32[8,128]{1,0:T(8,128)S(1)} %pad_add_fusion.rules), custom_call_target="tpu_custom_call" | custom-call | bytes 1048576 | tf_op jit(solution)/shard_map/pack_level/pallas_call | solution.py:99
  52.8 2.2 %collective-permute-done.20 = bf16[1,1,128,128]{3,2,1,0:T(8,128)(2,1)S(1)} collective-permute-done((bf16[1,1,128,128]{3,2,1,0:T(8,128)(2,1)S(1)}, bf16[1,1,128,128]{3,2,1,0:T(8,128)(2,1)S(1)}, u32[]{:S(2)}, u32[]{:S(2)}) %collective-permute-start.20) | collective-permute-done | bytes 32800 | tf_op jit(solution)/shard_map/ppermute | solution.py:212
  56.0 1.5 %collective-permute-start.27 = (bf16[2,1,128,128]{3,2,1,0:T(8,128)(2,1)S(1)}, bf16[2,1,128,128]{3,2,1,0:T(8,128)(2,1)S(1)}, u32[]{:S(2)}, u32[]{:S(2)}) collective-permute-start(bf16[2,1,128,128]{3,2,1,0:T(8,128)(2,1)S(1)} %get-tuple-element.100), channel_id=1, source_target_pairs={{0,6},{1,7},{2,4},{3,5},{4,2},{5,3},{6,0},{7,1},{8,14},{9,15},{10,... | collective-permute-start | bytes 196616 | tf_op jit(solution)/shard_map/ppermute | solution.py:202
  59.4 1.7 %collective-permute-done.27.refs_3_ = bf16[2,1,128,128]{3,2,1,0:T(8,128)(2,1)S(1)} collective-permute-done((bf16[2,1,128,128]{3,2,1,0:T(8,128)(2,1)S(1)}, bf16[2,1,128,128]{3,2,1,0:T(8,128)(2,1)S(1)}, u32[]{:S(2)}, u32[]{:S(2)}) %collective-permute-start.27) | collective-permute-done | bytes 65568 | tf_op jit(solution)/shard_map/ppermute | solution.py:202
  64.8 1.7 %pack_level.4.refs_4_ = bf16[16,128,128]{2,1,0:T(8,128)(2,1)S(1)} custom-call(bf16[48,2,3,128,128]{4,3,2,1,0:T(8,128)(2,1)} %bitcast.62, bf16[1,128,128]{2,1,0:T(8,128)(2,1)S(1)} %get-tuple-element.66.after, s32[8,128]{1,0:T(8,128)S(1)} %pad_add_fusion.rules), custom_call_target="tpu_custom_call" | custom-call | bytes 1048576 | tf_op jit(solution)/shard_map/pack_level/pallas_call | solution.py:99
  66.5 1.8 %collective-permute-done.30 = bf16[1,1,128,128]{3,2,1,0:T(8,128)(2,1)S(1)} collective-permute-done((bf16[1,1,128,128]{3,2,1,0:T(8,128)(2,1)S(1)}, bf16[1,1,128,128]{3,2,1,0:T(8,128)(2,1)S(1)}, u32[]{:S(2)}, u32[]{:S(2)}) %collective-permute-start.30) | collective-permute-done | bytes 32800 | tf_op jit(solution)/shard_map/ppermute | solution.py:212
  69.6 1.4 %collective-permute-start.36 = (bf16[2,1,128,128]{3,2,1,0:T(8,128)(2,1)S(1)}, bf16[2,1,128,128]{3,2,1,0:T(8,128)(2,1)S(1)}, u32[]{:S(2)}, u32[]{:S(2)}) collective-permute-start(bf16[2,1,128,128]{3,2,1,0:T(8,128)(2,1)S(1)} %get-tuple-element.97), channel_id=1, source_target_pairs={{0,6},{1,7},{2,4},{3,5},{4,2},{5,3},{6,0},{7,1},{8,14},{9,15},{10,... | collective-permute-start | bytes 196616 | tf_op jit(solution)/shard_map/ppermute | solution.py:202
  72.7 2.1 %collective-permute-done.36.refs_3_ = bf16[2,1,128,128]{3,2,1,0:T(8,128)(2,1)S(1)} collective-permute-done((bf16[2,1,128,128]{3,2,1,0:T(8,128)(2,1)S(1)}, bf16[2,1,128,128]{3,2,1,0:T(8,128)(2,1)S(1)}, u32[]{:S(2)}, u32[]{:S(2)}) %collective-permute-start.36) | collective-permute-done | bytes 65568 | tf_op jit(solution)/shard_map/ppermute | solution.py:202
  77.1 2.3 %collective-permute-start.40 = (bf16[1,1,128,128]{3,2,1,0:T(8,128)(2,1)S(1)}, bf16[1,1,128,128]{3,2,1,0:T(8,128)(2,1)S(1)}, u32[]{:S(2)}, u32[]{:S(2)}) collective-permute-start(bf16[1,1,128,128]{3,2,1,0:T(8,128)(2,1)S(1)} %bitcast.54), channel_id=1, source_target_pairs={{0,24},{1,25},{2,26},{3,27},{4,28},{5,29},{6,30},{7,31},{8,16},{9,... | collective-permute-start | bytes 98312 | tf_op jit(solution)/shard_map/ppermute | solution.py:202
  79.5 2.0 %collective-permute-start.38 = (bf16[1,1,128,128]{3,2,1,0:T(8,128)(2,1)S(1)}, bf16[1,1,128,128]{3,2,1,0:T(8,128)(2,1)S(1)}, u32[]{:S(2)}, u32[]{:S(2)}) collective-permute-start(bf16[1,1,128,128]{3,2,1,0:T(8,128)(2,1)S(1)} %bitcast.56), channel_id=1, source_target_pairs={{0,8},{1,9},{2,10},{3,11},{4,12},{5,13},{6,14},{7,15},{8,0},{9,1},... | collective-permute-start | bytes 98312 | tf_op jit(solution)/shard_map/ppermute | solution.py:202
  81.5 2.3 %pack_up.1.refs_4_ = bf16[64,128,128]{2,1,0:T(8,128)(2,1)S(1)} custom-call(bf16[48,2,3,128,128]{4,3,2,1,0:T(8,128)(2,1)} %bitcast.63, bf16[1,128,128]{2,1,0:T(8,128)(2,1)S(1)} %get-tuple-element.71.after, s32[8,128]{1,0:T(8,128)S(1)} %pad_add_fusion.rules), custom_call_target="tpu_custom_call" | custom-call | bytes 4194304 | tf_op jit(solution)/shard_map/pack_up/pallas_call | solution.py:99
  84.4 1.5 %collective-permute-start.46 = (bf16[4,1,128,128]{3,2,1,0:T(8,128)(2,1)S(1)}, bf16[4,1,128,128]{3,2,1,0:T(8,128)(2,1)S(1)}, u32[]{:S(2)}, u32[]{:S(2)}) collective-permute-start(bf16[4,1,128,128]{3,2,1,0:T(8,128)(2,1)S(1)} %constant_dynamic-update-slice_fusion.12.refs_0_), channel_id=1, source_target_pairs={{0,6},{1,7},{2,4},{3,5},{4,2},{5,3},{6,0},{7,1},{8,14},{9,15},{10,... | collective-permute-start | bytes 393224 | tf_op jit(solution)/shard_map/ppermute | solution.py:202
  87.9 3.4 %collective-permute-done.46.refs_3_ = bf16[4,1,128,128]{3,2,1,0:T(8,128)(2,1)S(1)} collective-permute-done((bf16[4,1,128,128]{3,2,1,0:T(8,128)(2,1)S(1)}, bf16[4,1,128,128]{3,2,1,0:T(8,128)(2,1)S(1)}, u32[]{:S(2)}, u32[]{:S(2)}) %collective-permute-start.46) | collective-permute-done | bytes 131104 | tf_op jit(solution)/shard_map/ppermute | solution.py:202
  96.1 1.5 %collective-permute-start.48 = (bf16[1,2,128,128]{3,2,1,0:T(8,128)(2,1)S(1)}, bf16[1,2,128,128]{3,2,1,0:T(8,128)(2,1)S(1)}, u32[]{:S(2)}, u32[]{:S(2)}) collective-permute-start(bf16[1,2,128,128]{3,2,1,0:T(8,128)(2,1)S(1)} %bitcast.43), channel_id=1, source_target_pairs={{0,24},{1,25},{2,26},{3,27},{4,28},{5,29},{6,30},{7,31},{8,0},{9,1... | collective-permute-start | bytes 196616 | tf_op jit(solution)/shard_map/ppermute | solution.py:212
  97.7 1.9 %pack_level.5.refs_4_ = bf16[32,128,128]{2,1,0:T(8,128)(2,1)S(1)} custom-call(bf16[48,2,3,128,128]{4,3,2,1,0:T(8,128)(2,1)} %bitcast.64, bf16[2,128,128]{2,1,0:T(8,128)(2,1)S(1)} %correction.1.after, s32[8,128]{1,0:T(8,128)S(1)} %pad_add_fusion.rules), custom_call_target="tpu_custom_call" | custom-call | bytes 2097152 | tf_op jit(solution)/shard_map/pack_level/pallas_call | solution.py:99
  99.6 2.1 %collective-permute-done.49 = bf16[1,2,128,128]{3,2,1,0:T(8,128)(2,1)S(1)} collective-permute-done((bf16[1,2,128,128]{3,2,1,0:T(8,128)(2,1)S(1)}, bf16[1,2,128,128]{3,2,1,0:T(8,128)(2,1)S(1)}, u32[]{:S(2)}, u32[]{:S(2)}) %collective-permute-start.49) | collective-permute-done | bytes 65568 | tf_op jit(solution)/shard_map/ppermute | solution.py:212
  102.6 1.5 %collective-permute-start.55 = (bf16[2,2,128,128]{3,2,1,0:T(8,128)(2,1)S(1)}, bf16[2,2,128,128]{3,2,1,0:T(8,128)(2,1)S(1)}, u32[]{:S(2)}, u32[]{:S(2)}) collective-permute-start(bf16[2,2,128,128]{3,2,1,0:T(8,128)(2,1)S(1)} %get-tuple-element.88), channel_id=1, source_target_pairs={{0,6},{1,7},{2,4},{3,5},{4,2},{5,3},{6,0},{7,1},{8,14},{9,15},{10,... | collective-permute-start | bytes 393224 | tf_op jit(solution)/shard_map/ppermute | solution.py:202
  105.3 2.9 %collective-permute-done.51.refs_1_ = bf16[2,2,128,128]{3,2,1,0:T(8,128)(2,1)S(1)} collective-permute-done((bf16[2,2,128,128]{3,2,1,0:T(8,128)(2,1)S(1)}, bf16[2,2,128,128]{3,2,1,0:T(8,128)(2,1)S(1)}, u32[]{:S(2)}, u32[]{:S(2)}) %collective-permute-start.51) | collective-permute-done | bytes 131104 | tf_op jit(solution)/shard_map/ppermute | solution.py:202
  108.2 1.9 %collective-permute-done.55.refs_3_ = bf16[2,2,128,128]{3,2,1,0:T(8,128)(2,1)S(1)} collective-permute-done((bf16[2,2,128,128]{3,2,1,0:T(8,128)(2,1)S(1)}, bf16[2,2,128,128]{3,2,1,0:T(8,128)(2,1)S(1)}, u32[]{:S(2)}, u32[]{:S(2)}) %collective-permute-start.55) | collective-permute-done | bytes 131104 | tf_op jit(solution)/shard_map/ppermute | solution.py:202
  (138 shorter events, 42.0 us)
Async XLA Ops:
  1.7 9.5 %collective-permute-start.1 = (bf16[1,2,128,128]{3,2,1,0:T(8,128)(2,1)S(1)}, bf16[1,2,128,128]{3,2,1,0:T(8,128)(2,1)S(1)}, u32[]{:S(2)}, u32[]{:S(2)}) collective-permute-start(bf16[1,2,128,128]{3,2,1,0:T(8,128)(2,1)S(1)} %get-tuple-element.48), channel_id=1, source_target_pairs={{0,16},{1,17},{2,18},{3,19},{4,20},{5,21},{6,22},{7,23},{8,24},{9,... | collective-permute-start | bytes 196616 | tf_op jit(solution)/shard_map/ppermute | solution.py:212
  5.8 6.1 %collective-permute-start = (bf16[1,2,128,128]{3,2,1,0:T(8,128)(2,1)S(1)}, bf16[1,2,128,128]{3,2,1,0:T(8,128)(2,1)S(1)}, u32[]{:S(2)}, u32[]{:S(2)}) collective-permute-start(bf16[1,2,128,128]{3,2,1,0:T(8,128)(2,1)S(1)} %get-tuple-element.48), channel_id=1, source_target_pairs={{0,8},{1,9},{2,10},{3,11},{4,12},{5,13},{6,14},{7,15},{8,16},{9,17... | collective-permute-start | bytes 196616 | tf_op jit(solution)/shard_map/ppermute | solution.py:212
  11.8 10.4 %collective-permute-start.10 = (bf16[16,128,128]{2,1,0:T(8,128)(2,1)S(1)}, bf16[16,128,128]{2,1,0:T(8,128)(2,1)S(1)}, u32[]{:S(2)}, u32[]{:S(2)}) collective-permute-start(bf16[16,128,128]{2,1,0:T(8,128)(2,1)S(1)} %get-tuple-element.55), channel_id=1, source_target_pairs={{0,1},{1,0},{2,3},{3,2},{4,5},{5,4},{6,7},{7,6},{8,9},{9,8},{10,11... | collective-permute-start | bytes 1572872 | tf_op jit(solution)/shard_map/ppermute | solution.py:202
  11.9 7.3 %collective-permute-start.7 = (bf16[2,2,128,128]{3,2,1,0:T(8,128)(2,1)S(1)}, bf16[2,2,128,128]{3,2,1,0:T(8,128)(2,1)S(1)}, u32[]{:S(2)}, u32[]{:S(2)}) collective-permute-start(bf16[2,2,128,128]{3,2,1,0:T(8,128)(2,1)S(1)} %get-tuple-element.94), channel_id=1, source_target_pairs={{0,6},{1,7},{2,4},{3,5},{4,2},{5,3},{6,0},{7,1},{8,14},{9,15},{10,... | collective-permute-start | bytes 393224 | tf_op jit(solution)/shard_map/ppermute | solution.py:202
  14.4 7.3 %collective-permute-start.3 = (bf16[2,2,128,128]{3,2,1,0:T(8,128)(2,1)S(1)}, bf16[2,2,128,128]{3,2,1,0:T(8,128)(2,1)S(1)}, u32[]{:S(2)}, u32[]{:S(2)}) collective-permute-start(bf16[2,2,128,128]{3,2,1,0:T(8,128)(2,1)S(1)} %get-tuple-element.95), channel_id=1, source_target_pairs={{0,2},{1,3},{2,0},{3,1},{4,6},{5,7},{6,4},{7,5},{8,10},{9,11},{10,... | collective-permute-start | bytes 393224 | tf_op jit(solution)/shard_map/ppermute | solution.py:202
  15.0 6.7 %collective-permute-start.5 = (bf16[2,2,128,128]{3,2,1,0:T(8,128)(2,1)S(1)}, bf16[2,2,128,128]{3,2,1,0:T(8,128)(2,1)S(1)}, u32[]{:S(2)}, u32[]{:S(2)}) collective-permute-start(bf16[2,2,128,128]{3,2,1,0:T(8,128)(2,1)S(1)} %get-tuple-element.94), channel_id=1, source_target_pairs={{0,4},{1,5},{2,6},{3,7},{4,0},{5,1},{6,2},{7,3},{8,12},{9,13},{10,... | collective-permute-start | bytes 393224 | tf_op jit(solution)/shard_map/ppermute | solution.py:202
  15.5 8.5 %collective-permute-start.2 = (bf16[2,2,128,128]{3,2,1,0:T(8,128)(2,1)S(1)}, bf16[2,2,128,128]{3,2,1,0:T(8,128)(2,1)S(1)}, u32[]{:S(2)}, u32[]{:S(2)}) collective-permute-start(bf16[2,2,128,128]{3,2,1,0:T(8,128)(2,1)S(1)} %get-tuple-element.96), channel_id=1, source_target_pairs={{0,1},{1,0},{2,3},{3,2},{4,5},{5,4},{6,7},{7,6},{8,9},{9,8},{10,11... | collective-permute-start | bytes 393224 | tf_op jit(solution)/shard_map/ppermute | solution.py:202
  19.2 7.4 %collective-permute-start.8 = (bf16[2,2,128,128]{3,2,1,0:T(8,128)(2,1)S(1)}, bf16[2,2,128,128]{3,2,1,0:T(8,128)(2,1)S(1)}, u32[]{:S(2)}, u32[]{:S(2)}) collective-permute-start(bf16[2,2,128,128]{3,2,1,0:T(8,128)(2,1)S(1)} %collective-permute-done.7.refs_3_), channel_id=1, source_target_pairs={{0,1},{1,0},{2,3},{3,2},{4,5},{5,4},{6,7},{7,6},{8,9},{9,8},{10,11... | collective-permute-start | bytes 393224 | tf_op jit(solution)/shard_map/ppermute | solution.py:202
  21.7 4.9 %collective-permute-start.6 = (bf16[2,2,128,128]{3,2,1,0:T(8,128)(2,1)S(1)}, bf16[2,2,128,128]{3,2,1,0:T(8,128)(2,1)S(1)}, u32[]{:S(2)}, u32[]{:S(2)}) collective-permute-start(bf16[2,2,128,128]{3,2,1,0:T(8,128)(2,1)S(1)} %collective-permute-done.5.refs_2_), channel_id=1, source_target_pairs={{0,1},{1,0},{2,3},{3,2},{4,5},{5,4},{6,7},{7,6},{8,9},{9,8},{10,11... | collective-permute-start | bytes 393224 | tf_op jit(solution)/shard_map/ppermute | solution.py:202
  22.3 10.6 %collective-permute-start.11 = (bf16[8,128,128]{2,1,0:T(8,128)(2,1)S(1)}, bf16[8,128,128]{2,1,0:T(8,128)(2,1)S(1)}, u32[]{:S(2)}, u32[]{:S(2)}) collective-permute-start(bf16[8,128,128]{2,1,0:T(8,128)(2,1)S(1)} %pad_maximum_fusion), channel_id=1, source_target_pairs={{0,2},{1,3},{2,0},{3,1},{4,6},{5,7},{6,4},{7,5},{8,10},{9,11},{10,... | collective-permute-start | bytes 786440 | tf_op jit(solution)/shard_map/ppermute | solution.py:202
  24.0 13.6 %collective-permute-start.12 = (bf16[8,128,128]{2,1,0:T(8,128)(2,1)S(1)}, bf16[8,128,128]{2,1,0:T(8,128)(2,1)S(1)}, u32[]{:S(2)}, u32[]{:S(2)}) collective-permute-start(bf16[8,128,128]{2,1,0:T(8,128)(2,1)S(1)} %pad_maximum_fusion.1), channel_id=1, source_target_pairs={{0,4},{1,5},{2,6},{3,7},{4,0},{5,1},{6,2},{7,3},{8,12},{9,13},{10,... | collective-permute-start | bytes 786440 | tf_op jit(solution)/shard_map/ppermute | solution.py:202
  24.9 12.6 %collective-permute-start.13 = (bf16[8,128,128]{2,1,0:T(8,128)(2,1)S(1)}, bf16[8,128,128]{2,1,0:T(8,128)(2,1)S(1)}, u32[]{:S(2)}, u32[]{:S(2)}) collective-permute-start(bf16[8,128,128]{2,1,0:T(8,128)(2,1)S(1)} %pad_maximum_fusion.2), channel_id=1, source_target_pairs={{0,6},{1,7},{2,4},{3,5},{4,2},{5,3},{6,0},{7,1},{8,14},{9,15},{10,... | collective-permute-start | bytes 786440 | tf_op jit(solution)/shard_map/ppermute | solution.py:202
  27.1 5.0 %collective-permute-start.9 = (bf16[1,2,128,128]{3,2,1,0:T(8,128)(2,1)S(1)}, bf16[1,2,128,128]{3,2,1,0:T(8,128)(2,1)S(1)}, u32[]{:S(2)}, u32[]{:S(2)}) collective-permute-start(bf16[1,2,128,128]{3,2,1,0:T(8,128)(2,1)S(1)} %bitcast.58), channel_id=1, source_target_pairs={{0,8},{1,9},{2,10},{3,11},{4,12},{5,13},{6,14},{7,15},{8,0},{9,1},... | collective-permute-start | bytes 196616 | tf_op jit(solution)/shard_map/ppermute | solution.py:202
  27.2 10.4 %collective-permute-start.15 = (bf16[1,2,128,128]{3,2,1,0:T(8,128)(2,1)S(1)}, bf16[1,2,128,128]{3,2,1,0:T(8,128)(2,1)S(1)}, u32[]{:S(2)}, u32[]{:S(2)}) collective-permute-start(bf16[1,2,128,128]{3,2,1,0:T(8,128)(2,1)S(1)} %bitcast.59), channel_id=1, source_target_pairs={{0,24},{1,25},{2,26},{3,27},{4,28},{5,29},{6,30},{7,31},{8,16},{9,... | collective-permute-start | bytes 196616 | tf_op jit(solution)/shard_map/ppermute | solution.py:202
  32.2 5.4 %collective-permute-start.14 = (bf16[1,2,128,128]{3,2,1,0:T(8,128)(2,1)S(1)}, bf16[1,2,128,128]{3,2,1,0:T(8,128)(2,1)S(1)}, u32[]{:S(2)}, u32[]{:S(2)}) collective-permute-start(bf16[1,2,128,128]{3,2,1,0:T(8,128)(2,1)S(1)} %bitcast.60), channel_id=1, source_target_pairs={{0,16},{1,17},{2,18},{3,19},{4,20},{5,21},{6,22},{7,23},{8,24},{9,... | collective-permute-start | bytes 196616 | tf_op jit(solution)/shard_map/ppermute | solution.py:202
  41.5 5.4 %collective-permute-start.19 = (f32[128,128]{1,0:T(8,128)S(1)}, f32[128,128]{1,0:T(8,128)S(1)}, u32[]{:S(2)}, u32[]{:S(2)}) collective-permute-start(f32[128,128]{1,0:T(8,128)S(1)} %get-tuple-element.92), channel_id=1, source_target_pairs={{0,6},{1,7},{2,4},{3,5},{4,2},{5,3},{6,0},{7,1},{8,14},{9,15},{10,... | collective-permute-start | bytes 196616 | tf_op jit(solution)/shard_map/ppermute | solution.py:202
  49.3 5.7 %collective-permute-start.20 = (bf16[1,1,128,128]{3,2,1,0:T(8,128)(2,1)S(1)}, bf16[1,1,128,128]{3,2,1,0:T(8,128)(2,1)S(1)}, u32[]{:S(2)}, u32[]{:S(2)}) collective-permute-start(bf16[1,1,128,128]{3,2,1,0:T(8,128)(2,1)S(1)} %bitcast.47), channel_id=1, source_target_pairs={{0,8},{1,9},{2,10},{3,11},{4,12},{5,13},{6,14},{7,15},{8,16},{9,17... | collective-permute-start | bytes 98312 | tf_op jit(solution)/shard_map/ppermute | solution.py:212
  56.0 5.2 %collective-permute-start.27 = (bf16[2,1,128,128]{3,2,1,0:T(8,128)(2,1)S(1)}, bf16[2,1,128,128]{3,2,1,0:T(8,128)(2,1)S(1)}, u32[]{:S(2)}, u32[]{:S(2)}) collective-permute-start(bf16[2,1,128,128]{3,2,1,0:T(8,128)(2,1)S(1)} %get-tuple-element.100), channel_id=1, source_target_pairs={{0,6},{1,7},{2,4},{3,5},{4,2},{5,3},{6,0},{7,1},{8,14},{9,15},{10,... | collective-permute-start | bytes 196616 | tf_op jit(solution)/shard_map/ppermute | solution.py:202
  63.4 4.9 %collective-permute-start.30 = (bf16[1,1,128,128]{3,2,1,0:T(8,128)(2,1)S(1)}, bf16[1,1,128,128]{3,2,1,0:T(8,128)(2,1)S(1)}, u32[]{:S(2)}, u32[]{:S(2)}) collective-permute-start(bf16[1,1,128,128]{3,2,1,0:T(8,128)(2,1)S(1)} %bitcast.50), channel_id=1, source_target_pairs={{0,16},{1,17},{2,18},{3,19},{4,20},{5,21},{6,22},{7,23},{8,24},{9,... | collective-permute-start | bytes 98312 | tf_op jit(solution)/shard_map/ppermute | solution.py:212
  69.6 5.2 %collective-permute-start.36 = (bf16[2,1,128,128]{3,2,1,0:T(8,128)(2,1)S(1)}, bf16[2,1,128,128]{3,2,1,0:T(8,128)(2,1)S(1)}, u32[]{:S(2)}, u32[]{:S(2)}) collective-permute-start(bf16[2,1,128,128]{3,2,1,0:T(8,128)(2,1)S(1)} %get-tuple-element.97), channel_id=1, source_target_pairs={{0,6},{1,7},{2,4},{3,5},{4,2},{5,3},{6,0},{7,1},{8,14},{9,15},{10,... | collective-permute-start | bytes 196616 | tf_op jit(solution)/shard_map/ppermute | solution.py:202
  77.1 6.8 %collective-permute-start.40 = (bf16[1,1,128,128]{3,2,1,0:T(8,128)(2,1)S(1)}, bf16[1,1,128,128]{3,2,1,0:T(8,128)(2,1)S(1)}, u32[]{:S(2)}, u32[]{:S(2)}) collective-permute-start(bf16[1,1,128,128]{3,2,1,0:T(8,128)(2,1)S(1)} %bitcast.54), channel_id=1, source_target_pairs={{0,24},{1,25},{2,26},{3,27},{4,28},{5,29},{6,30},{7,31},{8,16},{9,... | collective-permute-start | bytes 98312 | tf_op jit(solution)/shard_map/ppermute | solution.py:202
  79.3 5.0 %collective-permute-start.39 = (bf16[1,1,128,128]{3,2,1,0:T(8,128)(2,1)S(1)}, bf16[1,1,128,128]{3,2,1,0:T(8,128)(2,1)S(1)}, u32[]{:S(2)}, u32[]{:S(2)}) collective-permute-start(bf16[1,1,128,128]{3,2,1,0:T(8,128)(2,1)S(1)} %bitcast.55), channel_id=1, source_target_pairs={{0,16},{1,17},{2,18},{3,19},{4,20},{5,21},{6,22},{7,23},{8,24},{9,... | collective-permute-start | bytes 98312 | tf_op jit(solution)/shard_map/ppermute | solution.py:202
  84.4 6.9 %collective-permute-start.46 = (bf16[4,1,128,128]{3,2,1,0:T(8,128)(2,1)S(1)}, bf16[4,1,128,128]{3,2,1,0:T(8,128)(2,1)S(1)}, u32[]{:S(2)}, u32[]{:S(2)}) collective-permute-start(bf16[4,1,128,128]{3,2,1,0:T(8,128)(2,1)S(1)} %constant_dynamic-update-slice_fusion.12.refs_0_), channel_id=1, source_target_pairs={{0,6},{1,7},{2,4},{3,5},{4,2},{5,3},{6,0},{7,1},{8,14},{9,15},{10,... | collective-permute-start | bytes 393224 | tf_op jit(solution)/shard_map/ppermute | solution.py:202
  85.9 6.8 %collective-permute-start.44 = (bf16[4,1,128,128]{3,2,1,0:T(8,128)(2,1)S(1)}, bf16[4,1,128,128]{3,2,1,0:T(8,128)(2,1)S(1)}, u32[]{:S(2)}, u32[]{:S(2)}) collective-permute-start(bf16[4,1,128,128]{3,2,1,0:T(8,128)(2,1)S(1)} %constant_dynamic-update-slice_fusion.12.refs_0_), channel_id=1, source_target_pairs={{0,4},{1,5},{2,6},{3,7},{4,0},{5,1},{6,2},{7,3},{8,12},{9,13},{10,... | collective-permute-start | bytes 393224 | tf_op jit(solution)/shard_map/ppermute | solution.py:202
  86.7 6.0 %collective-permute-start.42 = (bf16[4,1,128,128]{3,2,1,0:T(8,128)(2,1)S(1)}, bf16[4,1,128,128]{3,2,1,0:T(8,128)(2,1)S(1)}, u32[]{:S(2)}, u32[]{:S(2)}) collective-permute-start(bf16[4,1,128,128]{3,2,1,0:T(8,128)(2,1)S(1)} %constant_dynamic-update-slice_fusion.12.refs_0_), channel_id=1, source_target_pairs={{0,2},{1,3},{2,0},{3,1},{4,6},{5,7},{6,4},{7,5},{8,10},{9,11},{10,... | collective-permute-start | bytes 393224 | tf_op jit(solution)/shard_map/ppermute | solution.py:202
  87.9 5.8 %collective-permute-start.41 = (bf16[4,1,128,128]{3,2,1,0:T(8,128)(2,1)S(1)}, bf16[4,1,128,128]{3,2,1,0:T(8,128)(2,1)S(1)}, u32[]{:S(2)}, u32[]{:S(2)}) collective-permute-start(bf16[4,1,128,128]{3,2,1,0:T(8,128)(2,1)S(1)} %constant_dynamic-update-slice_fusion.12.refs_0_), channel_id=1, source_target_pairs={{0,1},{1,0},{2,3},{3,2},{4,5},{5,4},{6,7},{7,6},{8,9},{9,8},{10,11... | collective-permute-start | bytes 393224 | tf_op jit(solution)/shard_map/ppermute | solution.py:202
  94.8 6.9 %collective-permute-start.49 = (bf16[1,2,128,128]{3,2,1,0:T(8,128)(2,1)S(1)}, bf16[1,2,128,128]{3,2,1,0:T(8,128)(2,1)S(1)}, u32[]{:S(2)}, u32[]{:S(2)}) collective-permute-start(bf16[1,2,128,128]{3,2,1,0:T(8,128)(2,1)S(1)} %bitcast.42), channel_id=1, source_target_pairs={{0,16},{1,17},{2,18},{3,19},{4,20},{5,21},{6,22},{7,23},{8,24},{9,... | collective-permute-start | bytes 196616 | tf_op jit(solution)/shard_map/ppermute | solution.py:212
  96.1 5.5 %collective-permute-start.48 = (bf16[1,2,128,128]{3,2,1,0:T(8,128)(2,1)S(1)}, bf16[1,2,128,128]{3,2,1,0:T(8,128)(2,1)S(1)}, u32[]{:S(2)}, u32[]{:S(2)}) collective-permute-start(bf16[1,2,128,128]{3,2,1,0:T(8,128)(2,1)S(1)} %bitcast.43), channel_id=1, source_target_pairs={{0,24},{1,25},{2,26},{3,27},{4,28},{5,29},{6,30},{7,31},{8,0},{9,1... | collective-permute-start | bytes 196616 | tf_op jit(solution)/shard_map/ppermute | solution.py:212
  101.7 6.5 %collective-permute-start.51 = (bf16[2,2,128,128]{3,2,1,0:T(8,128)(2,1)S(1)}, bf16[2,2,128,128]{3,2,1,0:T(8,128)(2,1)S(1)}, u32[]{:S(2)}, u32[]{:S(2)}) collective-permute-start(bf16[2,2,128,128]{3,2,1,0:T(8,128)(2,1)S(1)} %get-tuple-element.89), channel_id=1, source_target_pairs={{0,2},{1,3},{2,0},{3,1},{4,6},{5,7},{6,4},{7,5},{8,10},{9,11},{10,... | collective-permute-start | bytes 393224 | tf_op jit(solution)/shard_map/ppermute | solution.py:202
  102.6 7.5 %collective-permute-start.55 = (bf16[2,2,128,128]{3,2,1,0:T(8,128)(2,1)S(1)}, bf16[2,2,128,128]{3,2,1,0:T(8,128)(2,1)S(1)}, u32[]{:S(2)}, u32[]{:S(2)}) collective-permute-start(bf16[2,2,128,128]{3,2,1,0:T(8,128)(2,1)S(1)} %get-tuple-element.88), channel_id=1, source_target_pairs={{0,6},{1,7},{2,4},{3,5},{4,2},{5,3},{6,0},{7,1},{8,14},{9,15},{10,... | collective-permute-start | bytes 393224 | tf_op jit(solution)/shard_map/ppermute | solution.py:202
  104.1 7.4 %collective-permute-start.53 = (bf16[2,2,128,128]{3,2,1,0:T(8,128)(2,1)S(1)}, bf16[2,2,128,128]{3,2,1,0:T(8,128)(2,1)S(1)}, u32[]{:S(2)}, u32[]{:S(2)}) collective-permute-start(bf16[2,2,128,128]{3,2,1,0:T(8,128)(2,1)S(1)} %get-tuple-element.88), channel_id=1, source_target_pairs={{0,4},{1,5},{2,6},{3,7},{4,0},{5,1},{6,2},{7,3},{8,12},{9,13},{10,... | collective-permute-start | bytes 393224 | tf_op jit(solution)/shard_map/ppermute | solution.py:202
  105.3 7.6 %collective-permute-start.50 = (bf16[2,2,128,128]{3,2,1,0:T(8,128)(2,1)S(1)}, bf16[2,2,128,128]{3,2,1,0:T(8,128)(2,1)S(1)}, u32[]{:S(2)}, u32[]{:S(2)}) collective-permute-start(bf16[2,2,128,128]{3,2,1,0:T(8,128)(2,1)S(1)} %get-tuple-element.90), channel_id=1, source_target_pairs={{0,1},{1,0},{2,3},{3,2},{4,5},{5,4},{6,7},{7,6},{8,9},{9,8},{10,11... | collective-permute-start | bytes 393224 | tf_op jit(solution)/shard_map/ppermute | solution.py:202
  (26 other events, 79.8 us)

commit v6 on v5

--- a/solution.py
+++ b/solution.py
@@ -9,6 +9,7 @@
 SPAN = 16
 PLANE = 8
 PLANES = 4
+TURNS = ((4, 2, 6), (2, 4, 6))
 VMEM_BYTES = 48 * 1024 * 1024
 
 
@@ -213,21 +214,33 @@
     return parts
 
 
+def in_turn(value, distances):
+    pairs = [(i, i ^ distances[i % 2]) for i in range(PLANE * PLANES)]
+    return lax.ppermute(value, "prow", pairs)
+
+
+def offsets_of(side):
+    core = lax.axis_index("prow") & 1
+    mine, other = TURNS if side == 0 else TURNS[::-1]
+    return [side] + [jnp.where(core == 0, a, b) + side for a, b in zip(mine, other, strict=True)]
+
+
 def in_plane(parts, direction):
     stacked = jnp.concatenate(parts, 0)
+    me = lax.axis_index("prow")
+
+    def sent(bit):
+        if direction == 0:
+            return stacked
+        near, far = jnp.concatenate(parts[:2], 0), jnp.concatenate(parts[1:], 0)
+        after = (me & bit) != 0
+        return jnp.where(after if direction > 0 else jnp.logical_not(after), far, near)
+
     pieces = {0: stacked}
-    if direction == 0:
-        sent = {1: stacked, 2: stacked, 4: stacked}
-    else:
-        near, far = jnp.concatenate(parts[:2], 0), jnp.concatenate(parts[1:], 0)
-        me = lax.axis_index("prow")
-        sent = {}
-        for bit in (1, 2, 4):
-            after = (me & bit) != 0
-            sent[bit] = jnp.where(after if direction > 0 else jnp.logical_not(after), far, near)
-    for k in (2, 4, 6):
-        pieces[k] = swap(sent[2 if k == 2 else 4], k)
-    pieces[1] = swap(sent[1], 1)
+    for place, pair in enumerate(zip(*TURNS, strict=True)):
+        bits = [2 if k == 2 else 4 for k in pair]
+        pieces[2 * place + 2] = in_turn(sent(jnp.where((me & 1) == 0, *bits)), pair)
+    pieces[1] = swap(sent(1), 1)
     for k in (2, 4, 6):
         pieces[k + 1] = swap(pieces[k], 1)
     return [pieces[k] for k in range(PLANE)]
@@ -244,12 +257,10 @@
     offset, parity = me & (PLANE - 1), (me & 1) ^ side
     size, lines = xs.shape[0], PLANE // 2
     pair = first_pair(start, parity)
-    for k, piece in zip(range(side, PLANE, 2), pieces, strict=True):
+    for k, piece in zip(offsets_of(side), pieces, strict=True):
         other = offset ^ k
         first = (other // 2 - pair) & (lines - 1)
-        skipped = jnp.int32(0)
-        if k > 0:
-            skipped = (other > offset if direction > 0 else other < offset).astype(jnp.int32)
+        skipped = (other > offset if direction > 0 else other < offset).astype(jnp.int32)
         for half in range(2):
             slot = first + half * lines
             source = 2 * (pair + slot) + parity
@@ -301,9 +312,9 @@
     plane = me // PLANE
     size = xs.shape[0]
     sources = ((own, 0, brought, 0), (near, 0, near, 4), (level, 0, level, 4), (far, 0, far, 4))
-    for m in range(4):
+    for m, k in enumerate(offsets_of(0)):
         for slot in range(4):
-            block = table[4 * (2 * m + odd) + slot]
+            block = table[4 * (k + odd) + slot]
             along = (block // PLANE) % PLANES ^ plane
             xs[:, slot * size : (slot + 1) * size] = known[along, block // (PLANE * PLANES)]
         factor, at = sources[m][2 * odd : 2 * odd + 2]
@@ -316,7 +327,7 @@
     size = xs.shape[0]
     many = xs.shape[1] // size
     if row == 0:
-        for k, piece in zip(range(side, PLANE, 2), pieces, strict=True):
+        for k, piece in zip(offsets_of(side), pieces, strict=True):
             for along in range(PLANES):
                 pair = (plane ^ along) * (PLANE // 2) + (offset ^ k) // 2
                 xs[:, pl.ds(pl.multiple_of(pair * size, size), size)] = piece[along, 0]
@@ -420,14 +431,19 @@
     rhs_lower = own[:2]
     parts = along_z(rhs_lower, forward)
     packed = first_pack(lower, rhs_lower, rules)
-    parts, (l1, even, odd, table) = barrier((parts, packed))
+    l1, even, odd, table = packed
+    parts, l1, even, table = barrier((parts, l1, even, table))
     pieces = in_plane(parts, forward)
     brought = swap(odd, 1)
     even, pieces[6] = barrier((even, pieces[6]))
     pairs = [
         jnp.concatenate([even[4 * m : 4 * m + 4], brought[4 * m : 4 * m + 4]], 0) for m in (1, 2, 3)
     ]
-    down = [swap(pair, 2 * (m + 1)) for m, pair in enumerate(pairs)]
+    turned = (lax.axis_index("prow") & 1) != 0
+    down = [
+        in_turn(jnp.where(turned, pairs[b // 2 - 1], pairs[a // 2 - 1]), (a, b))
+        for a, b in zip(*TURNS, strict=True)
+    ]
     solved, known = window("forward_lower", 2, forward, pieces, l1)
     parts = along_z(known, whole)
     parts[1], down = barrier((parts[1], down))
@@ -442,19 +458,25 @@
             4 * size,
             1,
         )
-    sums = sums[1] + swap(sums[0], 1)
-    arrived = [swap(sums[m], 2 * m) for m in (1, 2, 3)]
+    other = swap(sums[0], 1)
+    places = [0] + [TURNS[1].index(k) + 1 for k in TURNS[0]]
+    sums = [sums[1][m] + other[place] for m, place in enumerate(places)]
+    arrived = [in_turn(sums[m + 1], pair) for m, pair in enumerate(zip(*TURNS, strict=True))]
     coupling = (sums[0] + arrived[0] + arrived[1] + arrived[2]).astype(bf16).astype(f32)
     difference = (own[2:].astype(f32) - coupling).astype(bf16)
     pieces, packed = gather(difference, forward, level(lower, forward, 1))
     forward_upper, upper_known = window("forward_upper", 1, forward, pieces, packed)
-    pieces, packed = gather(upper_known, backward, level(upper, backward, 1))
+    upper_known, solved_now, upper_now = barrier((upper_known, solved, forward_upper))
+    parts = along_z(upper_known, backward)
     (forward_solution,) = local_call(
         forward_out_kernel,
         "forward_out",
         [((rows, 1, size, width), f32)],
-        [solved, forward_upper],
-    )
+        [solved_now, upper_now],
+    )
+    packed = level(upper, backward, 1)(upper_known)
+    parts, packed, forward_solution = barrier((parts, packed, forward_solution))
+    pieces = in_plane(parts, backward)
     backward_upper, back_known = window("backward_upper", 1, backward, pieces, packed)
     pieces, packed = gather(back_known, whole, pack_up)
     (part,) = local_call(

time: 115 us -> 112 us (0.974)
  waiting for transfers between devices: 45.8 us -> 41.7 us
  starting transfers between devices: 46.3 us -> 48.1 us
    ppermute x49 -> x28, waiting for transfers between devices: 38 us -> 6.97 us  [swap(): lax.ppermute(value, 'prow', [(i, i ^ distance) for i in range(PLANE * PLA...]
    ppermute x0 -> x21, waiting for transfers between devices: none -> 29.5 us  [in_turn(): return lax.ppermute(value, 'prow', pairs)]
    ppermute x0 -> x21, starting transfers between devices: none -> 24.9 us  [in_turn(): return lax.ppermute(value, 'prow', pairs)]
    ppermute x49 -> x28, starting transfers between devices: 34.3 us -> 9.44 us  [swap(): lax.ppermute(value, 'prow', [(i, i ^ distance) for i in range(PLANE * PLA...]
    ppermute x8, waiting for transfers between devices: 7.78 us -> 5.26 us  [along_z(): parts.append(lax.ppermute(block[None], 'prow', pairs))]
    ppermute x8, starting transfers between devices: 12 us -> 13.7 us  [along_z(): parts.append(lax.ppermute(block[None], 'prow', pairs))]
  transfers between devices with their start and end apart: 57 -> 57, of which waited for: 31 -> 33; matrix products, arithmetic and copies ran while one was open for 1% -> 1% of each run, Pallas kernels for 13% -> 14%
where the time goes in v6:
time: 112 us
  starting transfers between devices  48.1 us (43%)
  waiting for transfers between devices  41.7 us (37%)
  Pallas kernels  18.7 us (17%)
  local copies, waits for them, and re-layouts  1.13 us (1%)
    ppermute x21, waiting for transfers between devices, in_turn(): return lax.ppermute(value, 'prow', pairs)  29.5 us
    ppermute x21, starting transfers between devices, in_turn(): return lax.ppermute(value, 'prow', pairs)  24.9 us
    ppermute x8, starting transfers between devices, along_z(): parts.append(lax.ppermute(block[None], 'prow', pairs))  13.7 us
    ppermute x28, starting transfers between devices, swap(): lax.ppermute(value, 'prow', [(i, i ^ distance) for i in range(PLANE * PLA...  9.44 us
    pallas_call x14, Pallas kernels, local_call(): pl.pallas_call(kernel, out_shape=outs, in_specs=[pl.BlockSpec(memory_spac...  8.02 us
    pallas_call x4, Pallas kernels, pack_call(): pl.pallas_call(kernel, out_shape=jax.ShapeDtypeStruct((blocks, size, size...  7.63 us
    ppermute x28, waiting for transfers between devices, swap(): lax.ppermute(value, 'prow', [(i, i ^ distance) for i in range(PLANE * PLA...  6.97 us
    ppermute x8, waiting for transfers between devices, along_z(): parts.append(lax.ppermute(block[None], 'prow', pairs))  5.26 us
  transfers between devices with their start and end apart: 57, of which 33 were waited for; matrix products, arithmetic and copies ran while one was open for 1% of the time, Pallas kernels for 14%

profile of v6, /device:TPU:0, one launch (start us, length us, event | category | flops | bytes accessed | tf_op | source)
XLA Modules:
  0.0 111.9 jit_solution(3799775156297808966)
XLA Ops:
  1.7 4.1 %collective-permute-start.1 = (bf16[1,2,128,128]{3,2,1,0:T(8,128)(2,1)S(1)}, bf16[1,2,128,128]{3,2,1,0:T(8,128)(2,1)S(1)}, u32[]{:S(2)}, u32[]{:S(2)}) collective-permute-start(bf16[1,2,128,128]{3,2,1,0:T(8,128)(2,1)S(1)} %get-tuple-element.50), channel_id=1, source_target_pairs={{0,16},{1,17},{2,18},{3,19},{4,20},{5,21},{6,22},{7,23},{8,24},{9,... | collective-permute-start | bytes 196616 | tf_op jit(solution)/shard_map/ppermute | solution.py:213
  5.8 1.6 %collective-permute-start = (bf16[1,2,128,128]{3,2,1,0:T(8,128)(2,1)S(1)}, bf16[1,2,128,128]{3,2,1,0:T(8,128)(2,1)S(1)}, u32[]{:S(2)}, u32[]{:S(2)}) collective-permute-start(bf16[1,2,128,128]{3,2,1,0:T(8,128)(2,1)S(1)} %get-tuple-element.50), channel_id=1, source_target_pairs={{0,8},{1,9},{2,10},{3,11},{4,12},{5,13},{6,14},{7,15},{8,16},{9,17... | collective-permute-start | bytes 196616 | tf_op jit(solution)/shard_map/ppermute | solution.py:213
  8.1 3.1 %first_pack.1 = (bf16[32,128,128]{2,1,0:T(8,128)(2,1)S(1)}, bf16[16,128,128]{2,1,0:T(8,128)(2,1)S(1)}, bf16[16,128,128]{2,1,0:T(8,128)(2,1)S(1)}, s32[32]{0:T(128)S(1)}) custom-call(bf16[48,2,3,128,128]{4,3,2,1,0:T(8,128)(2,1)} %bitcast.65, bf16[2,128,128]{2,1,0:T(8,128)(2,1)S(1)} %get-tuple-element.115.after, s32[8,128]{1,0:T(8,128)S(1)} %pad_add_fusion.rules), custom_call_target="tpu_custom_call" | custom-call | bytes 4194304 | tf_op jit(solution)/shard_map/first_pack/pallas_call | solution.py:184
  11.9 2.5 %collective-permute-start.7 = (bf16[2,2,128,128]{3,2,1,0:T(8,128)(2,1)S(1)}, bf16[2,2,128,128]{3,2,1,0:T(8,128)(2,1)S(1)}, u32[]{:S(2)}, u32[]{:S(2)}) collective-permute-start(bf16[2,2,128,128]{3,2,1,0:T(8,128)(2,1)S(1)} %get-tuple-element.103), channel_id=1, source_target_pairs={{0,6},{1,7},{2,4},{3,5},{4,2},{5,3},{6,0},{7,1},{8,14},{9,15},{10,... | collective-permute-start | bytes 393224 | tf_op jit(solution)/shard_map/ppermute | solution.py:219
  15.5 3.0 %collective-permute-done.7.refs_3_ = bf16[2,2,128,128]{3,2,1,0:T(8,128)(2,1)S(1)} collective-permute-done((bf16[2,2,128,128]{3,2,1,0:T(8,128)(2,1)S(1)}, bf16[2,2,128,128]{3,2,1,0:T(8,128)(2,1)S(1)}, u32[]{:S(2)}, u32[]{:S(2)}) %collective-permute-start.7) | collective-permute-done | bytes 131104 | tf_op jit(solution)/shard_map/ppermute | solution.py:219
  18.5 2.6 %collective-permute-done.5.refs_2_ = bf16[2,2,128,128]{3,2,1,0:T(8,128)(2,1)S(1)} collective-permute-done((bf16[2,2,128,128]{3,2,1,0:T(8,128)(2,1)S(1)}, bf16[2,2,128,128]{3,2,1,0:T(8,128)(2,1)S(1)}, u32[]{:S(2)}, u32[]{:S(2)}) %collective-permute-start.5) | collective-permute-done | bytes 131104 | tf_op jit(solution)/shard_map/ppermute | solution.py:219
  21.7 1.6 %collective-permute-start.12 = (bf16[8,128,128]{2,1,0:T(8,128)(2,1)S(1)}, bf16[8,128,128]{2,1,0:T(8,128)(2,1)S(1)}, u32[]{:S(2)}, u32[]{:S(2)}) collective-permute-start(bf16[8,128,128]{2,1,0:T(8,128)(2,1)S(1)} %get-tuple-element.97), channel_id=1, source_target_pairs={{0,2},{1,5},{2,0},{3,7},{4,6},{5,1},{6,4},{7,3},{8,10},{9,13},{10,... | collective-permute-start | bytes 786440 | tf_op jit(solution)/shard_map/ppermute | solution.py:219
  23.9 1.5 %collective-permute-start.13 = (bf16[8,128,128]{2,1,0:T(8,128)(2,1)S(1)}, bf16[8,128,128]{2,1,0:T(8,128)(2,1)S(1)}, u32[]{:S(2)}, u32[]{:S(2)}) collective-permute-start(bf16[8,128,128]{2,1,0:T(8,128)(2,1)S(1)} %pad_maximum_fusion.2), channel_id=1, source_target_pairs={{0,6},{1,7},{2,4},{3,5},{4,2},{5,3},{6,0},{7,1},{8,14},{9,15},{10,... | collective-permute-start | bytes 786440 | tf_op jit(solution)/shard_map/ppermute | solution.py:219
  26.6 2.7 %collective-permute-start.15 = (bf16[1,2,128,128]{3,2,1,0:T(8,128)(2,1)S(1)}, bf16[1,2,128,128]{3,2,1,0:T(8,128)(2,1)S(1)}, u32[]{:S(2)}, u32[]{:S(2)}) collective-permute-start(bf16[1,2,128,128]{3,2,1,0:T(8,128)(2,1)S(1)} %bitcast.59), channel_id=1, source_target_pairs={{0,24},{1,25},{2,26},{3,27},{4,28},{5,29},{6,30},{7,31},{8,16},{9,... | collective-permute-start | bytes 196616 | tf_op jit(solution)/shard_map/ppermute | solution.py:203
  29.2 2.3 %collective-permute-done.9 = bf16[1,2,128,128]{3,2,1,0:T(8,128)(2,1)S(1)} collective-permute-done((bf16[1,2,128,128]{3,2,1,0:T(8,128)(2,1)S(1)}, bf16[1,2,128,128]{3,2,1,0:T(8,128)(2,1)S(1)}, u32[]{:S(2)}, u32[]{:S(2)}) %collective-permute-start.9) | collective-permute-done | bytes 65568 | tf_op jit(solution)/shard_map/ppermute | solution.py:203
  32.1 4.8 %collective-permute-done.13.far = bf16[8,128,128]{2,1,0:T(8,128)(2,1)S(1)} collective-permute-done((bf16[8,128,128]{2,1,0:T(8,128)(2,1)S(1)}, bf16[8,128,128]{2,1,0:T(8,128)(2,1)S(1)}, u32[]{:S(2)}, u32[]{:S(2)}) %collective-permute-start.13) | collective-permute-done | bytes 262176 | tf_op jit(solution)/shard_map/ppermute | solution.py:219
  40.4 2.0 %collective-permute-start.19 = (f32[128,128]{1,0:T(8,128)S(1)}, f32[128,128]{1,0:T(8,128)S(1)}, u32[]{:S(2)}, u32[]{:S(2)}) collective-permute-start(f32[128,128]{1,0:T(8,128)S(1)} %get-tuple-element.89), channel_id=1, source_target_pairs={{0,6},{1,7},{2,4},{3,5},{4,2},{5,3},{6,0},{7,1},{8,14},{9,15},{10,... | collective-permute-start | bytes 196616 | tf_op jit(solution)/shard_map/ppermute | solution.py:219
  43.9 1.9 %collective-permute-done.19 = f32[128,128]{1,0:T(8,128)S(1)} collective-permute-done((f32[128,128]{1,0:T(8,128)S(1)}, f32[128,128]{1,0:T(8,128)S(1)}, u32[]{:S(2)}, u32[]{:S(2)}) %collective-permute-start.19) | collective-permute-done | bytes 65568 | tf_op jit(solution)/shard_map/ppermute | solution.py:219
  47.4 2.1 %collective-permute-start.20 = (bf16[1,1,128,128]{3,2,1,0:T(8,128)(2,1)S(1)}, bf16[1,1,128,128]{3,2,1,0:T(8,128)(2,1)S(1)}, u32[]{:S(2)}, u32[]{:S(2)}) collective-permute-start(bf16[1,1,128,128]{3,2,1,0:T(8,128)(2,1)S(1)} %bitcast.47), channel_id=1, source_target_pairs={{0,8},{1,9},{2,10},{3,11},{4,12},{5,13},{6,14},{7,15},{8,16},{9,17... | collective-permute-start | bytes 98312 | tf_op jit(solution)/shard_map/ppermute | solution.py:213
  49.5 1.7 %pack_level.3.refs_4_ = bf16[16,128,128]{2,1,0:T(8,128)(2,1)S(1)} custom-call(bf16[48,2,3,128,128]{4,3,2,1,0:T(8,128)(2,1)} %bitcast.66, bf16[1,128,128]{2,1,0:T(8,128)(2,1)S(1)} %fusion.8.after, s32[8,128]{1,0:T(8,128)S(1)} %pad_add_fusion.rules), custom_call_target="tpu_custom_call" | custom-call | bytes 1048576 | tf_op jit(solution)/shard_map/pack_level/pallas_call | solution.py:100
  51.6 1.6 %collective-permute-done.20 = bf16[1,1,128,128]{3,2,1,0:T(8,128)(2,1)S(1)} collective-permute-done((bf16[1,1,128,128]{3,2,1,0:T(8,128)(2,1)S(1)}, bf16[1,1,128,128]{3,2,1,0:T(8,128)(2,1)S(1)}, u32[]{:S(2)}, u32[]{:S(2)}) %collective-permute-start.20) | collective-permute-done | bytes 32800 | tf_op jit(solution)/shard_map/ppermute | solution.py:213
  53.2 1.7 %collective-permute-start.27 = (bf16[2,1,128,128]{3,2,1,0:T(8,128)(2,1)S(1)}, bf16[2,1,128,128]{3,2,1,0:T(8,128)(2,1)S(1)}, u32[]{:S(2)}, u32[]{:S(2)}) collective-permute-start(bf16[2,1,128,128]{3,2,1,0:T(8,128)(2,1)S(1)} %get-tuple-element.111), channel_id=1, source_target_pairs={{0,6},{1,7},{2,4},{3,5},{4,2},{5,3},{6,0},{7,1},{8,14},{9,15},{10,... | collective-permute-start | bytes 196616 | tf_op jit(solution)/shard_map/ppermute | solution.py:219
  54.9 1.3 %collective-permute-start.25 = (bf16[2,1,128,128]{3,2,1,0:T(8,128)(2,1)S(1)}, bf16[2,1,128,128]{3,2,1,0:T(8,128)(2,1)S(1)}, u32[]{:S(2)}, u32[]{:S(2)}) collective-permute-start(bf16[2,1,128,128]{3,2,1,0:T(8,128)(2,1)S(1)} %get-tuple-element.112), channel_id=1, source_target_pairs={{0,2},{1,5},{2,0},{3,7},{4,6},{5,1},{6,4},{7,3},{8,10},{9,13},{10,... | collective-permute-start | bytes 196616 | tf_op jit(solution)/shard_map/ppermute | solution.py:219
  56.8 1.7 %collective-permute-done.27.refs_3_ = bf16[2,1,128,128]{3,2,1,0:T(8,128)(2,1)S(1)} collective-permute-done((bf16[2,1,128,128]{3,2,1,0:T(8,128)(2,1)S(1)}, bf16[2,1,128,128]{3,2,1,0:T(8,128)(2,1)S(1)}, u32[]{:S(2)}, u32[]{:S(2)}) %collective-permute-start.27) | collective-permute-done | bytes 65568 | tf_op jit(solution)/shard_map/ppermute | solution.py:219
  59.2 1.3 %collective-permute-done.23.refs_1_ = bf16[2,1,128,128]{3,2,1,0:T(8,128)(2,1)S(1)} collective-permute-done((bf16[2,1,128,128]{3,2,1,0:T(8,128)(2,1)S(1)}, bf16[2,1,128,128]{3,2,1,0:T(8,128)(2,1)S(1)}, u32[]{:S(2)}, u32[]{:S(2)}) %collective-permute-start.23) | collective-permute-done | bytes 65568 | tf_op jit(solution)/shard_map/ppermute | solution.py:219
  62.1 2.1 %collective-permute-start.29 = (bf16[1,1,128,128]{3,2,1,0:T(8,128)(2,1)S(1)}, bf16[1,1,128,128]{3,2,1,0:T(8,128)(2,1)S(1)}, u32[]{:S(2)}, u32[]{:S(2)}) collective-permute-start(bf16[1,1,128,128]{3,2,1,0:T(8,128)(2,1)S(1)} %bitcast.51), channel_id=1, source_target_pairs={{0,24},{1,25},{2,26},{3,27},{4,28},{5,29},{6,30},{7,31},{8,0},{9,1... | collective-permute-start | bytes 98312 | tf_op jit(solution)/shard_map/ppermute | solution.py:213
  64.3 1.7 %pack_level.4.refs_4_ = bf16[16,128,128]{2,1,0:T(8,128)(2,1)S(1)} custom-call(bf16[48,2,3,128,128]{4,3,2,1,0:T(8,128)(2,1)} %bitcast.62, bf16[1,128,128]{2,1,0:T(8,128)(2,1)S(1)} %get-tuple-element.69.after, s32[8,128]{1,0:T(8,128)S(1)} %pad_add_fusion.rules), custom_call_target="tpu_custom_call" | custom-call | bytes 1048576 | tf_op jit(solution)/shard_map/pack_level/pallas_call | solution.py:100
  70.8 1.9 %collective-permute-done.36.refs_3_ = bf16[2,1,128,128]{3,2,1,0:T(8,128)(2,1)S(1)} collective-permute-done((bf16[2,1,128,128]{3,2,1,0:T(8,128)(2,1)S(1)}, bf16[2,1,128,128]{3,2,1,0:T(8,128)(2,1)S(1)}, u32[]{:S(2)}, u32[]{:S(2)}) %collective-permute-start.36) | collective-permute-done | bytes 65568 | tf_op jit(solution)/shard_map/ppermute | solution.py:219
  75.3 3.2 %collective-permute-start.40 = (bf16[1,1,128,128]{3,2,1,0:T(8,128)(2,1)S(1)}, bf16[1,1,128,128]{3,2,1,0:T(8,128)(2,1)S(1)}, u32[]{:S(2)}, u32[]{:S(2)}) collective-permute-start(bf16[1,1,128,128]{3,2,1,0:T(8,128)(2,1)S(1)} %bitcast.54), channel_id=1, source_target_pairs={{0,24},{1,25},{2,26},{3,27},{4,28},{5,29},{6,30},{7,31},{8,16},{9,... | collective-permute-start | bytes 98312 | tf_op jit(solution)/shard_map/ppermute | solution.py:203
  79.8 2.3 %pack_up.1.refs_4_ = bf16[64,128,128]{2,1,0:T(8,128)(2,1)S(1)} custom-call(bf16[48,2,3,128,128]{4,3,2,1,0:T(8,128)(2,1)} %bitcast.63, bf16[1,128,128]{2,1,0:T(8,128)(2,1)S(1)} %get-tuple-element.77.after, s32[8,128]{1,0:T(8,128)S(1)} %pad_add_fusion.rules), custom_call_target="tpu_custom_call" | custom-call | bytes 4194304 | tf_op jit(solution)/shard_map/pack_up/pallas_call | solution.py:100
  84.6 1.3 %collective-permute-start.44 = (bf16[4,1,128,128]{3,2,1,0:T(8,128)(2,1)S(1)}, bf16[4,1,128,128]{3,2,1,0:T(8,128)(2,1)S(1)}, u32[]{:S(2)}, u32[]{:S(2)}) collective-permute-start(bf16[4,1,128,128]{3,2,1,0:T(8,128)(2,1)S(1)} %constant_dynamic-update-slice_fusion.12.refs_0_), channel_id=1, source_target_pairs={{0,2},{1,5},{2,0},{3,7},{4,6},{5,1},{6,4},{7,3},{8,10},{9,13},{10,... | collective-permute-start | bytes 393224 | tf_op jit(solution)/shard_map/ppermute | solution.py:219
  87.0 3.0 %collective-permute-done.46.refs_3_ = bf16[4,1,128,128]{3,2,1,0:T(8,128)(2,1)S(1)} collective-permute-done((bf16[4,1,128,128]{3,2,1,0:T(8,128)(2,1)S(1)}, bf16[4,1,128,128]{3,2,1,0:T(8,128)(2,1)S(1)}, u32[]{:S(2)}, u32[]{:S(2)}) %collective-permute-start.46) | collective-permute-done | bytes 131104 | tf_op jit(solution)/shard_map/ppermute | solution.py:219
  93.3 2.0 %collective-permute-start.49 = (bf16[1,2,128,128]{3,2,1,0:T(8,128)(2,1)S(1)}, bf16[1,2,128,128]{3,2,1,0:T(8,128)(2,1)S(1)}, u32[]{:S(2)}, u32[]{:S(2)}) collective-permute-start(bf16[1,2,128,128]{3,2,1,0:T(8,128)(2,1)S(1)} %bitcast.42), channel_id=1, source_target_pairs={{0,16},{1,17},{2,18},{3,19},{4,20},{5,21},{6,22},{7,23},{8,24},{9,... | collective-permute-start | bytes 196616 | tf_op jit(solution)/shard_map/ppermute | solution.py:213
  96.3 1.9 %pack_level.5.refs_4_ = bf16[32,128,128]{2,1,0:T(8,128)(2,1)S(1)} custom-call(bf16[48,2,3,128,128]{4,3,2,1,0:T(8,128)(2,1)} %bitcast.64, bf16[2,128,128]{2,1,0:T(8,128)(2,1)S(1)} %correction.1.after, s32[8,128]{1,0:T(8,128)S(1)} %pad_add_fusion.rules), custom_call_target="tpu_custom_call" | custom-call | bytes 2097152 | tf_op jit(solution)/shard_map/pack_level/pallas_call | solution.py:100
  98.2 1.9 %collective-permute-done.49 = bf16[1,2,128,128]{3,2,1,0:T(8,128)(2,1)S(1)} collective-permute-done((bf16[1,2,128,128]{3,2,1,0:T(8,128)(2,1)S(1)}, bf16[1,2,128,128]{3,2,1,0:T(8,128)(2,1)S(1)}, u32[]{:S(2)}, u32[]{:S(2)}) %collective-permute-start.49) | collective-permute-done | bytes 65568 | tf_op jit(solution)/shard_map/ppermute | solution.py:213
  100.7 1.5 %collective-permute-start.55 = (bf16[2,2,128,128]{3,2,1,0:T(8,128)(2,1)S(1)}, bf16[2,2,128,128]{3,2,1,0:T(8,128)(2,1)S(1)}, u32[]{:S(2)}, u32[]{:S(2)}) collective-permute-start(bf16[2,2,128,128]{3,2,1,0:T(8,128)(2,1)S(1)} %get-tuple-element.99), channel_id=1, source_target_pairs={{0,6},{1,7},{2,4},{3,5},{4,2},{5,3},{6,0},{7,1},{8,14},{9,15},{10,... | collective-permute-start | bytes 393224 | tf_op jit(solution)/shard_map/ppermute | solution.py:219
  104.3 3.7 %collective-permute-done.55.refs_3_ = bf16[2,2,128,128]{3,2,1,0:T(8,128)(2,1)S(1)} collective-permute-done((bf16[2,2,128,128]{3,2,1,0:T(8,128)(2,1)S(1)}, bf16[2,2,128,128]{3,2,1,0:T(8,128)(2,1)S(1)}, u32[]{:S(2)}, u32[]{:S(2)}) %collective-permute-start.55) | collective-permute-done | bytes 131104 | tf_op jit(solution)/shard_map/ppermute | solution.py:219
  (136 shorter events, 39.3 us)
Async XLA Ops:
  1.7 9.6 %collective-permute-start.1 = (bf16[1,2,128,128]{3,2,1,0:T(8,128)(2,1)S(1)}, bf16[1,2,128,128]{3,2,1,0:T(8,128)(2,1)S(1)}, u32[]{:S(2)}, u32[]{:S(2)}) collective-permute-start(bf16[1,2,128,128]{3,2,1,0:T(8,128)(2,1)S(1)} %get-tuple-element.50), channel_id=1, source_target_pairs={{0,16},{1,17},{2,18},{3,19},{4,20},{5,21},{6,22},{7,23},{8,24},{9,... | collective-permute-start | bytes 196616 | tf_op jit(solution)/shard_map/ppermute | solution.py:213
  5.8 6.1 %collective-permute-start = (bf16[1,2,128,128]{3,2,1,0:T(8,128)(2,1)S(1)}, bf16[1,2,128,128]{3,2,1,0:T(8,128)(2,1)S(1)}, u32[]{:S(2)}, u32[]{:S(2)}) collective-permute-start(bf16[1,2,128,128]{3,2,1,0:T(8,128)(2,1)S(1)} %get-tuple-element.50), channel_id=1, source_target_pairs={{0,8},{1,9},{2,10},{3,11},{4,12},{5,13},{6,14},{7,15},{8,16},{9,17... | collective-permute-start | bytes 196616 | tf_op jit(solution)/shard_map/ppermute | solution.py:213
  11.1 10.5 %collective-permute-start.10 = (bf16[16,128,128]{2,1,0:T(8,128)(2,1)S(1)}, bf16[16,128,128]{2,1,0:T(8,128)(2,1)S(1)}, u32[]{:S(2)}, u32[]{:S(2)}) collective-permute-start(bf16[16,128,128]{2,1,0:T(8,128)(2,1)S(1)} %get-tuple-element.56), channel_id=1, source_target_pairs={{0,1},{1,0},{2,3},{3,2},{4,5},{5,4},{6,7},{7,6},{8,9},{9,8},{10,11... | collective-permute-start | bytes 1572872 | tf_op jit(solution)/shard_map/ppermute | solution.py:203
  11.9 6.6 %collective-permute-start.7 = (bf16[2,2,128,128]{3,2,1,0:T(8,128)(2,1)S(1)}, bf16[2,2,128,128]{3,2,1,0:T(8,128)(2,1)S(1)}, u32[]{:S(2)}, u32[]{:S(2)}) collective-permute-start(bf16[2,2,128,128]{3,2,1,0:T(8,128)(2,1)S(1)} %get-tuple-element.103), channel_id=1, source_target_pairs={{0,6},{1,7},{2,4},{3,5},{4,2},{5,3},{6,0},{7,1},{8,14},{9,15},{10,... | collective-permute-start | bytes 393224 | tf_op jit(solution)/shard_map/ppermute | solution.py:219
  14.4 6.6 %collective-permute-start.5 = (bf16[2,2,128,128]{3,2,1,0:T(8,128)(2,1)S(1)}, bf16[2,2,128,128]{3,2,1,0:T(8,128)(2,1)S(1)}, u32[]{:S(2)}, u32[]{:S(2)}) collective-permute-start(bf16[2,2,128,128]{3,2,1,0:T(8,128)(2,1)S(1)} %get-tuple-element.104), channel_id=1, source_target_pairs={{0,2},{1,5},{2,0},{3,7},{4,6},{5,1},{6,4},{7,3},{8,10},{9,13},{10,... | collective-permute-start | bytes 393224 | tf_op jit(solution)/shard_map/ppermute | solution.py:219
  15.0 6.1 %collective-permute-start.3 = (bf16[2,2,128,128]{3,2,1,0:T(8,128)(2,1)S(1)}, bf16[2,2,128,128]{3,2,1,0:T(8,128)(2,1)S(1)}, u32[]{:S(2)}, u32[]{:S(2)}) collective-permute-start(bf16[2,2,128,128]{3,2,1,0:T(8,128)(2,1)S(1)} %get-tuple-element.105), channel_id=1, source_target_pairs={{0,4},{1,3},{2,6},{3,1},{4,0},{5,7},{6,2},{7,5},{8,12},{9,11},{10,... | collective-permute-start | bytes 393224 | tf_op jit(solution)/shard_map/ppermute | solution.py:219
  15.5 7.9 %collective-permute-start.2 = (bf16[2,2,128,128]{3,2,1,0:T(8,128)(2,1)S(1)}, bf16[2,2,128,128]{3,2,1,0:T(8,128)(2,1)S(1)}, u32[]{:S(2)}, u32[]{:S(2)}) collective-permute-start(bf16[2,2,128,128]{3,2,1,0:T(8,128)(2,1)S(1)} %get-tuple-element.106), channel_id=1, source_target_pairs={{0,1},{1,0},{2,3},{3,2},{4,5},{5,4},{6,7},{7,6},{8,9},{9,8},{10,11... | collective-permute-start | bytes 393224 | tf_op jit(solution)/shard_map/ppermute | solution.py:203
  18.5 5.4 %collective-permute-start.8 = (bf16[2,2,128,128]{3,2,1,0:T(8,128)(2,1)S(1)}, bf16[2,2,128,128]{3,2,1,0:T(8,128)(2,1)S(1)}, u32[]{:S(2)}, u32[]{:S(2)}) collective-permute-start(bf16[2,2,128,128]{3,2,1,0:T(8,128)(2,1)S(1)} %collective-permute-done.7.refs_3_), channel_id=1, source_target_pairs={{0,1},{1,0},{2,3},{3,2},{4,5},{5,4},{6,7},{7,6},{8,9},{9,8},{10,11... | collective-permute-start | bytes 393224 | tf_op jit(solution)/shard_map/ppermute | solution.py:203
  21.7 10.4 %collective-permute-start.12 = (bf16[8,128,128]{2,1,0:T(8,128)(2,1)S(1)}, bf16[8,128,128]{2,1,0:T(8,128)(2,1)S(1)}, u32[]{:S(2)}, u32[]{:S(2)}) collective-permute-start(bf16[8,128,128]{2,1,0:T(8,128)(2,1)S(1)} %get-tuple-element.97), channel_id=1, source_target_pairs={{0,2},{1,5},{2,0},{3,7},{4,6},{5,1},{6,4},{7,3},{8,10},{9,13},{10,... | collective-permute-start | bytes 786440 | tf_op jit(solution)/shard_map/ppermute | solution.py:219
  23.4 8.8 %collective-permute-start.11 = (bf16[8,128,128]{2,1,0:T(8,128)(2,1)S(1)}, bf16[8,128,128]{2,1,0:T(8,128)(2,1)S(1)}, u32[]{:S(2)}, u32[]{:S(2)}) collective-permute-start(bf16[8,128,128]{2,1,0:T(8,128)(2,1)S(1)} %get-tuple-element.98), channel_id=1, source_target_pairs={{0,4},{1,3},{2,6},{3,1},{4,0},{5,7},{6,2},{7,5},{8,12},{9,11},{10,... | collective-permute-start | bytes 786440 | tf_op jit(solution)/shard_map/ppermute | solution.py:219
  23.9 13.0 %collective-permute-start.13 = (bf16[8,128,128]{2,1,0:T(8,128)(2,1)S(1)}, bf16[8,128,128]{2,1,0:T(8,128)(2,1)S(1)}, u32[]{:S(2)}, u32[]{:S(2)}) collective-permute-start(bf16[8,128,128]{2,1,0:T(8,128)(2,1)S(1)} %pad_maximum_fusion.2), channel_id=1, source_target_pairs={{0,6},{1,7},{2,4},{3,5},{4,2},{5,3},{6,0},{7,1},{8,14},{9,15},{10,... | collective-permute-start | bytes 786440 | tf_op jit(solution)/shard_map/ppermute | solution.py:219
  26.5 5.0 %collective-permute-start.9 = (bf16[1,2,128,128]{3,2,1,0:T(8,128)(2,1)S(1)}, bf16[1,2,128,128]{3,2,1,0:T(8,128)(2,1)S(1)}, u32[]{:S(2)}, u32[]{:S(2)}) collective-permute-start(bf16[1,2,128,128]{3,2,1,0:T(8,128)(2,1)S(1)} %bitcast.58), channel_id=1, source_target_pairs={{0,8},{1,9},{2,10},{3,11},{4,12},{5,13},{6,14},{7,15},{8,0},{9,1},... | collective-permute-start | bytes 196616 | tf_op jit(solution)/shard_map/ppermute | solution.py:203
  26.6 10.3 %collective-permute-start.15 = (bf16[1,2,128,128]{3,2,1,0:T(8,128)(2,1)S(1)}, bf16[1,2,128,128]{3,2,1,0:T(8,128)(2,1)S(1)}, u32[]{:S(2)}, u32[]{:S(2)}) collective-permute-start(bf16[1,2,128,128]{3,2,1,0:T(8,128)(2,1)S(1)} %bitcast.59), channel_id=1, source_target_pairs={{0,24},{1,25},{2,26},{3,27},{4,28},{5,29},{6,30},{7,31},{8,16},{9,... | collective-permute-start | bytes 196616 | tf_op jit(solution)/shard_map/ppermute | solution.py:203
  31.5 5.4 %collective-permute-start.14 = (bf16[1,2,128,128]{3,2,1,0:T(8,128)(2,1)S(1)}, bf16[1,2,128,128]{3,2,1,0:T(8,128)(2,1)S(1)}, u32[]{:S(2)}, u32[]{:S(2)}) collective-permute-start(bf16[1,2,128,128]{3,2,1,0:T(8,128)(2,1)S(1)} %bitcast.60), channel_id=1, source_target_pairs={{0,16},{1,17},{2,18},{3,19},{4,20},{5,21},{6,22},{7,23},{8,24},{9,... | collective-permute-start | bytes 196616 | tf_op jit(solution)/shard_map/ppermute | solution.py:203
  40.4 5.4 %collective-permute-start.19 = (f32[128,128]{1,0:T(8,128)S(1)}, f32[128,128]{1,0:T(8,128)S(1)}, u32[]{:S(2)}, u32[]{:S(2)}) collective-permute-start(f32[128,128]{1,0:T(8,128)S(1)} %get-tuple-element.89), channel_id=1, source_target_pairs={{0,6},{1,7},{2,4},{3,5},{4,2},{5,3},{6,0},{7,1},{8,14},{9,15},{10,... | collective-permute-start | bytes 196616 | tf_op jit(solution)/shard_map/ppermute | solution.py:219
  46.7 4.9 %collective-permute-start.21 = (bf16[1,1,128,128]{3,2,1,0:T(8,128)(2,1)S(1)}, bf16[1,1,128,128]{3,2,1,0:T(8,128)(2,1)S(1)}, u32[]{:S(2)}, u32[]{:S(2)}) collective-permute-start(bf16[1,1,128,128]{3,2,1,0:T(8,128)(2,1)S(1)} %bitcast.46), channel_id=1, source_target_pairs={{0,16},{1,17},{2,18},{3,19},{4,20},{5,21},{6,22},{7,23},{8,24},{9,... | collective-permute-start | bytes 98312 | tf_op jit(solution)/shard_map/ppermute | solution.py:213
  47.4 5.7 %collective-permute-start.20 = (bf16[1,1,128,128]{3,2,1,0:T(8,128)(2,1)S(1)}, bf16[1,1,128,128]{3,2,1,0:T(8,128)(2,1)S(1)}, u32[]{:S(2)}, u32[]{:S(2)}) collective-permute-start(bf16[1,1,128,128]{3,2,1,0:T(8,128)(2,1)S(1)} %bitcast.47), channel_id=1, source_target_pairs={{0,8},{1,9},{2,10},{3,11},{4,12},{5,13},{6,14},{7,15},{8,16},{9,17... | collective-permute-start | bytes 98312 | tf_op jit(solution)/shard_map/ppermute | solution.py:213
  53.2 5.2 %collective-permute-start.27 = (bf16[2,1,128,128]{3,2,1,0:T(8,128)(2,1)S(1)}, bf16[2,1,128,128]{3,2,1,0:T(8,128)(2,1)S(1)}, u32[]{:S(2)}, u32[]{:S(2)}) collective-permute-start(bf16[2,1,128,128]{3,2,1,0:T(8,128)(2,1)S(1)} %get-tuple-element.111), channel_id=1, source_target_pairs={{0,6},{1,7},{2,4},{3,5},{4,2},{5,3},{6,0},{7,1},{8,14},{9,15},{10,... | collective-permute-start | bytes 196616 | tf_op jit(solution)/shard_map/ppermute | solution.py:219
  62.1 5.1 %collective-permute-start.30 = (bf16[1,1,128,128]{3,2,1,0:T(8,128)(2,1)S(1)}, bf16[1,1,128,128]{3,2,1,0:T(8,128)(2,1)S(1)}, u32[]{:S(2)}, u32[]{:S(2)}) collective-permute-start(bf16[1,1,128,128]{3,2,1,0:T(8,128)(2,1)S(1)} %bitcast.50), channel_id=1, source_target_pairs={{0,16},{1,17},{2,18},{3,19},{4,20},{5,21},{6,22},{7,23},{8,24},{9,... | collective-permute-start | bytes 98312 | tf_op jit(solution)/shard_map/ppermute | solution.py:213
  62.1 5.0 %collective-permute-start.29 = (bf16[1,1,128,128]{3,2,1,0:T(8,128)(2,1)S(1)}, bf16[1,1,128,128]{3,2,1,0:T(8,128)(2,1)S(1)}, u32[]{:S(2)}, u32[]{:S(2)}) collective-permute-start(bf16[1,1,128,128]{3,2,1,0:T(8,128)(2,1)S(1)} %bitcast.51), channel_id=1, source_target_pairs={{0,24},{1,25},{2,26},{3,27},{4,28},{5,29},{6,30},{7,31},{8,0},{9,1... | collective-permute-start | bytes 98312 | tf_op jit(solution)/shard_map/ppermute | solution.py:213
  67.2 5.5 %collective-permute-start.36 = (bf16[2,1,128,128]{3,2,1,0:T(8,128)(2,1)S(1)}, bf16[2,1,128,128]{3,2,1,0:T(8,128)(2,1)S(1)}, u32[]{:S(2)}, u32[]{:S(2)}) collective-permute-start(bf16[2,1,128,128]{3,2,1,0:T(8,128)(2,1)S(1)} %get-tuple-element.107), channel_id=1, source_target_pairs={{0,6},{1,7},{2,4},{3,5},{4,2},{5,3},{6,0},{7,1},{8,14},{9,15},{10,... | collective-permute-start | bytes 196616 | tf_op jit(solution)/shard_map/ppermute | solution.py:219
  75.3 6.8 %collective-permute-start.40 = (bf16[1,1,128,128]{3,2,1,0:T(8,128)(2,1)S(1)}, bf16[1,1,128,128]{3,2,1,0:T(8,128)(2,1)S(1)}, u32[]{:S(2)}, u32[]{:S(2)}) collective-permute-start(bf16[1,1,128,128]{3,2,1,0:T(8,128)(2,1)S(1)} %bitcast.54), channel_id=1, source_target_pairs={{0,24},{1,25},{2,26},{3,27},{4,28},{5,29},{6,30},{7,31},{8,16},{9,... | collective-permute-start | bytes 98312 | tf_op jit(solution)/shard_map/ppermute | solution.py:203
  83.4 6.6 %collective-permute-start.46 = (bf16[4,1,128,128]{3,2,1,0:T(8,128)(2,1)S(1)}, bf16[4,1,128,128]{3,2,1,0:T(8,128)(2,1)S(1)}, u32[]{:S(2)}, u32[]{:S(2)}) collective-permute-start(bf16[4,1,128,128]{3,2,1,0:T(8,128)(2,1)S(1)} %constant_dynamic-update-slice_fusion.12.refs_0_), channel_id=1, source_target_pairs={{0,6},{1,7},{2,4},{3,5},{4,2},{5,3},{6,0},{7,1},{8,14},{9,15},{10,... | collective-permute-start | bytes 393224 | tf_op jit(solution)/shard_map/ppermute | solution.py:219
  84.6 6.6 %collective-permute-start.44 = (bf16[4,1,128,128]{3,2,1,0:T(8,128)(2,1)S(1)}, bf16[4,1,128,128]{3,2,1,0:T(8,128)(2,1)S(1)}, u32[]{:S(2)}, u32[]{:S(2)}) collective-permute-start(bf16[4,1,128,128]{3,2,1,0:T(8,128)(2,1)S(1)} %constant_dynamic-update-slice_fusion.12.refs_0_), channel_id=1, source_target_pairs={{0,2},{1,5},{2,0},{3,7},{4,6},{5,1},{6,4},{7,3},{8,10},{9,13},{10,... | collective-permute-start | bytes 393224 | tf_op jit(solution)/shard_map/ppermute | solution.py:219
  85.9 5.5 %collective-permute-start.42 = (bf16[4,1,128,128]{3,2,1,0:T(8,128)(2,1)S(1)}, bf16[4,1,128,128]{3,2,1,0:T(8,128)(2,1)S(1)}, u32[]{:S(2)}, u32[]{:S(2)}) collective-permute-start(bf16[4,1,128,128]{3,2,1,0:T(8,128)(2,1)S(1)} %constant_dynamic-update-slice_fusion.12.refs_0_), channel_id=1, source_target_pairs={{0,4},{1,3},{2,6},{3,1},{4,0},{5,7},{6,2},{7,5},{8,12},{9,11},{10,... | collective-permute-start | bytes 393224 | tf_op jit(solution)/shard_map/ppermute | solution.py:219
  87.0 5.3 %collective-permute-start.41 = (bf16[4,1,128,128]{3,2,1,0:T(8,128)(2,1)S(1)}, bf16[4,1,128,128]{3,2,1,0:T(8,128)(2,1)S(1)}, u32[]{:S(2)}, u32[]{:S(2)}) collective-permute-start(bf16[4,1,128,128]{3,2,1,0:T(8,128)(2,1)S(1)} %constant_dynamic-update-slice_fusion.12.refs_0_), channel_id=1, source_target_pairs={{0,1},{1,0},{2,3},{3,2},{4,5},{5,4},{6,7},{7,6},{8,9},{9,8},{10,11... | collective-permute-start | bytes 393224 | tf_op jit(solution)/shard_map/ppermute | solution.py:203
  93.3 6.8 %collective-permute-start.49 = (bf16[1,2,128,128]{3,2,1,0:T(8,128)(2,1)S(1)}, bf16[1,2,128,128]{3,2,1,0:T(8,128)(2,1)S(1)}, u32[]{:S(2)}, u32[]{:S(2)}) collective-permute-start(bf16[1,2,128,128]{3,2,1,0:T(8,128)(2,1)S(1)} %bitcast.42), channel_id=1, source_target_pairs={{0,16},{1,17},{2,18},{3,19},{4,20},{5,21},{6,22},{7,23},{8,24},{9,... | collective-permute-start | bytes 196616 | tf_op jit(solution)/shard_map/ppermute | solution.py:213
  95.3 5.3 %collective-permute-start.48 = (bf16[1,2,128,128]{3,2,1,0:T(8,128)(2,1)S(1)}, bf16[1,2,128,128]{3,2,1,0:T(8,128)(2,1)S(1)}, u32[]{:S(2)}, u32[]{:S(2)}) collective-permute-start(bf16[1,2,128,128]{3,2,1,0:T(8,128)(2,1)S(1)} %bitcast.43), channel_id=1, source_target_pairs={{0,24},{1,25},{2,26},{3,27},{4,28},{5,29},{6,30},{7,31},{8,0},{9,1... | collective-permute-start | bytes 196616 | tf_op jit(solution)/shard_map/ppermute | solution.py:213
  100.7 7.3 %collective-permute-start.55 = (bf16[2,2,128,128]{3,2,1,0:T(8,128)(2,1)S(1)}, bf16[2,2,128,128]{3,2,1,0:T(8,128)(2,1)S(1)}, u32[]{:S(2)}, u32[]{:S(2)}) collective-permute-start(bf16[2,2,128,128]{3,2,1,0:T(8,128)(2,1)S(1)} %get-tuple-element.99), channel_id=1, source_target_pairs={{0,6},{1,7},{2,4},{3,5},{4,2},{5,3},{6,0},{7,1},{8,14},{9,15},{10,... | collective-permute-start | bytes 393224 | tf_op jit(solution)/shard_map/ppermute | solution.py:219
  102.2 6.7 %collective-permute-start.53 = (bf16[2,2,128,128]{3,2,1,0:T(8,128)(2,1)S(1)}, bf16[2,2,128,128]{3,2,1,0:T(8,128)(2,1)S(1)}, u32[]{:S(2)}, u32[]{:S(2)}) collective-permute-start(bf16[2,2,128,128]{3,2,1,0:T(8,128)(2,1)S(1)} %get-tuple-element.100), channel_id=1, source_target_pairs={{0,2},{1,5},{2,0},{3,7},{4,6},{5,1},{6,4},{7,3},{8,10},{9,13},{10,... | collective-permute-start | bytes 393224 | tf_op jit(solution)/shard_map/ppermute | solution.py:219
  103.2 6.0 %collective-permute-start.51 = (bf16[2,2,128,128]{3,2,1,0:T(8,128)(2,1)S(1)}, bf16[2,2,128,128]{3,2,1,0:T(8,128)(2,1)S(1)}, u32[]{:S(2)}, u32[]{:S(2)}) collective-permute-start(bf16[2,2,128,128]{3,2,1,0:T(8,128)(2,1)S(1)} %get-tuple-element.101), channel_id=1, source_target_pairs={{0,4},{1,3},{2,6},{3,1},{4,0},{5,7},{6,2},{7,5},{8,12},{9,11},{10,... | collective-permute-start | bytes 393224 | tf_op jit(solution)/shard_map/ppermute | solution.py:219
  104.3 5.7 %collective-permute-start.50 = (bf16[2,2,128,128]{3,2,1,0:T(8,128)(2,1)S(1)}, bf16[2,2,128,128]{3,2,1,0:T(8,128)(2,1)S(1)}, u32[]{:S(2)}, u32[]{:S(2)}) collective-permute-start(bf16[2,2,128,128]{3,2,1,0:T(8,128)(2,1)S(1)} %get-tuple-element.102), channel_id=1, source_target_pairs={{0,1},{1,0},{2,3},{3,2},{4,5},{5,4},{6,7},{7,6},{8,9},{9,8},{10,11... | collective-permute-start | bytes 393224 | tf_op jit(solution)/shard_map/ppermute | solution.py:203
  (26 other events, 73.8 us)

commit v7 on v6

--- a/solution.py
+++ b/solution.py
@@ -252,7 +252,7 @@
     return in_plane(parts, direction), packed
 
 
-def copy_window(side, pieces, xs, block, start, direction):
+def copy_window(side, pieces, xs, block, start, direction, stream):
     me = lax.axis_index("prow")
     offset, parity = me & (PLANE - 1), (me & 1) ^ side
     size, lines = xs.shape[0], PLANE // 2
@@ -266,7 +266,7 @@
             source = 2 * (pair + slot) + parity
             apart = direction * (block // PLANE - source // PLANE)
             apart = jnp.clip(apart - skipped, 0, piece.shape[0] - 1)
-            level = source // (PLANE * PLANES) if piece.shape[1] > 1 else 0
+            level = source // (PLANE * PLANES) if stream is None else stream
             at = pl.multiple_of(slot * size, size)
             xs[:, pl.ds(at, size)] = piece[apart, level]
 
@@ -280,9 +280,13 @@
     size, half = xs.shape[0], SPAN // 2
     block = row * PLANE * PLANES + me
     start = window_start(block, direction, rows * PLANE * PLANES)
-    copy_window(side, pieces, xs, block, start, direction)
     at = row * SPAN + side * half
-    return dot(xs[...], factor[at : at + half].reshape(half * size, size))
+    result = None
+    for stream in range(pieces[0].shape[1]) if rows == 1 else (None,):
+        copy_window(side, pieces, xs, block, start, direction, stream)
+        term = dot(xs[...], factor[at : at + half].reshape(half * size, size))
+        result = term if result is None else result + term
+    return result
 
 
 def window_own_kernel(direction, *refs):
@@ -462,9 +466,9 @@
     places = [0] + [TURNS[1].index(k) + 1 for k in TURNS[0]]
     sums = [sums[1][m] + other[place] for m, place in enumerate(places)]
     arrived = [in_turn(sums[m + 1], pair) for m, pair in enumerate(zip(*TURNS, strict=True))]
-    coupling = (sums[0] + arrived[0] + arrived[1] + arrived[2]).astype(bf16).astype(f32)
-    difference = (own[2:].astype(f32) - coupling).astype(bf16)
-    pieces, packed = gather(difference, forward, level(lower, forward, 1))
+    coupling = (sums[0] + arrived[0] + arrived[1] + arrived[2]).astype(bf16)
+    streams = jnp.concatenate([own[2:], -coupling[None]], 0)
+    pieces, packed = gather(streams, forward, level(lower, forward, 1))
     forward_upper, upper_known = window("forward_upper", 1, forward, pieces, packed)
     upper_known, solved_now, upper_now = barrier((upper_known, solved, forward_upper))
     parts = along_z(upper_known, backward)

time: 112 us -> 115 us (1.027)
  waiting for transfers between devices: 41.7 us -> 43.5 us
    ppermute x21, waiting for transfers between devices: 29.5 us -> 31.3 us  [in_turn(): return lax.ppermute(value, 'prow', pairs)]
  transfers between devices with their start and end apart: 57 -> 57, of which waited for: 33 -> 36; matrix products, arithmetic and copies ran while one was open for 1% -> 1% of each run, Pallas kernels for 14% -> 13%
where the time goes in v7:
time: 115 us
  starting transfers between devices  48.7 us (42%)
  waiting for transfers between devices  43.5 us (38%)
  Pallas kernels  19.1 us (17%)
  local copies, waits for them, and re-layouts  1.16 us (1%)
    ppermute x21, waiting for transfers between devices, in_turn(): return lax.ppermute(value, 'prow', pairs)  31.3 us
    ppermute x21, starting transfers between devices, in_turn(): return lax.ppermute(value, 'prow', pairs)  24.9 us
    ppermute x8, starting transfers between devices, along_z(): parts.append(lax.ppermute(block[None], 'prow', pairs))  14 us
    ppermute x28, starting transfers between devices, swap(): lax.ppermute(value, 'prow', [(i, i ^ distance) for i in range(PLANE * PLA...  9.71 us
    pallas_call x14, Pallas kernels, local_call(): pl.pallas_call(kernel, out_shape=outs, in_specs=[pl.BlockSpec(memory_spac...  8.35 us
    pallas_call x4, Pallas kernels, pack_call(): pl.pallas_call(kernel, out_shape=jax.ShapeDtypeStruct((blocks, size, size...  7.63 us
    ppermute x8, waiting for transfers between devices, along_z(): parts.append(lax.ppermute(block[None], 'prow', pairs))  6.18 us
    ppermute x28, waiting for transfers between devices, swap(): lax.ppermute(value, 'prow', [(i, i ^ distance) for i in range(PLANE * PLA...  6.01 us
  transfers between devices with their start and end apart: 57, of which 36 were waited for; matrix products, arithmetic and copies ran while one was open for 1% of the time, Pallas kernels for 13%

profile of v7, /device:TPU:0, one launch (start us, length us, event | category | flops | bytes accessed | tf_op | source)
XLA Modules:
  0.0 114.6 jit_solution(10680443328266869883)
XLA Ops:
  1.7 4.1 %collective-permute-start.1 = (bf16[1,2,128,128]{3,2,1,0:T(8,128)(2,1)S(1)}, bf16[1,2,128,128]{3,2,1,0:T(8,128)(2,1)S(1)}, u32[]{:S(2)}, u32[]{:S(2)}) collective-permute-start(bf16[1,2,128,128]{3,2,1,0:T(8,128)(2,1)S(1)} %get-tuple-element.50), channel_id=1, source_target_pairs={{0,16},{1,17},{2,18},{3,19},{4,20},{5,21},{6,22},{7,23},{8,24},{9,... | collective-permute-start | bytes 196616 | tf_op jit(solution)/shard_map/ppermute | solution.py:213
  5.8 1.6 %collective-permute-start = (bf16[1,2,128,128]{3,2,1,0:T(8,128)(2,1)S(1)}, bf16[1,2,128,128]{3,2,1,0:T(8,128)(2,1)S(1)}, u32[]{:S(2)}, u32[]{:S(2)}) collective-permute-start(bf16[1,2,128,128]{3,2,1,0:T(8,128)(2,1)S(1)} %get-tuple-element.50), channel_id=1, source_target_pairs={{0,8},{1,9},{2,10},{3,11},{4,12},{5,13},{6,14},{7,15},{8,16},{9,17... | collective-permute-start | bytes 196616 | tf_op jit(solution)/shard_map/ppermute | solution.py:213
  8.1 3.1 %first_pack.1 = (bf16[32,128,128]{2,1,0:T(8,128)(2,1)S(1)}, bf16[16,128,128]{2,1,0:T(8,128)(2,1)S(1)}, bf16[16,128,128]{2,1,0:T(8,128)(2,1)S(1)}, s32[32]{0:T(128)S(1)}) custom-call(bf16[48,2,3,128,128]{4,3,2,1,0:T(8,128)(2,1)} %bitcast.59, bf16[2,128,128]{2,1,0:T(8,128)(2,1)S(1)} %get-tuple-element.115.after, s32[8,128]{1,0:T(8,128)S(1)} %pad_add_fusion.rules), custom_call_target="tpu_custom_call" | custom-call | bytes 4194304 | tf_op jit(solution)/shard_map/first_pack/pallas_call | solution.py:184
  11.9 2.5 %collective-permute-start.7 = (bf16[2,2,128,128]{3,2,1,0:T(8,128)(2,1)S(1)}, bf16[2,2,128,128]{3,2,1,0:T(8,128)(2,1)S(1)}, u32[]{:S(2)}, u32[]{:S(2)}) collective-permute-start(bf16[2,2,128,128]{3,2,1,0:T(8,128)(2,1)S(1)} %get-tuple-element.107), channel_id=1, source_target_pairs={{0,6},{1,7},{2,4},{3,5},{4,2},{5,3},{6,0},{7,1},{8,14},{9,15},{10,... | collective-permute-start | bytes 393224 | tf_op jit(solution)/shard_map/ppermute | solution.py:219
  15.5 3.1 %collective-permute-done.7.refs_3_ = bf16[2,2,128,128]{3,2,1,0:T(8,128)(2,1)S(1)} collective-permute-done((bf16[2,2,128,128]{3,2,1,0:T(8,128)(2,1)S(1)}, bf16[2,2,128,128]{3,2,1,0:T(8,128)(2,1)S(1)}, u32[]{:S(2)}, u32[]{:S(2)}) %collective-permute-start.7) | collective-permute-done | bytes 131104 | tf_op jit(solution)/shard_map/ppermute | solution.py:219
  18.5 2.5 %collective-permute-done.5.refs_2_ = bf16[2,2,128,128]{3,2,1,0:T(8,128)(2,1)S(1)} collective-permute-done((bf16[2,2,128,128]{3,2,1,0:T(8,128)(2,1)S(1)}, bf16[2,2,128,128]{3,2,1,0:T(8,128)(2,1)S(1)}, u32[]{:S(2)}, u32[]{:S(2)}) %collective-permute-start.5) | collective-permute-done | bytes 131104 | tf_op jit(solution)/shard_map/ppermute | solution.py:219
  21.7 1.6 %collective-permute-start.12 = (bf16[8,128,128]{2,1,0:T(8,128)(2,1)S(1)}, bf16[8,128,128]{2,1,0:T(8,128)(2,1)S(1)}, u32[]{:S(2)}, u32[]{:S(2)}) collective-permute-start(bf16[8,128,128]{2,1,0:T(8,128)(2,1)S(1)} %get-tuple-element.97), channel_id=1, source_target_pairs={{0,2},{1,5},{2,0},{3,7},{4,6},{5,1},{6,4},{7,3},{8,10},{9,13},{10,... | collective-permute-start | bytes 786440 | tf_op jit(solution)/shard_map/ppermute | solution.py:219
  23.9 1.5 %collective-permute-start.13 = (bf16[8,128,128]{2,1,0:T(8,128)(2,1)S(1)}, bf16[8,128,128]{2,1,0:T(8,128)(2,1)S(1)}, u32[]{:S(2)}, u32[]{:S(2)}) collective-permute-start(bf16[8,128,128]{2,1,0:T(8,128)(2,1)S(1)} %pad_maximum_fusion.2), channel_id=1, source_target_pairs={{0,6},{1,7},{2,4},{3,5},{4,2},{5,3},{6,0},{7,1},{8,14},{9,15},{10,... | collective-permute-start | bytes 786440 | tf_op jit(solution)/shard_map/ppermute | solution.py:219
  26.6 2.7 %collective-permute-start.15 = (bf16[1,2,128,128]{3,2,1,0:T(8,128)(2,1)S(1)}, bf16[1,2,128,128]{3,2,1,0:T(8,128)(2,1)S(1)}, u32[]{:S(2)}, u32[]{:S(2)}) collective-permute-start(bf16[1,2,128,128]{3,2,1,0:T(8,128)(2,1)S(1)} %bitcast.53), channel_id=1, source_target_pairs={{0,24},{1,25},{2,26},{3,27},{4,28},{5,29},{6,30},{7,31},{8,16},{9,... | collective-permute-start | bytes 196616 | tf_op jit(solution)/shard_map/ppermute | solution.py:203
  29.2 2.3 %collective-permute-done.9 = bf16[1,2,128,128]{3,2,1,0:T(8,128)(2,1)S(1)} collective-permute-done((bf16[1,2,128,128]{3,2,1,0:T(8,128)(2,1)S(1)}, bf16[1,2,128,128]{3,2,1,0:T(8,128)(2,1)S(1)}, u32[]{:S(2)}, u32[]{:S(2)}) %collective-permute-start.9) | collective-permute-done | bytes 65568 | tf_op jit(solution)/shard_map/ppermute | solution.py:203
  32.1 4.8 %collective-permute-done.13.far = bf16[8,128,128]{2,1,0:T(8,128)(2,1)S(1)} collective-permute-done((bf16[8,128,128]{2,1,0:T(8,128)(2,1)S(1)}, bf16[8,128,128]{2,1,0:T(8,128)(2,1)S(1)}, u32[]{:S(2)}, u32[]{:S(2)}) %collective-permute-start.13) | collective-permute-done | bytes 262176 | tf_op jit(solution)/shard_map/ppermute | solution.py:219
  40.4 2.0 %collective-permute-start.19 = (f32[128,128]{1,0:T(8,128)S(1)}, f32[128,128]{1,0:T(8,128)S(1)}, u32[]{:S(2)}, u32[]{:S(2)}) collective-permute-start(f32[128,128]{1,0:T(8,128)S(1)} %get-tuple-element.89), channel_id=1, source_target_pairs={{0,6},{1,7},{2,4},{3,5},{4,2},{5,3},{6,0},{7,1},{8,14},{9,15},{10,... | collective-permute-start | bytes 196616 | tf_op jit(solution)/shard_map/ppermute | solution.py:219
  43.9 1.9 %collective-permute-done.19 = f32[128,128]{1,0:T(8,128)S(1)} collective-permute-done((f32[128,128]{1,0:T(8,128)S(1)}, f32[128,128]{1,0:T(8,128)S(1)}, u32[]{:S(2)}, u32[]{:S(2)}) %collective-permute-start.19) | collective-permute-done | bytes 65568 | tf_op jit(solution)/shard_map/ppermute | solution.py:219
  47.4 2.1 %collective-permute-start.20 = (bf16[1,2,128,128]{3,2,1,0:T(8,128)(2,1)S(1)}, bf16[1,2,128,128]{3,2,1,0:T(8,128)(2,1)S(1)}, u32[]{:S(2)}, u32[]{:S(2)}) collective-permute-start(bf16[1,2,128,128]{3,2,1,0:T(8,128)(2,1)S(1)} %get-tuple-element.64), channel_id=1, source_target_pairs={{0,8},{1,9},{2,10},{3,11},{4,12},{5,13},{6,14},{7,15},{8,16},{9,17... | collective-permute-start | bytes 196616 | tf_op jit(solution)/shard_map/ppermute | solution.py:213
  49.5 1.7 %pack_level.3.refs_4_ = bf16[16,128,128]{2,1,0:T(8,128)(2,1)S(1)} custom-call(bf16[48,2,3,128,128]{4,3,2,1,0:T(8,128)(2,1)} %bitcast.60, bf16[2,128,128]{2,1,0:T(8,128)(2,1)S(1)} %get-tuple-element.121.after, s32[8,128]{1,0:T(8,128)S(1)} %pad_add_fusion.rules), custom_call_target="tpu_custom_call" | custom-call | bytes 1048576 | tf_op jit(solution)/shard_map/pack_level/pallas_call | solution.py:100
  51.3 2.5 %collective-permute-done.21 = bf16[1,2,128,128]{3,2,1,0:T(8,128)(2,1)S(1)} collective-permute-done((bf16[1,2,128,128]{3,2,1,0:T(8,128)(2,1)S(1)}, bf16[1,2,128,128]{3,2,1,0:T(8,128)(2,1)S(1)}, u32[]{:S(2)}, u32[]{:S(2)}) %collective-permute-start.21) | collective-permute-done | bytes 65568 | tf_op jit(solution)/shard_map/ppermute | solution.py:213
  53.9 1.5 %collective-permute-start.27 = (bf16[2,2,128,128]{3,2,1,0:T(8,128)(2,1)S(1)}, bf16[2,2,128,128]{3,2,1,0:T(8,128)(2,1)S(1)}, u32[]{:S(2)}, u32[]{:S(2)}) collective-permute-start(bf16[2,2,128,128]{3,2,1,0:T(8,128)(2,1)S(1)} %get-tuple-element.103), channel_id=1, source_target_pairs={{0,6},{1,7},{2,4},{3,5},{4,2},{5,3},{6,0},{7,1},{8,14},{9,15},{10,... | collective-permute-start | bytes 393224 | tf_op jit(solution)/shard_map/ppermute | solution.py:219
  57.4 3.6 %collective-permute-done.27.refs_3_ = bf16[2,2,128,128]{3,2,1,0:T(8,128)(2,1)S(1)} collective-permute-done((bf16[2,2,128,128]{3,2,1,0:T(8,128)(2,1)S(1)}, bf16[2,2,128,128]{3,2,1,0:T(8,128)(2,1)S(1)}, u32[]{:S(2)}, u32[]{:S(2)}) %collective-permute-start.27) | collective-permute-done | bytes 131104 | tf_op jit(solution)/shard_map/ppermute | solution.py:219
  64.0 2.1 %collective-permute-start.30 = (bf16[1,1,128,128]{3,2,1,0:T(8,128)(2,1)S(1)}, bf16[1,1,128,128]{3,2,1,0:T(8,128)(2,1)S(1)}, u32[]{:S(2)}, u32[]{:S(2)}) collective-permute-start(bf16[1,1,128,128]{3,2,1,0:T(8,128)(2,1)S(1)} %bitcast.44), channel_id=1, source_target_pairs={{0,16},{1,17},{2,18},{3,19},{4,20},{5,21},{6,22},{7,23},{8,24},{9,... | collective-permute-start | bytes 98312 | tf_op jit(solution)/shard_map/ppermute | solution.py:213
  66.5 1.7 %pack_level.4.refs_4_ = bf16[16,128,128]{2,1,0:T(8,128)(2,1)S(1)} custom-call(bf16[48,2,3,128,128]{4,3,2,1,0:T(8,128)(2,1)} %bitcast.56, bf16[1,128,128]{2,1,0:T(8,128)(2,1)S(1)} %get-tuple-element.69.after, s32[8,128]{1,0:T(8,128)S(1)} %pad_add_fusion.rules), custom_call_target="tpu_custom_call" | custom-call | bytes 1048576 | tf_op jit(solution)/shard_map/pack_level/pallas_call | solution.py:100
  70.1 1.8 %collective-permute-start.36 = (bf16[2,1,128,128]{3,2,1,0:T(8,128)(2,1)S(1)}, bf16[2,1,128,128]{3,2,1,0:T(8,128)(2,1)S(1)}, u32[]{:S(2)}, u32[]{:S(2)}) collective-permute-start(bf16[2,1,128,128]{3,2,1,0:T(8,128)(2,1)S(1)} %get-tuple-element.111), channel_id=1, source_target_pairs={{0,6},{1,7},{2,4},{3,5},{4,2},{5,3},{6,0},{7,1},{8,14},{9,15},{10,... | collective-permute-start | bytes 196616 | tf_op jit(solution)/shard_map/ppermute | solution.py:219
  73.6 2.4 %collective-permute-done.36.refs_3_ = bf16[2,1,128,128]{3,2,1,0:T(8,128)(2,1)S(1)} collective-permute-done((bf16[2,1,128,128]{3,2,1,0:T(8,128)(2,1)S(1)}, bf16[2,1,128,128]{3,2,1,0:T(8,128)(2,1)S(1)}, u32[]{:S(2)}, u32[]{:S(2)}) %collective-permute-start.36) | collective-permute-done | bytes 65568 | tf_op jit(solution)/shard_map/ppermute | solution.py:219
  78.4 2.5 %collective-permute-start.40 = (bf16[1,1,128,128]{3,2,1,0:T(8,128)(2,1)S(1)}, bf16[1,1,128,128]{3,2,1,0:T(8,128)(2,1)S(1)}, u32[]{:S(2)}, u32[]{:S(2)}) collective-permute-start(bf16[1,1,128,128]{3,2,1,0:T(8,128)(2,1)S(1)} %bitcast.48), channel_id=1, source_target_pairs={{0,24},{1,25},{2,26},{3,27},{4,28},{5,29},{6,30},{7,31},{8,16},{9,... | collective-permute-start | bytes 98312 | tf_op jit(solution)/shard_map/ppermute | solution.py:203
  80.9 1.9 %collective-permute-start.38 = (bf16[1,1,128,128]{3,2,1,0:T(8,128)(2,1)S(1)}, bf16[1,1,128,128]{3,2,1,0:T(8,128)(2,1)S(1)}, u32[]{:S(2)}, u32[]{:S(2)}) collective-permute-start(bf16[1,1,128,128]{3,2,1,0:T(8,128)(2,1)S(1)} %bitcast.50), channel_id=1, source_target_pairs={{0,8},{1,9},{2,10},{3,11},{4,12},{5,13},{6,14},{7,15},{8,0},{9,1},... | collective-permute-start | bytes 98312 | tf_op jit(solution)/shard_map/ppermute | solution.py:203
  82.8 2.3 %pack_up.1.refs_4_ = bf16[64,128,128]{2,1,0:T(8,128)(2,1)S(1)} custom-call(bf16[48,2,3,128,128]{4,3,2,1,0:T(8,128)(2,1)} %bitcast.57, bf16[1,128,128]{2,1,0:T(8,128)(2,1)S(1)} %get-tuple-element.77.after, s32[8,128]{1,0:T(8,128)S(1)} %pad_add_fusion.rules), custom_call_target="tpu_custom_call" | custom-call | bytes 4194304 | tf_op jit(solution)/shard_map/pack_up/pallas_call | solution.py:100
  85.7 1.5 %collective-permute-start.46 = (bf16[4,1,128,128]{3,2,1,0:T(8,128)(2,1)S(1)}, bf16[4,1,128,128]{3,2,1,0:T(8,128)(2,1)S(1)}, u32[]{:S(2)}, u32[]{:S(2)}) collective-permute-start(bf16[4,1,128,128]{3,2,1,0:T(8,128)(2,1)S(1)} %constant_dynamic-update-slice_fusion.12.refs_0_), channel_id=1, source_target_pairs={{0,6},{1,7},{2,4},{3,5},{4,2},{5,3},{6,0},{7,1},{8,14},{9,15},{10,... | collective-permute-start | bytes 393224 | tf_op jit(solution)/shard_map/ppermute | solution.py:219
  89.3 3.6 %collective-permute-done.46.refs_3_ = bf16[4,1,128,128]{3,2,1,0:T(8,128)(2,1)S(1)} collective-permute-done((bf16[4,1,128,128]{3,2,1,0:T(8,128)(2,1)S(1)}, bf16[4,1,128,128]{3,2,1,0:T(8,128)(2,1)S(1)}, u32[]{:S(2)}, u32[]{:S(2)}) %collective-permute-start.46) | collective-permute-done | bytes 131104 | tf_op jit(solution)/shard_map/ppermute | solution.py:219
  96.0 1.5 %collective-permute-start.49 = (bf16[1,2,128,128]{3,2,1,0:T(8,128)(2,1)S(1)}, bf16[1,2,128,128]{3,2,1,0:T(8,128)(2,1)S(1)}, u32[]{:S(2)}, u32[]{:S(2)}) collective-permute-start(bf16[1,2,128,128]{3,2,1,0:T(8,128)(2,1)S(1)} %bitcast.40), channel_id=1, source_target_pairs={{0,16},{1,17},{2,18},{3,19},{4,20},{5,21},{6,22},{7,23},{8,24},{9,... | collective-permute-start | bytes 196616 | tf_op jit(solution)/shard_map/ppermute | solution.py:213
  99.0 1.9 %pack_level.5.refs_4_ = bf16[32,128,128]{2,1,0:T(8,128)(2,1)S(1)} custom-call(bf16[48,2,3,128,128]{4,3,2,1,0:T(8,128)(2,1)} %bitcast.58, bf16[2,128,128]{2,1,0:T(8,128)(2,1)S(1)} %correction.1.after, s32[8,128]{1,0:T(8,128)S(1)} %pad_add_fusion.rules), custom_call_target="tpu_custom_call" | custom-call | bytes 2097152 | tf_op jit(solution)/shard_map/pack_level/pallas_call | solution.py:100
  100.9 1.8 %collective-permute-done.49 = bf16[1,2,128,128]{3,2,1,0:T(8,128)(2,1)S(1)} collective-permute-done((bf16[1,2,128,128]{3,2,1,0:T(8,128)(2,1)S(1)}, bf16[1,2,128,128]{3,2,1,0:T(8,128)(2,1)S(1)}, u32[]{:S(2)}, u32[]{:S(2)}) %collective-permute-start.49) | collective-permute-done | bytes 65568 | tf_op jit(solution)/shard_map/ppermute | solution.py:213
  103.2 1.6 %collective-permute-start.55 = (bf16[2,2,128,128]{3,2,1,0:T(8,128)(2,1)S(1)}, bf16[2,2,128,128]{3,2,1,0:T(8,128)(2,1)S(1)}, u32[]{:S(2)}, u32[]{:S(2)}) collective-permute-start(bf16[2,2,128,128]{3,2,1,0:T(8,128)(2,1)S(1)} %get-tuple-element.99), channel_id=1, source_target_pairs={{0,6},{1,7},{2,4},{3,5},{4,2},{5,3},{6,0},{7,1},{8,14},{9,15},{10,... | collective-permute-start | bytes 393224 | tf_op jit(solution)/shard_map/ppermute | solution.py:219
  106.8 3.6 %collective-permute-done.55.refs_3_ = bf16[2,2,128,128]{3,2,1,0:T(8,128)(2,1)S(1)} collective-permute-done((bf16[2,2,128,128]{3,2,1,0:T(8,128)(2,1)S(1)}, bf16[2,2,128,128]{3,2,1,0:T(8,128)(2,1)S(1)}, u32[]{:S(2)}, u32[]{:S(2)}) %collective-permute-start.55) | collective-permute-done | bytes 131104 | tf_op jit(solution)/shard_map/ppermute | solution.py:219
  (138 shorter events, 38.4 us)
Async XLA Ops:
  1.7 9.6 %collective-permute-start.1 = (bf16[1,2,128,128]{3,2,1,0:T(8,128)(2,1)S(1)}, bf16[1,2,128,128]{3,2,1,0:T(8,128)(2,1)S(1)}, u32[]{:S(2)}, u32[]{:S(2)}) collective-permute-start(bf16[1,2,128,128]{3,2,1,0:T(8,128)(2,1)S(1)} %get-tuple-element.50), channel_id=1, source_target_pairs={{0,16},{1,17},{2,18},{3,19},{4,20},{5,21},{6,22},{7,23},{8,24},{9,... | collective-permute-start | bytes 196616 | tf_op jit(solution)/shard_map/ppermute | solution.py:213
  5.8 6.1 %collective-permute-start = (bf16[1,2,128,128]{3,2,1,0:T(8,128)(2,1)S(1)}, bf16[1,2,128,128]{3,2,1,0:T(8,128)(2,1)S(1)}, u32[]{:S(2)}, u32[]{:S(2)}) collective-permute-start(bf16[1,2,128,128]{3,2,1,0:T(8,128)(2,1)S(1)} %get-tuple-element.50), channel_id=1, source_target_pairs={{0,8},{1,9},{2,10},{3,11},{4,12},{5,13},{6,14},{7,15},{8,16},{9,17... | collective-permute-start | bytes 196616 | tf_op jit(solution)/shard_map/ppermute | solution.py:213
  11.2 10.5 %collective-permute-start.10 = (bf16[16,128,128]{2,1,0:T(8,128)(2,1)S(1)}, bf16[16,128,128]{2,1,0:T(8,128)(2,1)S(1)}, u32[]{:S(2)}, u32[]{:S(2)}) collective-permute-start(bf16[16,128,128]{2,1,0:T(8,128)(2,1)S(1)} %get-tuple-element.56), channel_id=1, source_target_pairs={{0,1},{1,0},{2,3},{3,2},{4,5},{5,4},{6,7},{7,6},{8,9},{9,8},{10,11... | collective-permute-start | bytes 1572872 | tf_op jit(solution)/shard_map/ppermute | solution.py:203
  11.9 6.6 %collective-permute-start.7 = (bf16[2,2,128,128]{3,2,1,0:T(8,128)(2,1)S(1)}, bf16[2,2,128,128]{3,2,1,0:T(8,128)(2,1)S(1)}, u32[]{:S(2)}, u32[]{:S(2)}) collective-permute-start(bf16[2,2,128,128]{3,2,1,0:T(8,128)(2,1)S(1)} %get-tuple-element.107), channel_id=1, source_target_pairs={{0,6},{1,7},{2,4},{3,5},{4,2},{5,3},{6,0},{7,1},{8,14},{9,15},{10,... | collective-permute-start | bytes 393224 | tf_op jit(solution)/shard_map/ppermute | solution.py:219
  14.4 6.6 %collective-permute-start.5 = (bf16[2,2,128,128]{3,2,1,0:T(8,128)(2,1)S(1)}, bf16[2,2,128,128]{3,2,1,0:T(8,128)(2,1)S(1)}, u32[]{:S(2)}, u32[]{:S(2)}) collective-permute-start(bf16[2,2,128,128]{3,2,1,0:T(8,128)(2,1)S(1)} %get-tuple-element.108), channel_id=1, source_target_pairs={{0,2},{1,5},{2,0},{3,7},{4,6},{5,1},{6,4},{7,3},{8,10},{9,13},{10,... | collective-permute-start | bytes 393224 | tf_op jit(solution)/shard_map/ppermute | solution.py:219
  15.0 6.1 %collective-permute-start.3 = (bf16[2,2,128,128]{3,2,1,0:T(8,128)(2,1)S(1)}, bf16[2,2,128,128]{3,2,1,0:T(8,128)(2,1)S(1)}, u32[]{:S(2)}, u32[]{:S(2)}) collective-permute-start(bf16[2,2,128,128]{3,2,1,0:T(8,128)(2,1)S(1)} %get-tuple-element.109), channel_id=1, source_target_pairs={{0,4},{1,3},{2,6},{3,1},{4,0},{5,7},{6,2},{7,5},{8,12},{9,11},{10,... | collective-permute-start | bytes 393224 | tf_op jit(solution)/shard_map/ppermute | solution.py:219
  15.5 7.9 %collective-permute-start.2 = (bf16[2,2,128,128]{3,2,1,0:T(8,128)(2,1)S(1)}, bf16[2,2,128,128]{3,2,1,0:T(8,128)(2,1)S(1)}, u32[]{:S(2)}, u32[]{:S(2)}) collective-permute-start(bf16[2,2,128,128]{3,2,1,0:T(8,128)(2,1)S(1)} %get-tuple-element.110), channel_id=1, source_target_pairs={{0,1},{1,0},{2,3},{3,2},{4,5},{5,4},{6,7},{7,6},{8,9},{9,8},{10,11... | collective-permute-start | bytes 393224 | tf_op jit(solution)/shard_map/ppermute | solution.py:203
  18.5 5.4 %collective-permute-start.8 = (bf16[2,2,128,128]{3,2,1,0:T(8,128)(2,1)S(1)}, bf16[2,2,128,128]{3,2,1,0:T(8,128)(2,1)S(1)}, u32[]{:S(2)}, u32[]{:S(2)}) collective-permute-start(bf16[2,2,128,128]{3,2,1,0:T(8,128)(2,1)S(1)} %collective-permute-done.7.refs_3_), channel_id=1, source_target_pairs={{0,1},{1,0},{2,3},{3,2},{4,5},{5,4},{6,7},{7,6},{8,9},{9,8},{10,11... | collective-permute-start | bytes 393224 | tf_op jit(solution)/shard_map/ppermute | solution.py:203
  21.7 10.4 %collective-permute-start.12 = (bf16[8,128,128]{2,1,0:T(8,128)(2,1)S(1)}, bf16[8,128,128]{2,1,0:T(8,128)(2,1)S(1)}, u32[]{:S(2)}, u32[]{:S(2)}) collective-permute-start(bf16[8,128,128]{2,1,0:T(8,128)(2,1)S(1)} %get-tuple-element.97), channel_id=1, source_target_pairs={{0,2},{1,5},{2,0},{3,7},{4,6},{5,1},{6,4},{7,3},{8,10},{9,13},{10,... | collective-permute-start | bytes 786440 | tf_op jit(solution)/shard_map/ppermute | solution.py:219
  23.4 8.8 %collective-permute-start.11 = (bf16[8,128,128]{2,1,0:T(8,128)(2,1)S(1)}, bf16[8,128,128]{2,1,0:T(8,128)(2,1)S(1)}, u32[]{:S(2)}, u32[]{:S(2)}) collective-permute-start(bf16[8,128,128]{2,1,0:T(8,128)(2,1)S(1)} %get-tuple-element.98), channel_id=1, source_target_pairs={{0,4},{1,3},{2,6},{3,1},{4,0},{5,7},{6,2},{7,5},{8,12},{9,11},{10,... | collective-permute-start | bytes 786440 | tf_op jit(solution)/shard_map/ppermute | solution.py:219
  23.9 13.0 %collective-permute-start.13 = (bf16[8,128,128]{2,1,0:T(8,128)(2,1)S(1)}, bf16[8,128,128]{2,1,0:T(8,128)(2,1)S(1)}, u32[]{:S(2)}, u32[]{:S(2)}) collective-permute-start(bf16[8,128,128]{2,1,0:T(8,128)(2,1)S(1)} %pad_maximum_fusion.2), channel_id=1, source_target_pairs={{0,6},{1,7},{2,4},{3,5},{4,2},{5,3},{6,0},{7,1},{8,14},{9,15},{10,... | collective-permute-start | bytes 786440 | tf_op jit(solution)/shard_map/ppermute | solution.py:219
  26.6 10.3 %collective-permute-start.15 = (bf16[1,2,128,128]{3,2,1,0:T(8,128)(2,1)S(1)}, bf16[1,2,128,128]{3,2,1,0:T(8,128)(2,1)S(1)}, u32[]{:S(2)}, u32[]{:S(2)}) collective-permute-start(bf16[1,2,128,128]{3,2,1,0:T(8,128)(2,1)S(1)} %bitcast.53), channel_id=1, source_target_pairs={{0,24},{1,25},{2,26},{3,27},{4,28},{5,29},{6,30},{7,31},{8,16},{9,... | collective-permute-start | bytes 196616 | tf_op jit(solution)/shard_map/ppermute | solution.py:203
  31.5 5.4 %collective-permute-start.14 = (bf16[1,2,128,128]{3,2,1,0:T(8,128)(2,1)S(1)}, bf16[1,2,128,128]{3,2,1,0:T(8,128)(2,1)S(1)}, u32[]{:S(2)}, u32[]{:S(2)}) collective-permute-start(bf16[1,2,128,128]{3,2,1,0:T(8,128)(2,1)S(1)} %bitcast.54), channel_id=1, source_target_pairs={{0,16},{1,17},{2,18},{3,19},{4,20},{5,21},{6,22},{7,23},{8,24},{9,... | collective-permute-start | bytes 196616 | tf_op jit(solution)/shard_map/ppermute | solution.py:203
  40.4 5.4 %collective-permute-start.19 = (f32[128,128]{1,0:T(8,128)S(1)}, f32[128,128]{1,0:T(8,128)S(1)}, u32[]{:S(2)}, u32[]{:S(2)}) collective-permute-start(f32[128,128]{1,0:T(8,128)S(1)} %get-tuple-element.89), channel_id=1, source_target_pairs={{0,6},{1,7},{2,4},{3,5},{4,2},{5,3},{6,0},{7,1},{8,14},{9,15},{10,... | collective-permute-start | bytes 196616 | tf_op jit(solution)/shard_map/ppermute | solution.py:219
  46.7 7.1 %collective-permute-start.21 = (bf16[1,2,128,128]{3,2,1,0:T(8,128)(2,1)S(1)}, bf16[1,2,128,128]{3,2,1,0:T(8,128)(2,1)S(1)}, u32[]{:S(2)}, u32[]{:S(2)}) collective-permute-start(bf16[1,2,128,128]{3,2,1,0:T(8,128)(2,1)S(1)} %get-tuple-element.64), channel_id=1, source_target_pairs={{0,16},{1,17},{2,18},{3,19},{4,20},{5,21},{6,22},{7,23},{8,24},{9,... | collective-permute-start | bytes 196616 | tf_op jit(solution)/shard_map/ppermute | solution.py:213
  47.4 6.3 %collective-permute-start.20 = (bf16[1,2,128,128]{3,2,1,0:T(8,128)(2,1)S(1)}, bf16[1,2,128,128]{3,2,1,0:T(8,128)(2,1)S(1)}, u32[]{:S(2)}, u32[]{:S(2)}) collective-permute-start(bf16[1,2,128,128]{3,2,1,0:T(8,128)(2,1)S(1)} %get-tuple-element.64), channel_id=1, source_target_pairs={{0,8},{1,9},{2,10},{3,11},{4,12},{5,13},{6,14},{7,15},{8,16},{9,17... | collective-permute-start | bytes 196616 | tf_op jit(solution)/shard_map/ppermute | solution.py:213
  53.9 7.1 %collective-permute-start.27 = (bf16[2,2,128,128]{3,2,1,0:T(8,128)(2,1)S(1)}, bf16[2,2,128,128]{3,2,1,0:T(8,128)(2,1)S(1)}, u32[]{:S(2)}, u32[]{:S(2)}) collective-permute-start(bf16[2,2,128,128]{3,2,1,0:T(8,128)(2,1)S(1)} %get-tuple-element.103), channel_id=1, source_target_pairs={{0,6},{1,7},{2,4},{3,5},{4,2},{5,3},{6,0},{7,1},{8,14},{9,15},{10,... | collective-permute-start | bytes 393224 | tf_op jit(solution)/shard_map/ppermute | solution.py:219
  55.4 6.6 %collective-permute-start.25 = (bf16[2,2,128,128]{3,2,1,0:T(8,128)(2,1)S(1)}, bf16[2,2,128,128]{3,2,1,0:T(8,128)(2,1)S(1)}, u32[]{:S(2)}, u32[]{:S(2)}) collective-permute-start(bf16[2,2,128,128]{3,2,1,0:T(8,128)(2,1)S(1)} %get-tuple-element.104), channel_id=1, source_target_pairs={{0,2},{1,5},{2,0},{3,7},{4,6},{5,1},{6,4},{7,3},{8,10},{9,13},{10,... | collective-permute-start | bytes 393224 | tf_op jit(solution)/shard_map/ppermute | solution.py:219
  56.6 5.6 %collective-permute-start.23 = (bf16[2,2,128,128]{3,2,1,0:T(8,128)(2,1)S(1)}, bf16[2,2,128,128]{3,2,1,0:T(8,128)(2,1)S(1)}, u32[]{:S(2)}, u32[]{:S(2)}) collective-permute-start(bf16[2,2,128,128]{3,2,1,0:T(8,128)(2,1)S(1)} %get-tuple-element.105), channel_id=1, source_target_pairs={{0,4},{1,3},{2,6},{3,1},{4,0},{5,7},{6,2},{7,5},{8,12},{9,11},{10,... | collective-permute-start | bytes 393224 | tf_op jit(solution)/shard_map/ppermute | solution.py:219
  57.4 5.6 %collective-permute-start.22 = (bf16[2,2,128,128]{3,2,1,0:T(8,128)(2,1)S(1)}, bf16[2,2,128,128]{3,2,1,0:T(8,128)(2,1)S(1)}, u32[]{:S(2)}, u32[]{:S(2)}) collective-permute-start(bf16[2,2,128,128]{3,2,1,0:T(8,128)(2,1)S(1)} %get-tuple-element.106), channel_id=1, source_target_pairs={{0,1},{1,0},{2,3},{3,2},{4,5},{5,4},{6,7},{7,6},{8,9},{9,8},{10,11... | collective-permute-start | bytes 393224 | tf_op jit(solution)/shard_map/ppermute | solution.py:203
  70.1 5.9 %collective-permute-start.36 = (bf16[2,1,128,128]{3,2,1,0:T(8,128)(2,1)S(1)}, bf16[2,1,128,128]{3,2,1,0:T(8,128)(2,1)S(1)}, u32[]{:S(2)}, u32[]{:S(2)}) collective-permute-start(bf16[2,1,128,128]{3,2,1,0:T(8,128)(2,1)S(1)} %get-tuple-element.111), channel_id=1, source_target_pairs={{0,6},{1,7},{2,4},{3,5},{4,2},{5,3},{6,0},{7,1},{8,14},{9,15},{10,... | collective-permute-start | bytes 196616 | tf_op jit(solution)/shard_map/ppermute | solution.py:219
  78.4 6.8 %collective-permute-start.40 = (bf16[1,1,128,128]{3,2,1,0:T(8,128)(2,1)S(1)}, bf16[1,1,128,128]{3,2,1,0:T(8,128)(2,1)S(1)}, u32[]{:S(2)}, u32[]{:S(2)}) collective-permute-start(bf16[1,1,128,128]{3,2,1,0:T(8,128)(2,1)S(1)} %bitcast.48), channel_id=1, source_target_pairs={{0,24},{1,25},{2,26},{3,27},{4,28},{5,29},{6,30},{7,31},{8,16},{9,... | collective-permute-start | bytes 98312 | tf_op jit(solution)/shard_map/ppermute | solution.py:203
  85.7 7.2 %collective-permute-start.46 = (bf16[4,1,128,128]{3,2,1,0:T(8,128)(2,1)S(1)}, bf16[4,1,128,128]{3,2,1,0:T(8,128)(2,1)S(1)}, u32[]{:S(2)}, u32[]{:S(2)}) collective-permute-start(bf16[4,1,128,128]{3,2,1,0:T(8,128)(2,1)S(1)} %constant_dynamic-update-slice_fusion.12.refs_0_), channel_id=1, source_target_pairs={{0,6},{1,7},{2,4},{3,5},{4,2},{5,3},{6,0},{7,1},{8,14},{9,15},{10,... | collective-permute-start | bytes 393224 | tf_op jit(solution)/shard_map/ppermute | solution.py:219
  87.3 6.6 %collective-permute-start.44 = (bf16[4,1,128,128]{3,2,1,0:T(8,128)(2,1)S(1)}, bf16[4,1,128,128]{3,2,1,0:T(8,128)(2,1)S(1)}, u32[]{:S(2)}, u32[]{:S(2)}) collective-permute-start(bf16[4,1,128,128]{3,2,1,0:T(8,128)(2,1)S(1)} %constant_dynamic-update-slice_fusion.12.refs_0_), channel_id=1, source_target_pairs={{0,2},{1,5},{2,0},{3,7},{4,6},{5,1},{6,4},{7,3},{8,10},{9,13},{10,... | collective-permute-start | bytes 393224 | tf_op jit(solution)/shard_map/ppermute | solution.py:219
  88.2 5.8 %collective-permute-start.42 = (bf16[4,1,128,128]{3,2,1,0:T(8,128)(2,1)S(1)}, bf16[4,1,128,128]{3,2,1,0:T(8,128)(2,1)S(1)}, u32[]{:S(2)}, u32[]{:S(2)}) collective-permute-start(bf16[4,1,128,128]{3,2,1,0:T(8,128)(2,1)S(1)} %constant_dynamic-update-slice_fusion.12.refs_0_), channel_id=1, source_target_pairs={{0,4},{1,3},{2,6},{3,1},{4,0},{5,7},{6,2},{7,5},{8,12},{9,11},{10,... | collective-permute-start | bytes 393224 | tf_op jit(solution)/shard_map/ppermute | solution.py:219
  89.3 5.7 %collective-permute-start.41 = (bf16[4,1,128,128]{3,2,1,0:T(8,128)(2,1)S(1)}, bf16[4,1,128,128]{3,2,1,0:T(8,128)(2,1)S(1)}, u32[]{:S(2)}, u32[]{:S(2)}) collective-permute-start(bf16[4,1,128,128]{3,2,1,0:T(8,128)(2,1)S(1)} %constant_dynamic-update-slice_fusion.12.refs_0_), channel_id=1, source_target_pairs={{0,1},{1,0},{2,3},{3,2},{4,5},{5,4},{6,7},{7,6},{8,9},{9,8},{10,11... | collective-permute-start | bytes 393224 | tf_op jit(solution)/shard_map/ppermute | solution.py:203
  96.0 6.7 %collective-permute-start.49 = (bf16[1,2,128,128]{3,2,1,0:T(8,128)(2,1)S(1)}, bf16[1,2,128,128]{3,2,1,0:T(8,128)(2,1)S(1)}, u32[]{:S(2)}, u32[]{:S(2)}) collective-permute-start(bf16[1,2,128,128]{3,2,1,0:T(8,128)(2,1)S(1)} %bitcast.40), channel_id=1, source_target_pairs={{0,16},{1,17},{2,18},{3,19},{4,20},{5,21},{6,22},{7,23},{8,24},{9,... | collective-permute-start | bytes 196616 | tf_op jit(solution)/shard_map/ppermute | solution.py:213
  97.6 5.6 %collective-permute-start.48 = (bf16[1,2,128,128]{3,2,1,0:T(8,128)(2,1)S(1)}, bf16[1,2,128,128]{3,2,1,0:T(8,128)(2,1)S(1)}, u32[]{:S(2)}, u32[]{:S(2)}) collective-permute-start(bf16[1,2,128,128]{3,2,1,0:T(8,128)(2,1)S(1)} %bitcast.41), channel_id=1, source_target_pairs={{0,24},{1,25},{2,26},{3,27},{4,28},{5,29},{6,30},{7,31},{8,0},{9,1... | collective-permute-start | bytes 196616 | tf_op jit(solution)/shard_map/ppermute | solution.py:213
  103.2 7.2 %collective-permute-start.55 = (bf16[2,2,128,128]{3,2,1,0:T(8,128)(2,1)S(1)}, bf16[2,2,128,128]{3,2,1,0:T(8,128)(2,1)S(1)}, u32[]{:S(2)}, u32[]{:S(2)}) collective-permute-start(bf16[2,2,128,128]{3,2,1,0:T(8,128)(2,1)S(1)} %get-tuple-element.99), channel_id=1, source_target_pairs={{0,6},{1,7},{2,4},{3,5},{4,2},{5,3},{6,0},{7,1},{8,14},{9,15},{10,... | collective-permute-start | bytes 393224 | tf_op jit(solution)/shard_map/ppermute | solution.py:219
  104.8 6.6 %collective-permute-start.53 = (bf16[2,2,128,128]{3,2,1,0:T(8,128)(2,1)S(1)}, bf16[2,2,128,128]{3,2,1,0:T(8,128)(2,1)S(1)}, u32[]{:S(2)}, u32[]{:S(2)}) collective-permute-start(bf16[2,2,128,128]{3,2,1,0:T(8,128)(2,1)S(1)} %get-tuple-element.100), channel_id=1, source_target_pairs={{0,2},{1,5},{2,0},{3,7},{4,6},{5,1},{6,4},{7,3},{8,10},{9,13},{10,... | collective-permute-start | bytes 393224 | tf_op jit(solution)/shard_map/ppermute | solution.py:219
  105.6 6.3 %collective-permute-start.51 = (bf16[2,2,128,128]{3,2,1,0:T(8,128)(2,1)S(1)}, bf16[2,2,128,128]{3,2,1,0:T(8,128)(2,1)S(1)}, u32[]{:S(2)}, u32[]{:S(2)}) collective-permute-start(bf16[2,2,128,128]{3,2,1,0:T(8,128)(2,1)S(1)} %get-tuple-element.101), channel_id=1, source_target_pairs={{0,4},{1,3},{2,6},{3,1},{4,0},{5,7},{6,2},{7,5},{8,12},{9,11},{10,... | collective-permute-start | bytes 393224 | tf_op jit(solution)/shard_map/ppermute | solution.py:219
  106.8 5.8 %collective-permute-start.50 = (bf16[2,2,128,128]{3,2,1,0:T(8,128)(2,1)S(1)}, bf16[2,2,128,128]{3,2,1,0:T(8,128)(2,1)S(1)}, u32[]{:S(2)}, u32[]{:S(2)}) collective-permute-start(bf16[2,2,128,128]{3,2,1,0:T(8,128)(2,1)S(1)} %get-tuple-element.102), channel_id=1, source_target_pairs={{0,1},{1,0},{2,3},{3,2},{4,5},{5,4},{6,7},{7,6},{8,9},{9,8},{10,11... | collective-permute-start | bytes 393224 | tf_op jit(solution)/shard_map/ppermute | solution.py:203
  (26 other events, 74.9 us)
